TPU v7x, 512 devices: a whole 4x8x8 slice. The times are simulated.
512 devices in a mesh: replica: 64 (over y, z), fsdp: 8 (over x, core).
Axes of the slice: x: 4, y: 8, z: 8, core: 2. Of those that a mesh axis runs over, the one named last changes fastest.
Arguments:
- replica_params: bfloat16 [64, 2, 128, 8192], P('replica', None, 'fsdp'), may hold values from -1.1 to 1.1
- outer_base: float32 [2, 128, 8192], P(None, 'fsdp'), may hold values from -1 to 1
- outer_momentum: float32 [2, 128, 8192], P(None, 'fsdp', 'replica'), may hold values from -0.012 to 0.012
Outputs:
- new_base: float32 [2, 128, 8192], P(None, 'fsdp')
- new_momentum: float32 [2, 128, 8192], P(None, 'fsdp', 'replica')
All inputs are finite; a program needn't handle non-finite values.
Results may differ from a plain program's by a relative error of at most 0.0023.
Values may be sent and summed in bfloat16 or wider, within the bound.
No kernel may reach another device: no remote copies, remote signals or barrier semaphores. Data moves between devices by JAX's collectives and lax.ppermute only.
A program may use at most 64 MiB of HBM per device.

v0:
```python
import math

import jax
import jax.numpy as jnp
from jax import lax
from jax.sharding import PartitionSpec as P

BLOCK = 128


CODE_RANGE = 448.0
EPSILON = 1e-06
OUTER_RATE = 0.7
NESTEROV = 0.9
CLIP_RMS = 0.001


def encode(difference):
    blocks = difference.reshape(difference.shape[0], difference.shape[1] // BLOCK, BLOCK)
    largest = jnp.max(jnp.abs(blocks), axis=-1, keepdims=True)
    scales = ((largest + EPSILON) / CODE_RANGE).astype(jnp.bfloat16)
    code_words = (blocks / scales.astype(jnp.float32)).astype(jnp.bfloat16)
    return lax.optimization_barrier((code_words, scales))


def decode(code_words, scales):
    restored = code_words.astype(jnp.float32) * scales.astype(jnp.float32)
    return restored.reshape(restored.shape[0], restored.shape[1] * restored.shape[2])


def per_device(replica_params, outer_base, outer_momentum):
    replicas = lax.axis_size("replica")
    owner_index = lax.axis_index("replica")
    layer_count = outer_base.shape[0]
    row_count = outer_base.shape[1]
    width = outer_base.shape[2]
    owned_width = width // replicas
    limit = CLIP_RMS * math.sqrt(row_count * lax.axis_size("fsdp") * width)
    averaged_all = []
    for layer_id in range(layer_count):
        difference = outer_base[layer_id] - replica_params[0, layer_id].astype(jnp.float32)
        code_words, scales = encode(difference)
        summed = lax.psum_scatter(
            decode(code_words, scales), "replica", scatter_dimension=1, tiled=True
        )
        averaged_all.append(summed / replicas)
    square_list = [jnp.sum(averaged * averaged) for averaged in averaged_all]
    totals = [lax.psum(square_sum, ("replica", "fsdp")) for square_sum in square_list]
    base_list = []
    momentum_list = []
    for layer_id in range(layer_count):
        factor = jnp.minimum(1.0, limit / (jnp.sqrt(totals[layer_id]) + EPSILON))
        clipped = averaged_all[layer_id] * factor
        momentum_next = NESTEROV * outer_momentum[layer_id] + clipped
        outer_step = lax.optimization_barrier(
            (OUTER_RATE * (clipped + NESTEROV * momentum_next)).astype(jnp.bfloat16)
        )
        owned_base = lax.dynamic_slice_in_dim(
            outer_base[layer_id], owner_index * owned_width, owned_width, 1
        )
        refreshed = lax.all_gather(
            owned_base - outer_step.astype(jnp.float32), "replica", axis=1, tiled=True
        )
        base_list.append(refreshed)
        momentum_list.append(momentum_next)
    return (jnp.stack(base_list), jnp.stack(momentum_list))


def solution(mesh):
    placed = (P("replica", None, "fsdp", None), P(None, "fsdp", None), P(None, "fsdp", "replica"))
    return jax.shard_map(
        per_device,
        mesh=mesh,
        in_specs=placed,
        out_specs=(P(None, "fsdp", None), P(None, "fsdp", "replica")),
        check_vma=False,
    )
```

profile of v0, /device:TPU:8, one launch (start us, length us, event | category | flops | bytes accessed | tf_op | source)
XLA Modules:
  0.0 707.6 jit_solution(13904484472812428878)
XLA Ops:
  7.2 0.0 reduce-scatter.5.cloned.1.call-start
  7.2 1.3 fusion.6
  8.6 0.0 copy-start
  8.6 0.1 copy.8
  8.7 0.9 copy-done
  9.6 0.1 convert_bitcast_fusion.1
  9.7 0.1 copy.9
  9.8 0.1 bitcast_subtract_fusion
  9.8 0.2 abs_reduce_fusion
  10.1 0.2 divide_convert_fusion
  10.3 0.2 convert_multiply_fusion
  10.5 1.1 copy.13
  11.6 0.0 reduce-scatter.5.cloned.1.call-update
  11.6 0.0 reduce-scatter.3.cloned.1.call-start
  11.7 0.1 copy.5
  11.8 0.1 copy.6
  11.9 0.1 bitcast_subtract_fusion.1
  12.0 0.2 abs_reduce_fusion.1
  12.2 0.2 divide_convert_fusion.1
  12.4 0.2 convert_multiply_fusion.1
  12.6 1.1 copy.14
  13.7 0.0 reduce-scatter.3.cloned.1.call-update
  13.7 244.6 %reduce-scatter.5.cloned.1.call-done = f32[16,128]{1,0:T(8,128)} async-done(((f32[16,8192]{1,0:T(8,128)}), f32[16,128]{1,0:T(8,128)}) %reduce-scatter.5.cloned.1.call-update) | async-done | bytes 8208 | tf_op jit(solution)/shard_map/reduce_scatter | solution.py:43
  258.4 1.3 multiply_reduce_fusion
  259.7 0.0 copy-start.3
  259.7 243.2 %reduce-scatter.3.cloned.1.call-done = f32[16,128]{1,0:T(8,128)} async-done(((f32[16,8192]{1,0:T(8,128)}), f32[16,128]{1,0:T(8,128)}) %reduce-scatter.3.cloned.1.call-update) | async-done | bytes 8208 | tf_op jit(solution)/shard_map/reduce_scatter | solution.py:43
  502.9 1.3 multiply_reduce_fusion.1
  504.2 95.7 %all-reduce = (f32[]{:T(128)}, f32[]{:T(128)}) all-reduce(f32[]{:T(128)} %multiply_reduce_fusion, f32[]{:T(128)} %multiply_reduce_fusion.1), channel_id=1, replica_groups=mesh['replica'=64,'fsdp'=8] {'replica','fsdp'}, use_global_device_ids=true, to_apply=%region_7.0 | all-reduce | flops 2 | bytes 16 | tf_op jit(solution)/shard_map/psum | solution.py:48
  600.6 0.0 copy-start.2
  601.3 0.0 copy-start.1
  601.4 0.0 copy-done.3
  601.4 0.0 copy-done.2
  601.4 0.6 copy-done.1
  602.1 48.3 %all_gather.6 = f32[16,8192]{1,0:T(8,128)S(1)} all-gather(f32[16,128]{1,0:T(8,128)S(1)} %bitcast_subtract_fusion.3), channel_id=1, replica_groups=mesh['replica'=64,'fsdp'=8] {'replica'}, dimensions={1}, use_global_device_ids=true | all-gather | bytes 532480 | tf_op jit(solution)/shard_map/all_gather | solution.py:61
  650.4 48.7 %all_gather.7 = f32[16,8192]{1,0:T(8,128)S(1)} all-gather(f32[16,128]{1,0:T(8,128)S(1)} %bitcast_subtract_fusion.2), channel_id=1, replica_groups=mesh['replica'=64,'fsdp'=8] {'replica'}, dimensions={1}, use_global_device_ids=true | all-gather | bytes 532480 | tf_op jit(solution)/shard_map/all_gather | solution.py:61
  699.1 0.6 pad_maximum_fusion.1
  699.7 1.0 pad_maximum_fusion
  (7 shorter events, 0.0 us)
Async XLA Ops:
  7.2 251.2 %reduce-scatter.5.cloned.1.call-start = ((), (), s32[]{:S(2)}) async-start(), calls=%async_computation.3 | async-start | bytes 532480 | tf_op jit(solution)/shard_map/reduce_scatter | solution.py:43
  8.6 1.0 copy-start
  11.6 491.3 %reduce-scatter.3.cloned.1.call-start = ((), (), s32[]{:S(2)}) async-start(), calls=%async_computation.2 | async-start | bytes 532480 | tf_op jit(solution)/shard_map/reduce_scatter | solution.py:43
  259.7 341.8 %copy-start.3 = (f32[2,16,128]{2,1,0:T(8,128)S(1)}, f32[2,16,128]{2,1,0:T(8,128)}, u32[]{:S(2)}) copy-start(f32[2,16,128]{2,1,0:T(8,128)} %param.5) | copy-start | bytes 49156
  600.6 0.8 copy-start.2
  601.3 0.7 copy-start.1
Sparse Core Ops, SparseCore 0:
  12.0 246.2 reduce-scatter.4
  263.5 239.3 reduce-scatter.2
where the time goes:
time: 708 us
  waiting for transfers between devices  488 us (69%)
  blocking collectives  193 us (27%)
  between operations  15.7 us (2%)
    reduce_scatter x2, waiting for transfers between devices, per_device(): lax.psum_scatter(decode(code_words, scales), 'replica', scatter_dimension...  488 us
    all_gather x2, blocking collectives, per_device(): lax.all_gather(owned_base - outer_step.astype(jnp.float32), 'replica', ax...  97 us
    psum x1, blocking collectives, per_device(): lax.psum(square_sum, ('replica', 'fsdp'))  95.7 us
  transfers between devices with their start and end apart: 2, of which 2 were waited for; matrix products, arithmetic and copies ran while one was open for 0% of the time, Pallas kernels for 0%

commit v1 on v0

v1 whole, which is shorter than its diff:
```python
import math

import jax
import jax.numpy as jnp
from jax import lax
from jax.experimental import pallas as pl
from jax.sharding import PartitionSpec as P

BLOCK = 128


CODE_RANGE = 448.0
EPSILON = 1e-06
OUTER_RATE = 0.7
NESTEROV = 0.9
CLIP_RMS = 0.001


def split_kernel(params_ref, blocks_ref):
    replicas, layers, rows, width = blocks_ref.shape
    for replica in range(replicas):
        blocks_ref[replica] = params_ref[0, :, :, pl.ds(replica * width, width)]


def average_kernel(received_ref, base_ref, averaged_ref, square_ref):
    replicas = received_ref.shape[0]
    layers, rows, width = base_ref.shape
    base = base_ref[...].reshape(layers * rows, width)

    def accumulate(replica, summed):
        difference = base - received_ref[replica].reshape(layers * rows, width).astype(jnp.float32)
        largest = jnp.max(jnp.abs(difference), axis=-1, keepdims=True)
        scales = ((largest + EPSILON) / CODE_RANGE).astype(jnp.bfloat16).astype(jnp.float32)
        code_words = (difference / scales).astype(jnp.bfloat16)
        return summed + code_words.astype(jnp.float32) * scales

    summed = lax.fori_loop(
        0, replicas, accumulate, jnp.zeros((layers * rows, width), jnp.float32), unroll=8
    )
    averaged = summed / replicas
    averaged_ref[...] = averaged.reshape(layers, rows, width)
    squares = (averaged * averaged).reshape(layers, rows, width)
    square_sum = jnp.sum(jnp.sum(squares, axis=1), axis=-1, keepdims=True)
    for layer in range(layers):
        square_ref[layer : layer + 1] = jnp.broadcast_to(square_sum[layer : layer + 1], (1, width))


def step_kernel(limit, squares_ref, averaged_ref, momentum_ref, momentum_next_ref, step_ref):
    layers, rows, width = averaged_ref.shape
    sums = jnp.sum(squares_ref[...], axis=0, keepdims=True)
    share = width // layers
    for layer in range(layers):
        total = jnp.max(sums[:, layer * share : (layer + 1) * share], axis=-1, keepdims=True)
        factor = jnp.minimum(1.0, limit / (jnp.sqrt(total) + EPSILON))
        clipped = averaged_ref[layer] * factor
        momentum_next = NESTEROV * momentum_ref[layer] + clipped
        momentum_next_ref[layer] = momentum_next
        step = (OUTER_RATE * (clipped + NESTEROV * momentum_next)).astype(jnp.bfloat16)
        for replica in range(step_ref.shape[0]):
            step_ref[replica, layer] = step


def base_kernel(steps_ref, base_ref, new_base_ref):
    replicas, layers, rows, width = steps_ref.shape
    for replica in range(replicas):
        columns = pl.ds(replica * width, width)
        for layer in range(layers):
            step = steps_ref[replica, layer].astype(jnp.float32)
            new_base_ref[layer, :, columns] = base_ref[layer, :, columns] - step


def per_device(replica_params, outer_base, outer_momentum):
    replicas = lax.axis_size("replica")
    owner_index = lax.axis_index("replica")
    everyone = replicas * lax.axis_size("fsdp")
    layers, rows, width = outer_base.shape
    owned = width // replicas
    limit = CLIP_RMS * math.sqrt(rows * lax.axis_size("fsdp") * width)

    blocks = pl.pallas_call(
        split_kernel,
        out_shape=jax.ShapeDtypeStruct((replicas, layers, rows, owned), replica_params.dtype),
        name="split",
    )(replica_params)
    received = lax.all_to_all(blocks, "replica", 0, 0, tiled=True)
    owned_base = lax.dynamic_slice_in_dim(outer_base, owner_index * owned, owned, 2)

    averaged, square_sum = pl.pallas_call(
        average_kernel,
        out_shape=(
            jax.ShapeDtypeStruct((layers, rows, owned), jnp.float32),
            jax.ShapeDtypeStruct((layers, owned), jnp.float32),
        ),
        name="average",
    )(received, owned_base)

    mine = square_sum[:, : owned // layers].reshape(1, 1, owned)
    squares = lax.all_to_all(
        jnp.broadcast_to(mine, (everyone, 1, owned)), ("replica", "fsdp"), 0, 0, tiled=True
    )

    momentum_next, step = pl.pallas_call(
        lambda *refs: step_kernel(limit, *refs),
        out_shape=(
            jax.ShapeDtypeStruct((layers, rows, owned), jnp.float32),
            jax.ShapeDtypeStruct((replicas, layers, rows, owned), jnp.bfloat16),
        ),
        name="step",
    )(squares.reshape(everyone, owned), averaged, outer_momentum)

    steps = lax.all_to_all(step, "replica", 0, 0, tiled=True)
    new_base = pl.pallas_call(
        base_kernel,
        out_shape=jax.ShapeDtypeStruct((layers, rows, width), jnp.float32),
        name="base",
    )(steps, outer_base)
    return (new_base, momentum_next)


def solution(mesh):
    placed = (P("replica", None, "fsdp", None), P(None, "fsdp", None), P(None, "fsdp", "replica"))
    return jax.shard_map(
        per_device,
        mesh=mesh,
        in_specs=placed,
        out_specs=(P(None, "fsdp", None), P(None, "fsdp", "replica")),
        check_vma=False,
    )
```

time: 708 us -> 100 us (0.14)
  the two profiles are of different devices: /device:TPU:8 before, /device:TPU:1 now
where the time goes in v1:
time: 100 us; the launch traced here: 98.3 us
  blocking collectives  53.4 us (53%)
  starting transfers between devices  17.1 us (17%)
  waiting for transfers between devices  15 us (15%)
  Pallas kernels  9.11 us (9%)
  local copies, waits for them, and re-layouts  3.01 us (3%)
    all_to_all x1, blocking collectives, per_device(): lax.all_to_all(jnp.broadcast_to(mine, (everyone, 1, owned)), ('replica',...  30.7 us
    all_to_all x1, blocking collectives, per_device(): steps = lax.all_to_all(step, 'replica', 0, 0, tiled=True)  22.7 us
    all_to_all x1, starting transfers between devices, per_device(): received = lax.all_to_all(blocks, 'replica', 0, 0, tiled=True)  17.1 us
    all_to_all x1, waiting for transfers between devices, per_device(): received = lax.all_to_all(blocks, 'replica', 0, 0, tiled=True)  15 us
    pallas_call x1, Pallas kernels, per_device(): pl.pallas_call(average_kernel, out_shape=(jax.ShapeDtypeStruct((layers, r...  2.77 us
    pallas_call x1, Pallas kernels, per_device(): pl.pallas_call(base_kernel, out_shape=jax.ShapeDtypeStruct((layers, rows,...  2.45 us
  transfers between devices with their start and end apart: 1, of which 1 were waited for; matrix products, arithmetic and copies ran while one was open for 1% of the time, Pallas kernels for 0%

profile of v1, /device:TPU:1, one launch (start us, length us, event | category | flops | bytes accessed | tf_op | source)
XLA Modules:
  0.0 98.3 jit_solution(5504817190083963478)
XLA Ops:
  0.6 1.9 %split.1 = bf16[64,2,16,128]{3,2,1,0:T(8,128)(2,1)} custom-call(bf16[1,2,16,8192]{3,2,1,0:T(8,128)(2,1)} %params_ref.1), custom_call_target="tpu_custom_call" | custom-call | tf_op jit(solution)/shard_map/split/pallas_call | solution.py:80
  2.6 17.1 %all-to-all-start = ((bf16[64,2,16,128]{3,2,1,0:T(8,128)(2,1)}), bf16[64,2,16,128]{3,2,1,0:T(8,128)(2,1)S(1)}, u32[]{:S(2)}, u32[]{:S(2)}) async-start(bf16[64,2,16,128]{3,2,1,0:T(8,128)(2,1)} %split.1), calls=%async_computation | async-start | bytes 1048576 | tf_op jit(solution)/shard_map/all_to_all | solution.py:85
  19.7 1.3 %constant_dynamic-slice_fusion.base_ref = f32[2,16,128]{2,1,0:T(8,128)} fusion(f32[2,16,8192]{2,1,0:T(8,128)} %base_ref.1, s32[]{:T(128)S(6)} %select_n.3), kind=kLoop, calls=%fused_computation | loop fusion | bytes 32772 | tf_op jit(solution)/shard_map/dynamic_slice | solution.py:86
  21.0 15.0 %all-to-all-done.received_ref = bf16[64,2,16,128]{3,2,1,0:T(8,128)(2,1)S(1)} async-done(((bf16[64,2,16,128]{3,2,1,0:T(8,128)(2,1)}), bf16[64,2,16,128]{3,2,1,0:T(8,128)(2,1)S(1)}, u32[]{:S(2)}, u32[]{:S(2)}) %all-to-all-start) | async-done | bytes 524320 | tf_op jit(solution)/shard_map/all_to_all | solution.py:85
  36.0 0.0 copy-start
  36.0 0.8 copy-done
  36.8 2.8 %average.1 = (f32[2,16,128]{2,1,0:T(8,128)}, f32[2,128]{1,0:T(2,128)}) custom-call(bf16[64,2,16,128]{3,2,1,0:T(8,128)(2,1)} %copy-done, f32[2,16,128]{2,1,0:T(8,128)} %constant_dynamic-slice_fusion.base_ref), custom_call_target="tpu_custom_call" | custom-call | tf_op jit(solution)/shard_map/average/pallas_call | solution.py:88
  39.6 0.0 copy-start.1
  39.6 0.7 copy-done.1
  40.3 0.1 broadcast_in_dim.7
  40.4 0.1 broadcast_in_dim.8
  40.5 30.7 %all_to_all.15 = f32[512,1,128]{2,1,0:T(1,128)} all-to-all(f32[512,1,128]{2,1,0:T(1,128)S(1)} %broadcast_in_dim.8), channel_id=1, replica_groups=mesh['replica'=64,'fsdp'=8] {'replica','fsdp'}, dimensions={0} | all-to-all | bytes 524288 | tf_op jit(solution)/shard_map/all_to_all | solution.py:98
  71.2 2.0 %step.1 = (f32[2,16,128]{2,1,0:T(8,128)}, bf16[64,2,16,128]{3,2,1,0:T(8,128)(2,1)}) custom-call(f32[512,128]{1,0:T(8,128)} %bitcast.2, f32[2,16,128]{2,1,0:T(8,128)} %get-tuple-element.7.refs_1_, f32[2,16,128]{2,1,0:T(8,128)} %refs_2_.1), custom_call_target="tpu_custom_call" | custom-call | tf_op jit(solution)/shard_map/step/pallas_call | solution.py:102
  73.2 22.7 %all_to_all.16.steps_ref = bf16[64,2,16,128]{3,2,1,0:T(8,128)(2,1)} all-to-all(bf16[64,2,16,128]{3,2,1,0:T(8,128)(2,1)} %get-tuple-element.8), channel_id=1, replica_groups=mesh['replica'=64,'fsdp'=8] {'replica'}, dimensions={0} | all-to-all | bytes 1048576 | tf_op jit(solution)/shard_map/all_to_all | solution.py:111
  95.8 2.4 %base.1 = f32[2,16,8192]{2,1,0:T(8,128)} custom-call(bf16[64,2,16,128]{3,2,1,0:T(8,128)(2,1)} %all_to_all.16.steps_ref, f32[2,16,8192]{2,1,0:T(8,128)} %base_ref.1), custom_call_target="tpu_custom_call" | custom-call | tf_op jit(solution)/shard_map/base/pallas_call | solution.py:112
Async XLA Ops:
  2.6 33.5 %all-to-all-start = ((bf16[64,2,16,128]{3,2,1,0:T(8,128)(2,1)}), bf16[64,2,16,128]{3,2,1,0:T(8,128)(2,1)S(1)}, u32[]{:S(2)}, u32[]{:S(2)}) async-start(bf16[64,2,16,128]{3,2,1,0:T(8,128)(2,1)} %split.1), calls=%async_computation | async-start | bytes 1048576 | tf_op jit(solution)/shard_map/all_to_all | solution.py:85
  36.0 0.8 copy-start
  39.6 0.7 copy-start.1

commit v2 on v1

v2 whole, which is shorter than its diff:
```python
import math

import jax
import jax.numpy as jnp
from jax import lax
from jax.experimental import pallas as pl
from jax.experimental.pallas import tpu as pltpu
from jax.sharding import Mesh, PartitionSpec as P

BLOCK = 128


CODE_RANGE = 448.0
EPSILON = 1e-06
OUTER_RATE = 0.7
NESTEROV = 0.9
CLIP_RMS = 0.001
SUBLANES = 8
VMEM_LIMIT = 8 * 2**20


def split_kernel(params_ref, blocks_ref, semaphores):
    copies = [
        pltpu.make_async_copy(params_ref.at[group], blocks_ref.at[:, group], semaphores.at[group])
        for group in range(params_ref.shape[0])
    ]
    for copy in copies:
        copy.start()
    for copy in copies:
        copy.wait()


def average_kernel(received_ref, base_ref, averaged_ref, square_ref):
    replicas = received_ref.shape[0]
    base = base_ref[...]

    def accumulate(replica, summed):
        difference = base - received_ref[replica].astype(jnp.float32)
        largest = jnp.max(jnp.abs(difference), axis=-1, keepdims=True)
        scales = ((largest + EPSILON) / CODE_RANGE).astype(jnp.bfloat16).astype(jnp.float32)
        code_words = (difference / scales).astype(jnp.bfloat16)
        return summed + code_words.astype(jnp.float32) * scales

    summed = lax.fori_loop(0, replicas, accumulate, jnp.zeros(base.shape, jnp.float32), unroll=8)
    averaged = summed / replicas
    averaged_ref[...] = averaged
    squares = averaged * averaged
    half = squares.shape[0] // 2
    first = jnp.sum(jnp.sum(jnp.sum(squares[:half], axis=0), axis=0, keepdims=True), axis=-1, keepdims=True)
    second = jnp.sum(jnp.sum(jnp.sum(squares[half:], axis=0), axis=0, keepdims=True), axis=-1, keepdims=True)
    lanes = lax.broadcasted_iota(jnp.int32, square_ref.shape, 1)
    square_ref[...] = jnp.where(lanes < BLOCK // 2, first, second)


def pack_kernel(squares_ref, averaged_ref, momentum_ref, packed_ref):
    sums = jnp.broadcast_to(jnp.sum(squares_ref[...], axis=0, keepdims=True), (SUBLANES, BLOCK))
    groups = averaged_ref.shape[0]
    for peer in range(packed_ref.shape[0]):
        for group in range(groups):
            packed_ref[peer, group] = averaged_ref[group]
            packed_ref[peer, groups + group] = momentum_ref[group]
        packed_ref[peer, 2 * groups] = sums


def step_kernel(limit, packed_ref, averaged_ref, momentum_ref, momentum_next_ref, step_ref):
    peers = packed_ref.shape[0]
    groups = averaged_ref.shape[0]
    sums = packed_ref[0, 2 * groups]
    for peer in range(1, peers):
        sums = sums + packed_ref[peer, 2 * groups]
    factors = []
    for layer in range(2):
        total = jnp.max(sums[:, layer * 64 : (layer + 1) * 64], axis=-1, keepdims=True)
        factors.append(jnp.minimum(1.0, limit / (jnp.sqrt(total) + EPSILON)))
    for group in range(groups):
        factor = factors[group * 2 // groups]
        momentum_next_ref[group] = NESTEROV * momentum_ref[group] + averaged_ref[group] * factor
        for peer in range(peers):
            clipped = packed_ref[peer, group] * factor
            momentum_next = NESTEROV * packed_ref[peer, groups + group] + clipped
            step = (OUTER_RATE * (clipped + NESTEROV * momentum_next)).astype(jnp.bfloat16)
            for target in range(step_ref.shape[0]):
                step_ref[target, peer, group] = step


def base_kernel(steps_ref, base_ref, new_base_ref):
    owners, groups = steps_ref.shape[:2]
    layers = base_ref.shape[0]
    for owner in range(owners):
        columns = pl.ds(owner * BLOCK, BLOCK)
        for group in range(groups):
            layer, part = divmod(group, groups // layers)
            rows = pl.ds(part * SUBLANES, SUBLANES)
            step = steps_ref[owner, group].astype(jnp.float32)
            new_base_ref[layer, rows, columns] = base_ref[layer, rows, columns] - step


def per_device(replica_params, outer_base, outer_momentum):
    ys, zs = lax.axis_size("y"), lax.axis_size("z")
    replicas = ys * zs
    fsdp = lax.axis_size("fsdp")
    layers, rows, width = outer_base.shape
    groups = layers * rows // SUBLANES
    limit = CLIP_RMS * math.sqrt(rows * fsdp * width)
    owner_index = lax.axis_index("y") * zs + lax.axis_index("z")
    params = pltpu.CompilerParams(vmem_limit_bytes=VMEM_LIMIT)
    tile = (groups, SUBLANES, BLOCK)

    grouped = replica_params.reshape(groups, SUBLANES, replicas, BLOCK).transpose(0, 2, 1, 3)
    blocks = pl.pallas_call(
        split_kernel,
        out_shape=jax.ShapeDtypeStruct((replicas, *tile), replica_params.dtype),
        in_specs=[pl.BlockSpec(memory_space=pl.ANY)],
        out_specs=pl.BlockSpec(memory_space=pl.ANY),
        scratch_shapes=[pltpu.SemaphoreType.DMA((groups,))],
        compiler_params=pltpu.CompilerParams(vmem_limit_bytes=60 * 2**20),
        name="split",
    )(grouped)
    received = lax.all_to_all(blocks, ("y", "z"), 0, 0, tiled=True)
    owned_base = lax.dynamic_slice_in_dim(outer_base, owner_index * BLOCK, BLOCK, 2).reshape(tile)
    momentum = outer_momentum.reshape(tile)

    averaged, squares = pl.pallas_call(
        average_kernel,
        out_shape=(
            jax.ShapeDtypeStruct(tile, jnp.float32),
            jax.ShapeDtypeStruct((ys * fsdp, BLOCK), jnp.float32),
        ),
        compiler_params=params,
        name="average",
    )(received, owned_base)

    squares = lax.all_to_all(
        squares.reshape(ys * fsdp, 1, BLOCK), ("y", "fsdp"), 0, 0, tiled=True
    ).reshape(ys * fsdp, BLOCK)
    packed = pl.pallas_call(
        pack_kernel,
        out_shape=jax.ShapeDtypeStruct((zs, 2 * groups + 1, SUBLANES, BLOCK), jnp.float32),
        compiler_params=params,
        name="pack",
    )(squares, averaged, momentum)
    packed = lax.all_to_all(packed, "z", 0, 0, tiled=True)

    momentum_next, step = pl.pallas_call(
        lambda *refs: step_kernel(limit, *refs),
        out_shape=(
            jax.ShapeDtypeStruct(tile, jnp.float32),
            jax.ShapeDtypeStruct((ys, zs, *tile), jnp.bfloat16),
        ),
        compiler_params=params,
        name="step",
    )(packed, averaged, momentum)

    steps = lax.all_to_all(step, "y", 0, 0, tiled=True).reshape(replicas, *tile)
    chunks = 4
    new_base = pl.pallas_call(
        base_kernel,
        grid=(chunks,),
        in_specs=[
            pl.BlockSpec((replicas // chunks, *tile), lambda i: (i, 0, 0, 0)),
            pl.BlockSpec((layers, rows, width // chunks), lambda i: (0, 0, i)),
        ],
        out_specs=pl.BlockSpec((layers, rows, width // chunks), lambda i: (0, 0, i)),
        out_shape=jax.ShapeDtypeStruct((layers, rows, width), jnp.float32),
        compiler_params=params,
        name="base",
    )(steps, outer_base)
    return (new_base, momentum_next.reshape(outer_momentum.shape))


def solution(mesh):
    replicas, fsdp = mesh.devices.shape
    side = math.isqrt(replicas)
    torus = Mesh(mesh.devices.reshape(side, side, fsdp), ("y", "z", "fsdp"))
    return jax.shard_map(
        per_device,
        mesh=torus,
        in_specs=(
            P(("y", "z"), None, "fsdp", None),
            P(None, "fsdp", None),
            P(None, "fsdp", ("y", "z")),
        ),
        out_specs=(P(None, "fsdp", None), P(None, "fsdp", ("y", "z"))),
        check_vma=False,
    )
```

time: 100 us -> 108 us (1.080)
  Pallas kernels: 9.11 us -> 20.6 us
  local copies, waits for them, and re-layouts: 3.01 us -> 0.02 us
  waiting for transfers between devices: 15 us -> 16.3 us
    pallas_call x3 -> x4, Pallas kernels: 7.14 us -> 19.8 us  [the longest x1 17 us: per_device(): pl.pallas_call(split_kernel, out_shape=jax.ShapeDtypeStruct((replicas, *t...]
    unnamed x4, local copies, waits for them, and re-layouts: 1.46 us -> 0.01 us
    dynamic_slice x1, local copies, waits for them, and re-layouts: 1.33 us -> 0.01 us  [per_device(): lax.dynamic_slice_in_dim(outer_base, owner_index * BLOCK, BLOCK, 2)]
    all_to_all x1, waiting for transfers between devices: 15 us -> 16.3 us  [per_device(): received = lax.all_to_all(blocks, ('y', 'z'), 0, 0, tiled=True)]
    pallas_call x1, Pallas kernels: 1.97 us -> 0.78 us  [per_device(): pl.pallas_call(lambda *refs: step_kernel(limit, *refs), out_shape=(jax.Sh...]
    all_to_all x2 -> x3, blocking collectives: 53.4 us -> 52.5 us  [the longest x1 20.3 us: per_device(): lax.all_to_all(squares.reshape(ys * fsdp, 1, BLOCK), ('y', 'fsdp'), 0, 0,...]
  transfers between devices with their start and end apart: 1 -> 1, of which waited for: 1 -> 1; matrix products, arithmetic and copies ran while one was open for 1% -> 0% of each run, Pallas kernels for 0% -> 0%
where the time goes in v2:
time: 108 us; the launch traced here: 107 us
  blocking collectives  52.5 us (49%)
  Pallas kernels  20.6 us (19%)
  starting transfers between devices  17.1 us (16%)
  waiting for transfers between devices  16.3 us (15%)
    all_to_all x1, blocking collectives, per_device(): lax.all_to_all(squares.reshape(ys * fsdp, 1, BLOCK), ('y', 'fsdp'), 0, 0,...  20.3 us
    all_to_all x1, blocking collectives, per_device(): steps = lax.all_to_all(step, 'y', 0, 0, tiled=True).reshape(replicas, *tile)  17.8 us
    all_to_all x1, starting transfers between devices, per_device(): received = lax.all_to_all(blocks, ('y', 'z'), 0, 0, tiled=True)  17.1 us
    pallas_call x1, Pallas kernels, per_device(): pl.pallas_call(split_kernel, out_shape=jax.ShapeDtypeStruct((replicas, *t...  17 us
    all_to_all x1, waiting for transfers between devices, per_device(): received = lax.all_to_all(blocks, ('y', 'z'), 0, 0, tiled=True)  16.3 us
    all_to_all x1, blocking collectives, per_device(): packed = lax.all_to_all(packed, 'z', 0, 0, tiled=True)  14.5 us
  transfers between devices with their start and end apart: 1, of which 1 were waited for; matrix products, arithmetic and copies ran while one was open for 0% of the time, Pallas kernels for 0%

profile of v2, /device:TPU:1, one launch (start us, length us, event | category | flops | bytes accessed | tf_op | source)
XLA Modules:
  0.0 107.2 jit_solution(5555263957487254427)
XLA Ops:
  0.6 0.0 copy-start
  0.6 17.0 %split.1 = bf16[64,4,8,128]{3,2,1,0:T(8,128)(2,1)} custom-call(bf16[4,64,8,128]{3,2,1,0:T(8,128)(2,1)} %bitcast.17), custom_call_target="tpu_custom_call" | custom-call | tf_op jit(solution)/shard_map/split/pallas_call | solution.py:110
  17.7 17.1 %all-to-all-start = ((bf16[64,4,8,128]{3,2,1,0:T(8,128)(2,1)}), bf16[64,4,8,128]{3,2,1,0:T(8,128)(2,1)S(1)}, u32[]{:S(2)}, u32[]{:S(2)}) async-start(bf16[64,4,8,128]{3,2,1,0:T(8,128)(2,1)} %split.1), calls=%async_computation | async-start | bytes 1048576 | tf_op jit(solution)/shard_map/all_to_all | solution.py:119
  34.8 0.0 copy-done
  34.9 16.3 %all-to-all-done.received_ref = bf16[64,4,8,128]{3,2,1,0:T(8,128)(2,1)S(1)} async-done(((bf16[64,4,8,128]{3,2,1,0:T(8,128)(2,1)}), bf16[64,4,8,128]{3,2,1,0:T(8,128)(2,1)S(1)}, u32[]{:S(2)}, u32[]{:S(2)}) %all-to-all-start) | async-done | bytes 524320 | tf_op jit(solution)/shard_map/all_to_all | solution.py:119
  51.2 1.1 %average.1 = (f32[4,8,128]{2,1,0:T(8,128)S(1)}, f32[64,128]{1,0:T(8,128)S(1)}) custom-call(bf16[64,4,8,128]{3,2,1,0:T(8,128)(2,1)S(1)} %all-to-all-done.received_ref, f32[4,8,128]{2,1,0:T(8,128)S(1)} %bitcast.15), custom_call_target="tpu_custom_call" | custom-call | tf_op jit(solution)/shard_map/average/pallas_call | solution.py:123
  52.3 0.0 copy-start.1
  52.3 20.3 %all_to_all.20 = f32[64,1,128]{2,1,0:T(1,128)S(1)} all-to-all(f32[64,1,128]{2,1,0:T(1,128)S(1)} %bitcast.16), channel_id=1, replica_groups=mesh['y'=8,'z'=8,'fsdp'=8] {'y','fsdp'}, dimensions={0} | all-to-all | bytes 65536 | tf_op jit(solution)/shard_map/all_to_all | solution.py:133
  72.6 0.0 copy-done.1
  72.6 14.5 %all_to_all.21.refs_0_ = f32[8,9,8,128]{3,2,1,0:T(8,128)S(1)} all-to-all(f32[8,9,8,128]{3,2,1,0:T(8,128)S(1)} %pack.1), channel_id=1, replica_groups=mesh['y'=8,'z'=8,'fsdp'=8] {'z'}, dimensions={0} | all-to-all | bytes 589824 | tf_op jit(solution)/shard_map/all_to_all | solution.py:142
  87.1 0.8 step.1
  87.9 17.8 %all_to_all.22 = bf16[8,8,4,8,128]{4,3,2,1,0:T(8,128)(2,1)S(1)} all-to-all(bf16[8,8,4,8,128]{4,3,2,1,0:T(8,128)(2,1)S(1)} %get-tuple-element.8), channel_id=1, replica_groups=mesh['y'=8,'z'=8,'fsdp'=8] {'y'}, dimensions={0} | all-to-all | bytes 1048576 | tf_op jit(solution)/shard_map/all_to_all | solution.py:154
  105.6 1.6 %base.1 = f32[2,16,8192]{2,1,0:T(8,128)} custom-call(bf16[64,4,8,128]{3,2,1,0:T(8,128)(2,1)S(1)} %bitcast.11, f32[2,16,8192]{2,1,0:T(8,128)S(1)} %copy-done), custom_call_target="tpu_custom_call" | custom-call | tf_op jit(solution)/shard_map/base/pallas_call | solution.py:156
  (2 shorter events, 0.0 us)
Async XLA Ops:
  0.6 34.2 %copy-start = (f32[2,16,8192]{2,1,0:T(8,128)S(1)}, f32[2,16,8192]{2,1,0:T(8,128)}, u32[]{:S(2)}) copy-start(f32[2,16,8192]{2,1,0:T(8,128)} %base_ref.1) | copy-start | bytes 3145732
  17.7 33.5 %all-to-all-start = ((bf16[64,4,8,128]{3,2,1,0:T(8,128)(2,1)}), bf16[64,4,8,128]{3,2,1,0:T(8,128)(2,1)S(1)}, u32[]{:S(2)}, u32[]{:S(2)}) async-start(bf16[64,4,8,128]{3,2,1,0:T(8,128)(2,1)} %split.1), calls=%async_computation | async-start | bytes 1048576 | tf_op jit(solution)/shard_map/all_to_all | solution.py:119
  52.3 20.3 %copy-start.1 = (f32[2,16,128]{2,1,0:T(8,128)S(1)}, f32[2,16,128]{2,1,0:T(8,128)}, u32[]{:S(2)}) copy-start(f32[2,16,128]{2,1,0:T(8,128)} %param.5) | copy-start | bytes 49156

commit v3 on v2

v3 whole, which is shorter than its diff:
```python
import math

import jax
import jax.numpy as jnp
from jax import lax
from jax.experimental import pallas as pl
from jax.experimental.pallas import tpu as pltpu
from jax.sharding import Mesh, PartitionSpec as P

BLOCK = 128


CODE_RANGE = 448.0
EPSILON = 1e-06
OUTER_RATE = 0.7
NESTEROV = 0.9
CLIP_RMS = 0.001
SUBLANES = 8
VMEM_LIMIT = 8 * 2**20


def split_kernel(params_ref, blocks_ref):
    for owner in range(blocks_ref.shape[0]):
        blocks_ref[owner] = params_ref[:, owner]


def partial_kernel(received_ref, base_ref, momentum_ref, packed_ref):
    sources, blocks, groups = received_ref.shape[:3]
    layers = base_ref.shape[0]
    peers = packed_ref.shape[0]
    for block in range(blocks):
        columns = pl.ds(block * BLOCK, BLOCK)
        base = base_ref[:, :, columns].reshape(groups, SUBLANES, BLOCK)
        summed = jnp.zeros(base.shape, jnp.float32)
        for source in range(sources):
            difference = base - received_ref[source, block].astype(jnp.float32)
            largest = jnp.max(jnp.abs(difference), axis=-1, keepdims=True)
            scales = ((largest + EPSILON) / CODE_RANGE).astype(jnp.bfloat16).astype(jnp.float32)
            code_words = (difference / scales).astype(jnp.bfloat16)
            summed = summed + code_words.astype(jnp.float32) * scales
        sent = summed.astype(jnp.bfloat16)
        for peer in range(peers):
            packed_ref[peer, block] = sent
    momentum = momentum_ref[...].astype(jnp.bfloat16)
    for peer in range(peers):
        packed_ref[peer, blocks] = momentum


def average_kernel(replicas, packed_ref, averaged_ref, square_ref):
    sources = packed_ref.shape[0]
    blocks, groups = averaged_ref.shape[:2]
    squares = jnp.zeros((groups, SUBLANES, BLOCK), jnp.float32)
    for block in range(blocks):
        summed = packed_ref[0, block].astype(jnp.float32)
        for source in range(1, sources):
            summed = summed + packed_ref[source, block].astype(jnp.float32)
        averaged = summed / replicas
        averaged_ref[block] = averaged
        squares = squares + averaged * averaged
    half = groups // 2
    first = jnp.sum(jnp.sum(jnp.sum(squares[:half], axis=0), axis=0, keepdims=True), axis=-1, keepdims=True)
    second = jnp.sum(jnp.sum(jnp.sum(squares[half:], axis=0), axis=0, keepdims=True), axis=-1, keepdims=True)
    lanes = lax.broadcasted_iota(jnp.int32, square_ref.shape, 1)
    square_ref[...] = jnp.where(lanes < BLOCK // 2, first, second)


def step_kernel(limit, mine_ref, squares_ref, averaged_ref, packed_ref, momentum_ref, momentum_next_ref, step_ref):
    blocks, groups = averaged_ref.shape[:2]
    sums = jnp.sum(squares_ref[...], axis=0, keepdims=True)
    mine = mine_ref[0]
    for group in range(groups):
        layer = group * 2 // groups
        total = jnp.max(sums[:, layer * 64 : (layer + 1) * 64], axis=-1, keepdims=True)
        factor = jnp.minimum(1.0, limit / (jnp.sqrt(total) + EPSILON))
        momentum_next_ref[group] = NESTEROV * momentum_ref[group] + averaged_ref[mine, group] * factor
        for block in range(blocks):
            clipped = averaged_ref[block, group] * factor
            momentum_next = NESTEROV * packed_ref[block, blocks, group].astype(jnp.float32) + clipped
            step = (OUTER_RATE * (clipped + NESTEROV * momentum_next)).astype(jnp.bfloat16)
            for target in range(step_ref.shape[0]):
                step_ref[target, block, group] = step


def base_kernel(steps_ref, base_ref, new_base_ref):
    owners, groups = steps_ref.shape[:2]
    layers = base_ref.shape[0]
    for owner in range(owners):
        columns = pl.ds(owner * BLOCK, BLOCK)
        for group in range(groups):
            layer, part = divmod(group, groups // layers)
            rows = pl.ds(part * SUBLANES, SUBLANES)
            step = steps_ref[owner, group].astype(jnp.float32)
            new_base_ref[layer, rows, columns] = base_ref[layer, rows, columns] - step


def per_device(replica_params, outer_base, outer_momentum):
    ys, zs = lax.axis_size("y"), lax.axis_size("z")
    replicas = ys * zs
    fsdp = lax.axis_size("fsdp")
    layers, rows, width = outer_base.shape
    groups = layers * rows // SUBLANES
    limit = CLIP_RMS * math.sqrt(rows * fsdp * width)
    params = pltpu.CompilerParams(vmem_limit_bytes=VMEM_LIMIT)
    tile = (groups, SUBLANES, BLOCK)

    grouped = replica_params.reshape(groups, SUBLANES, replicas, BLOCK).transpose(0, 2, 1, 3)
    blocks = pl.pallas_call(
        split_kernel,
        out_shape=jax.ShapeDtypeStruct((replicas, *tile), replica_params.dtype),
        compiler_params=params,
        name="split",
    )(grouped)
    received = lax.all_to_all(blocks.reshape(ys, zs, *tile), "y", 0, 0, tiled=True)
    columns = zs * BLOCK
    owned_base = lax.dynamic_slice_in_dim(outer_base, lax.axis_index("y") * columns, columns, 2)
    momentum = outer_momentum.reshape(tile)

    packed = pl.pallas_call(
        partial_kernel,
        out_shape=jax.ShapeDtypeStruct((zs, zs + 1, *tile), jnp.bfloat16),
        compiler_params=params,
        name="partial",
    )(received, owned_base, momentum)
    packed = lax.all_to_all(packed, "z", 0, 0, tiled=True)

    averaged, squares = pl.pallas_call(
        lambda *refs: average_kernel(replicas, *refs),
        out_shape=(
            jax.ShapeDtypeStruct((zs, *tile), jnp.float32),
            jax.ShapeDtypeStruct((ys * fsdp, BLOCK), jnp.float32),
        ),
        compiler_params=params,
        name="average",
    )(packed)
    squares = lax.all_to_all(
        squares.reshape(ys * fsdp, 1, BLOCK), ("y", "fsdp"), 0, 0, tiled=True
    ).reshape(ys * fsdp, BLOCK)

    vmem = pl.BlockSpec(memory_space=pltpu.VMEM)
    momentum_next, step = pl.pallas_call(
        lambda *refs: step_kernel(limit, *refs),
        in_specs=[pl.BlockSpec(memory_space=pltpu.SMEM), vmem, vmem, vmem, vmem],
        out_shape=(
            jax.ShapeDtypeStruct(tile, jnp.float32),
            jax.ShapeDtypeStruct((ys, zs, *tile), jnp.bfloat16),
        ),
        compiler_params=params,
        name="step",
    )(lax.axis_index("z").reshape(1), squares, averaged, packed, momentum)

    steps = lax.all_to_all(step, "y", 0, 0, tiled=True).reshape(replicas, *tile)
    chunks = 4
    new_base = pl.pallas_call(
        base_kernel,
        grid=(chunks,),
        in_specs=[
            pl.BlockSpec((replicas // chunks, *tile), lambda i: (i, 0, 0, 0)),
            pl.BlockSpec((layers, rows, width // chunks), lambda i: (0, 0, i)),
        ],
        out_specs=pl.BlockSpec((layers, rows, width // chunks), lambda i: (0, 0, i)),
        out_shape=jax.ShapeDtypeStruct((layers, rows, width), jnp.float32),
        compiler_params=params,
        name="base",
    )(steps, outer_base)
    return (new_base, momentum_next.reshape(outer_momentum.shape))


def solution(mesh):
    replicas, fsdp = mesh.devices.shape
    side = math.isqrt(replicas)
    torus = Mesh(mesh.devices.reshape(side, side, fsdp), ("y", "z", "fsdp"))
    return jax.shard_map(
        per_device,
        mesh=torus,
        in_specs=(
            P(("y", "z"), None, "fsdp", None),
            P(None, "fsdp", None),
            P(None, "fsdp", ("y", "z")),
        ),
        out_specs=(P(None, "fsdp", None), P(None, "fsdp", ("y", "z"))),
        check_vma=False,
    )
```

time: 108 us -> 95 us (0.88)
  Pallas kernels: 20.6 us -> 4.53 us
  waiting for transfers between devices: 16.3 us -> 24 us
  starting transfers between devices: 17.1 us -> 14.1 us
  blocking collectives: 52.5 us -> 50.2 us
    all_to_all x1 -> x0, blocking collectives: 20.3 us -> none  [per_device(): lax.all_to_all(squares.reshape(ys * fsdp, 1, BLOCK), ('y', 'fsdp'), 0, 0,...]
    all_to_all x1, blocking collectives: 14.5 us -> 31.3 us  [per_device(): packed = lax.all_to_all(packed, 'z', 0, 0, tiled=True)]
    pallas_call x1, Pallas kernels: 17 us -> 0.88 us  [per_device(): pl.pallas_call(split_kernel, out_shape=jax.ShapeDtypeStruct((replicas, *t...]
    all_to_all x1 -> x2, waiting for transfers between devices: 16.3 us -> 24 us  [the longest x1 14.7 us: per_device(): lax.all_to_all(blocks.reshape(ys, zs, *tile), 'y', 0, 0, tiled=True)]
    all_to_all x1 -> x2, starting transfers between devices: 17.1 us -> 14.1 us  [the longest x1 7.65 us: per_device(): lax.all_to_all(blocks.reshape(ys, zs, *tile), 'y', 0, 0, tiled=True)]
    all_to_all x1, blocking collectives: 17.8 us -> 19 us  [per_device(): steps = lax.all_to_all(step, 'y', 0, 0, tiled=True).reshape(replicas, *tile)]
  transfers between devices with their start and end apart: 1 -> 2, of which waited for: 1 -> 2; matrix products, arithmetic and copies ran while one was open for 0% -> 0% of each run, Pallas kernels for 0% -> 0%
where the time goes in v3:
time: 95 us; the launch traced here: 94.6 us
  blocking collectives  50.2 us (53%)
  waiting for transfers between devices  24 us (25%)
  starting transfers between devices  14.1 us (15%)
  Pallas kernels  4.53 us (5%)
  local copies, waits for them, and re-layouts  1.06 us (1%)
    all_to_all x1, blocking collectives, per_device(): packed = lax.all_to_all(packed, 'z', 0, 0, tiled=True)  31.3 us
    all_to_all x1, blocking collectives, per_device(): steps = lax.all_to_all(step, 'y', 0, 0, tiled=True).reshape(replicas, *tile)  19 us
    all_to_all x1, waiting for transfers between devices, per_device(): lax.all_to_all(blocks.reshape(ys, zs, *tile), 'y', 0, 0, tiled=True)  14.7 us
    all_to_all x1, waiting for transfers between devices, per_device(): lax.all_to_all(squares.reshape(ys * fsdp, 1, BLOCK), ('y', 'fsdp'), 0, 0,...  9.3 us
    all_to_all x1, starting transfers between devices, per_device(): lax.all_to_all(blocks.reshape(ys, zs, *tile), 'y', 0, 0, tiled=True)  7.65 us
    all_to_all x1, starting transfers between devices, per_device(): lax.all_to_all(squares.reshape(ys * fsdp, 1, BLOCK), ('y', 'fsdp'), 0, 0,...  6.49 us
  transfers between devices with their start and end apart: 2, of which 2 were waited for; matrix products, arithmetic and copies ran while one was open for 0% of the time, Pallas kernels for 0%

profile of v3, /device:TPU:1, one launch (start us, length us, event | category | flops | bytes accessed | tf_op | source)
XLA Modules:
  0.0 94.6 jit_solution(9833069722721585479)
XLA Ops:
  0.6 0.0 copy-start.1
  0.6 1.0 %copy-done.1 = bf16[1,2,16,8192]{3,2,1,0:T(8,128)(2,1)S(1)} copy-done((bf16[1,2,16,8192]{3,2,1,0:T(8,128)(2,1)S(1)}, bf16[1,2,16,8192]{3,2,1,0:T(8,128)(2,1)}, u32[]{:S(2)}) %copy-start.1) | copy-done | bytes 524312
  1.7 0.0 copy-start
  1.7 0.9 split.1
  2.6 7.7 %all-to-all-start = ((bf16[8,8,4,8,128]{4,3,2,1,0:T(8,128)(2,1)}), bf16[8,8,4,8,128]{4,3,2,1,0:T(8,128)(2,1)S(1)}, u32[]{:S(2)}, u32[]{:S(2)}) async-start(bf16[8,8,4,8,128]{4,3,2,1,0:T(8,128)(2,1)} %bitcast.3), calls=%async_computation | async-start | bytes 1048576 | tf_op jit(solution)/shard_map/all_to_all | solution.py:113
  10.2 0.0 copy-done
  10.2 0.0 copy-start.2
  10.2 14.7 %all-to-all-done.received_ref = bf16[8,8,4,8,128]{4,3,2,1,0:T(8,128)(2,1)S(1)} async-done(((bf16[8,8,4,8,128]{4,3,2,1,0:T(8,128)(2,1)}), bf16[8,8,4,8,128]{4,3,2,1,0:T(8,128)(2,1)S(1)}, u32[]{:S(2)}, u32[]{:S(2)}) %all-to-all-start) | async-done | bytes 524320 | tf_op jit(solution)/shard_map/all_to_all | solution.py:113
  25.0 0.0 copy-done.2
  25.0 0.5 partial.1
  25.4 31.3 %all_to_all.20.refs_0_.refs_3_ = bf16[8,9,4,8,128]{4,3,2,1,0:T(8,128)(2,1)S(1)} all-to-all(bf16[8,9,4,8,128]{4,3,2,1,0:T(8,128)(2,1)S(1)} %partial.1), channel_id=1, replica_groups=mesh['y'=8,'z'=8,'fsdp'=8] {'z'}, dimensions={0} | all-to-all | bytes 1179648 | tf_op jit(solution)/shard_map/all_to_all | solution.py:124
  56.7 0.8 average.1
  57.5 6.5 %all-to-all-start.2 = ((f32[64,1,128]{2,1,0:T(1,128)}), f32[64,1,128]{2,1,0:T(1,128)S(1)}, u32[]{:S(2)}, u32[]{:S(2)}) async-start(f32[64,1,128]{2,1,0:T(1,128)} %bitcast.6), calls=%async_computation.2 | async-start | bytes 65536 | tf_op jit(solution)/shard_map/all_to_all | solution.py:135
  64.0 9.3 %all-to-all-done.2 = f32[64,1,128]{2,1,0:T(1,128)S(1)} async-done(((f32[64,1,128]{2,1,0:T(1,128)}), f32[64,1,128]{2,1,0:T(1,128)S(1)}, u32[]{:S(2)}, u32[]{:S(2)}) %all-to-all-start.2) | async-done | bytes 32800 | tf_op jit(solution)/shard_map/all_to_all | solution.py:135
  73.3 0.8 step.1
  74.1 19.0 %all_to_all.21 = bf16[8,8,4,8,128]{4,3,2,1,0:T(8,128)(2,1)S(1)} all-to-all(bf16[8,8,4,8,128]{4,3,2,1,0:T(8,128)(2,1)S(1)} %get-tuple-element.8), channel_id=1, replica_groups=mesh['y'=8,'z'=8,'fsdp'=8] {'y'}, dimensions={0} | all-to-all | bytes 1048576 | tf_op jit(solution)/shard_map/all_to_all | solution.py:151
  93.0 1.6 %base.1 = f32[2,16,8192]{2,1,0:T(8,128)} custom-call(bf16[64,4,8,128]{3,2,1,0:T(8,128)(2,1)S(1)} %bitcast.12, f32[2,16,8192]{2,1,0:T(8,128)S(1)} %copy-done), custom_call_target="tpu_custom_call" | custom-call | tf_op jit(solution)/shard_map/base/pallas_call | solution.py:153
  (1 shorter events, 0.0 us)
Async XLA Ops:
  0.6 1.0 %copy-start.1 = (bf16[1,2,16,8192]{3,2,1,0:T(8,128)(2,1)S(1)}, bf16[1,2,16,8192]{3,2,1,0:T(8,128)(2,1)}, u32[]{:S(2)}) copy-start(bf16[1,2,16,8192]{3,2,1,0:T(8,128)(2,1)} %param.3) | copy-start | bytes 1572868
  1.7 8.5 %copy-start = (f32[2,16,8192]{2,1,0:T(8,128)S(1)}, f32[2,16,8192]{2,1,0:T(8,128)}, u32[]{:S(2)}) copy-start(f32[2,16,8192]{2,1,0:T(8,128)} %base_ref.1) | copy-start | bytes 3145732
  2.6 22.4 %all-to-all-start = ((bf16[8,8,4,8,128]{4,3,2,1,0:T(8,128)(2,1)}), bf16[8,8,4,8,128]{4,3,2,1,0:T(8,128)(2,1)S(1)}, u32[]{:S(2)}, u32[]{:S(2)}) async-start(bf16[8,8,4,8,128]{4,3,2,1,0:T(8,128)(2,1)} %bitcast.3), calls=%async_computation | async-start | bytes 1048576 | tf_op jit(solution)/shard_map/all_to_all | solution.py:113
  10.2 14.7 %copy-start.2 = (f32[2,16,128]{2,1,0:T(8,128)S(1)}, f32[2,16,128]{2,1,0:T(8,128)}, u32[]{:S(2)}) copy-start(f32[2,16,128]{2,1,0:T(8,128)} %param.5) | copy-start | bytes 49156
  57.5 15.8 %all-to-all-start.2 = ((f32[64,1,128]{2,1,0:T(1,128)}), f32[64,1,128]{2,1,0:T(1,128)S(1)}, u32[]{:S(2)}, u32[]{:S(2)}) async-start(f32[64,1,128]{2,1,0:T(1,128)} %bitcast.6), calls=%async_computation.2 | async-start | bytes 65536 | tf_op jit(solution)/shard_map/all_to_all | solution.py:135

commit v4 on v3

v4 whole, which is shorter than its diff:
```python
import math

import jax
import jax.numpy as jnp
from jax import lax
from jax.experimental import pallas as pl
from jax.experimental.pallas import tpu as pltpu
from jax.sharding import Mesh, PartitionSpec as P

BLOCK = 128


CODE_RANGE = 448.0
EPSILON = 1e-06
OUTER_RATE = 0.7
NESTEROV = 0.9
CLIP_RMS = 0.001
SUBLANES = 8
VMEM_LIMIT = 8 * 2**20


def split_kernel(params_ref, blocks_ref, held_ref, semaphores):
    ys, lows, highs = blocks_ref.shape[:3]
    share = highs * lows
    copies = [
        pltpu.make_async_copy(
            params_ref.at[:, pl.ds(y * share, share)],
            held_ref.at[:, pl.ds(y * share, share)],
            semaphores.at[y],
        )
        for y in range(ys)
    ]
    for copy in copies:
        copy.start()
    for y in range(ys):
        copies[y].wait()
        for low in range(lows):
            for high in range(highs):
                blocks_ref[y, low, high] = held_ref[:, y * share + high * lows + low]


def partial_kernel(place_ref, received_ref, base_ref, momentum_ref, packed_ref):
    sources, blocks, groups = received_ref.shape[:3]
    peers = packed_ref.shape[0]
    for block in range(blocks):
        start = pl.multiple_of((place_ref[0] + block * place_ref[1]) * BLOCK, BLOCK)
        base = base_ref[:, :, pl.ds(start, BLOCK)].reshape(groups, SUBLANES, BLOCK)
        summed = jnp.zeros(base.shape, jnp.float32)
        for source in range(sources):
            difference = base - received_ref[source, block].astype(jnp.float32)
            largest = jnp.max(jnp.abs(difference), axis=-1, keepdims=True)
            scales = ((largest + EPSILON) / CODE_RANGE).astype(jnp.bfloat16).astype(jnp.float32)
            code_words = (difference / scales).astype(jnp.bfloat16)
            summed = summed + code_words.astype(jnp.float32) * scales
        sent = summed.astype(jnp.bfloat16)
        for peer in range(peers):
            packed_ref[peer, block] = sent
    momentum = momentum_ref[...].astype(jnp.bfloat16)
    for peer in range(peers):
        packed_ref[peer, blocks] = momentum


def average_kernel(replicas, packed_ref, averaged_ref, square_ref):
    sources = packed_ref.shape[0]
    blocks, groups = averaged_ref.shape[:2]
    squares = jnp.zeros((groups, SUBLANES, BLOCK), jnp.float32)
    for block in range(blocks):
        summed = packed_ref[0, block].astype(jnp.float32)
        for source in range(1, sources):
            summed = summed + packed_ref[source, block].astype(jnp.float32)
        averaged = summed / replicas
        averaged_ref[block] = averaged
        squares = squares + averaged * averaged
    half = groups // 2
    first = jnp.sum(jnp.sum(jnp.sum(squares[:half], axis=0), axis=0, keepdims=True), axis=-1, keepdims=True)
    second = jnp.sum(jnp.sum(jnp.sum(squares[half:], axis=0), axis=0, keepdims=True), axis=-1, keepdims=True)
    lanes = lax.broadcasted_iota(jnp.int32, square_ref.shape, 1)
    square_ref[...] = jnp.where(lanes < BLOCK // 2, first, second)


def step_kernel(limit, mine_ref, squares_ref, averaged_ref, packed_ref, momentum_ref, momentum_next_ref, step_ref):
    blocks, groups = averaged_ref.shape[:2]
    sums = jnp.sum(squares_ref[...], axis=0, keepdims=True)
    mine = mine_ref[2]
    for group in range(groups):
        layer = group * 2 // groups
        total = jnp.max(sums[:, layer * 64 : (layer + 1) * 64], axis=-1, keepdims=True)
        factor = jnp.minimum(1.0, limit / (jnp.sqrt(total) + EPSILON))
        momentum_next_ref[group] = NESTEROV * momentum_ref[group] + averaged_ref[mine, group] * factor
        for block in range(blocks):
            clipped = averaged_ref[block, group] * factor
            momentum_next = NESTEROV * packed_ref[block, blocks, group].astype(jnp.float32) + clipped
            step = (OUTER_RATE * (clipped + NESTEROV * momentum_next)).astype(jnp.bfloat16)
            for target in range(step_ref.shape[0]):
                step_ref[target, block, group] = step


def base_kernel(steps_ref, base_ref, new_base_ref):
    ys, lows, highs, groups = steps_ref.shape[:4]
    layers = base_ref.shape[0]
    for y in range(ys):
        for high in range(highs):
            for low in range(lows):
                columns = pl.ds(((y * highs + high) * lows + low) * BLOCK, BLOCK)
                for group in range(groups):
                    layer, part = divmod(group, groups // layers)
                    rows = pl.ds(part * SUBLANES, SUBLANES)
                    step = steps_ref[y, low, high, group].astype(jnp.float32)
                    new_base_ref[layer, rows, columns] = base_ref[layer, rows, columns] - step


def per_device(replica_params, outer_base, outer_momentum):
    ys, highs, lows = lax.axis_size("y"), lax.axis_size("z_hi"), lax.axis_size("z_lo")
    xs, cores = lax.axis_size("x"), lax.axis_size("core")
    replicas = ys * highs * lows
    layers, rows, width = outer_base.shape
    groups = layers * rows // SUBLANES
    limit = CLIP_RMS * math.sqrt(rows * xs * cores * width)
    params = pltpu.CompilerParams(vmem_limit_bytes=VMEM_LIMIT)
    tile = (groups, SUBLANES, BLOCK)
    vmem = pl.BlockSpec(memory_space=pltpu.VMEM)
    smem = pl.BlockSpec(memory_space=pltpu.SMEM)
    y, high, low = (lax.axis_index(name) for name in ("y", "z_hi", "z_lo"))
    place = jnp.stack([y * (highs * lows) + low, jnp.int32(lows), high]).astype(jnp.int32)

    grouped = replica_params.reshape(groups, SUBLANES, replicas, BLOCK).transpose(0, 2, 1, 3)
    blocks = pl.pallas_call(
        split_kernel,
        in_specs=[pl.BlockSpec(memory_space=pltpu.HBM)],
        out_shape=jax.ShapeDtypeStruct((ys, lows, highs, *tile), replica_params.dtype),
        scratch_shapes=[
            pltpu.VMEM((groups, replicas, SUBLANES, BLOCK), replica_params.dtype),
            pltpu.SemaphoreType.DMA((ys,)),
        ],
        compiler_params=pltpu.CompilerParams(vmem_limit_bytes=60 * 2**20),
        name="split",
    )(grouped)
    received = lax.all_to_all(
        blocks.reshape(ys * lows, highs, *tile), ("y", "z_lo"), 0, 0, tiled=True
    )
    momentum = outer_momentum.reshape(tile)

    packed = pl.pallas_call(
        partial_kernel,
        in_specs=[smem, vmem, vmem, vmem],
        out_shape=jax.ShapeDtypeStruct((highs, highs + 1, *tile), jnp.bfloat16),
        compiler_params=params,
        name="partial",
    )(place, received, outer_base, momentum)
    packed = lax.all_to_all(packed, "z_hi", 0, 0, tiled=True)

    averaged, squares = pl.pallas_call(
        lambda *refs: average_kernel(replicas, *refs),
        out_shape=(
            jax.ShapeDtypeStruct((highs, *tile), jnp.float32),
            jax.ShapeDtypeStruct((1, BLOCK), jnp.float32),
        ),
        compiler_params=params,
        name="average",
    )(packed)
    owners = ys * lows * xs
    squares = jnp.broadcast_to(lax.psum(squares, "core")[None], (owners, 1, BLOCK))
    squares = lax.all_to_all(squares, ("y", "z_lo", "x"), 0, 0, tiled=True).reshape(owners, BLOCK)

    momentum_next, step = pl.pallas_call(
        lambda *refs: step_kernel(limit, *refs),
        in_specs=[smem, vmem, vmem, vmem, vmem],
        out_shape=(
            jax.ShapeDtypeStruct(tile, jnp.float32),
            jax.ShapeDtypeStruct((ys * lows, highs, *tile), jnp.bfloat16),
        ),
        compiler_params=params,
        name="step",
    )(place, squares, averaged, packed, momentum)

    steps = lax.all_to_all(step, ("y", "z_lo"), 0, 0, tiled=True)
    chunks = 4
    new_base = pl.pallas_call(
        base_kernel,
        grid=(chunks,),
        in_specs=[
            pl.BlockSpec((ys // chunks, lows, highs, *tile), lambda i: (i, 0, 0, 0, 0, 0)),
            pl.BlockSpec((layers, rows, width // chunks), lambda i: (0, 0, i)),
        ],
        out_specs=pl.BlockSpec((layers, rows, width // chunks), lambda i: (0, 0, i)),
        out_shape=jax.ShapeDtypeStruct((layers, rows, width), jnp.float32),
        compiler_params=params,
        name="base",
    )(steps.reshape(ys, lows, highs, *tile), outer_base)
    return (new_base, momentum_next.reshape(outer_momentum.shape))


def solution(mesh):
    replicas, fsdp = mesh.devices.shape
    side = math.isqrt(replicas)
    owners, shards = ("y", "z_hi", "z_lo"), ("x", "core")
    torus = Mesh(
        mesh.devices.reshape(side, side // 2, 2, fsdp // 2, 2), owners + shards
    )
    return jax.shard_map(
        per_device,
        mesh=torus,
        in_specs=(
            P(owners, None, shards, None),
            P(None, shards, None),
            P(None, shards, owners),
        ),
        out_specs=(P(None, shards, None), P(None, shards, owners)),
        check_vma=False,
    )
```

time: 95 us -> 90.2 us (0.949); the launches traced: 94.6 us -> 88.6 us
  waiting for transfers between devices: 24 us -> 15.5 us
  blocking collectives: 50.2 us -> 56.7 us
  starting transfers between devices: 14.1 us -> 9.58 us
  Pallas kernels: 4.53 us -> 6.06 us
  local copies, waits for them, and re-layouts: 1.06 us -> 0.03 us
    all_to_all x2 -> x1, waiting for transfers between devices: 24 us -> 15.5 us  [per_device(): lax.all_to_all(blocks.reshape(ys * lows, highs, *tile), ('y', 'z_lo'), 0,...]
    psum x0 -> x1, blocking collectives: none -> 6.45 us  [per_device(): lax.psum(squares, 'core')[None]]
    all_to_all x2 -> x1, starting transfers between devices: 14.1 us -> 9.58 us  [per_device(): lax.all_to_all(blocks.reshape(ys * lows, highs, *tile), ('y', 'z_lo'), 0,...]
    pallas_call x4, Pallas kernels: 3.75 us -> 5.97 us  [the longest x1 2.02 us: per_device(): pl.pallas_call(split_kernel, in_specs=[pl.BlockSpec(memory_space=pltpu.HB...]
    unnamed x6 -> x4, local copies, waits for them, and re-layouts: 1.04 us -> 0.01 us
    all_to_all x2 -> x3, blocking collectives: 50.2 us -> 50.2 us  [the longest x1 17.6 us: per_device(): steps = lax.all_to_all(step, ('y', 'z_lo'), 0, 0, tiled=True)]
  transfers between devices with their start and end apart: 2 -> 1, of which waited for: 2 -> 1; matrix products, arithmetic and copies ran while one was open for 0% -> 0% of each run, Pallas kernels for 0% -> 0%
where the time goes in v4:
time: 90.2 us; the launch traced here: 88.6 us
  blocking collectives  56.7 us (63%)
  waiting for transfers between devices  15.5 us (17%)
  starting transfers between devices  9.58 us (11%)
  Pallas kernels  6.06 us (7%)
    all_to_all x1, blocking collectives, per_device(): steps = lax.all_to_all(step, ('y', 'z_lo'), 0, 0, tiled=True)  17.6 us
    all_to_all x1, blocking collectives, per_device(): packed = lax.all_to_all(packed, 'z_hi', 0, 0, tiled=True)  16.3 us
    all_to_all x1, blocking collectives, per_device(): lax.all_to_all(squares, ('y', 'z_lo', 'x'), 0, 0, tiled=True)  16.3 us
    all_to_all x1, waiting for transfers between devices, per_device(): lax.all_to_all(blocks.reshape(ys * lows, highs, *tile), ('y', 'z_lo'), 0,...  15.5 us
    all_to_all x1, starting transfers between devices, per_device(): lax.all_to_all(blocks.reshape(ys * lows, highs, *tile), ('y', 'z_lo'), 0,...  9.58 us
    psum x1, blocking collectives, per_device(): lax.psum(squares, 'core')[None]  6.45 us
    pallas_call x1, Pallas kernels, per_device(): pl.pallas_call(split_kernel, in_specs=[pl.BlockSpec(memory_space=pltpu.HB...  2.02 us
  transfers between devices with their start and end apart: 1, of which 1 were waited for; matrix products, arithmetic and copies ran while one was open for 0% of the time, Pallas kernels for 0%

profile of v4, /device:TPU:1, one launch (start us, length us, event | category | flops | bytes accessed | tf_op | source)
XLA Modules:
  0.0 88.6 jit_solution(1621552343536853383)
XLA Ops:
  0.6 0.0 copy-start
  0.6 2.0 %split.1 = bf16[8,2,4,4,8,128]{5,4,3,2,1,0:T(8,128)(2,1)} custom-call(bf16[4,64,8,128]{3,2,1,0:T(8,128)(2,1)} %bitcast.17), custom_call_target="tpu_custom_call" | custom-call | tf_op jit(solution)/shard_map/split/pallas_call | solution.py:127
  2.7 9.6 %all-to-all-start = ((bf16[16,4,4,8,128]{4,3,2,1,0:T(8,128)(2,1)}), bf16[16,4,4,8,128]{4,3,2,1,0:T(8,128)(2,1)S(1)}, u32[]{:S(2)}, u32[]{:S(2)}) async-start(bf16[16,4,4,8,128]{4,3,2,1,0:T(8,128)(2,1)} %bitcast.16), calls=%async_computation | async-start | bytes 1048576 | tf_op jit(solution)/shard_map/all_to_all | solution.py:138
  12.3 0.0 copy-start.1
  12.3 0.1 pad_add_fusion.place_ref.refs_0_
  12.3 15.5 %all-to-all-done.received_ref = bf16[16,4,4,8,128]{4,3,2,1,0:T(8,128)(2,1)S(1)} async-done(((bf16[16,4,4,8,128]{4,3,2,1,0:T(8,128)(2,1)}), bf16[16,4,4,8,128]{4,3,2,1,0:T(8,128)(2,1)S(1)}, u32[]{:S(2)}, u32[]{:S(2)}) %all-to-all-start) | async-done | bytes 524320 | tf_op jit(solution)/shard_map/all_to_all | solution.py:138
  27.9 0.0 copy-done
  27.9 0.0 copy-done.1
  27.9 1.0 %partial.1 = bf16[4,5,4,8,128]{4,3,2,1,0:T(8,128)(2,1)S(1)} custom-call(s32[3]{0:T(128)S(1)} %pad_add_fusion.place_ref.refs_0_, bf16[16,4,4,8,128]{4,3,2,1,0:T(8,128)(2,1)S(1)} %all-to-all-done.received_ref, f32[2,16,8192]{2,1,0:T(8,128)S(1)} %copy-done, f32[4,8,128]{2,1,0:T(8,128)S(1)} %bitcast.13), custom_call_target="tpu_custom_call" | custom-call | tf_op jit(solution)/shard_map/partial/pallas_call | solution.py:143
  28.9 16.3 %all_to_all.20.refs_0_.refs_3_ = bf16[4,5,4,8,128]{4,3,2,1,0:T(8,128)(2,1)S(1)} all-to-all(bf16[4,5,4,8,128]{4,3,2,1,0:T(8,128)(2,1)S(1)} %partial.1), channel_id=1, replica_groups=mesh['y'=8,'z_hi'=4,'z_lo'=2,'x'=4,'core'=2] {'z_hi'}, dimensions={0} | all-to-all | bytes 327680 | tf_op jit(solution)/shard_map/all_to_all | solution.py:150
  45.3 0.1 average.1
  45.4 6.5 %psum.7 = f32[128]{0:T(128)S(1)} all-reduce(f32[128]{0:T(128)S(1)} %bitcast.15), channel_id=1, replica_groups=mesh['y'=8,'z_hi'=4,'z_lo'=2,'x'=4,'core'=2] {'core'}, use_global_device_ids=true, to_apply=%region_0.0 | all-reduce | flops 128 | bytes 1024 | tf_op jit(solution)/shard_map/psum | solution.py:162
  51.8 16.3 %all_to_all.21 = f32[64,1,128]{2,1,0:T(1,128)S(1)} all-to-all(f32[64,1,128]{2,1,0:T(1,128)S(1)} %broadcast_in_dim.9), channel_id=1, replica_groups=mesh['y'=8,'z_hi'=4,'z_lo'=2,'x'=4,'core'=2] {'y','z_lo','x'}, dimensions={0} | all-to-all | bytes 65536 | tf_op jit(solution)/shard_map/all_to_all | solution.py:163
  68.1 1.3 %step.1 = (f32[4,8,128]{2,1,0:T(8,128)}, bf16[16,4,4,8,128]{4,3,2,1,0:T(8,128)(2,1)S(1)}) custom-call(s32[3]{0:T(128)S(1)} %pad_add_fusion.place_ref.refs_0_, f32[64,128]{1,0:T(8,128)S(1)} %bitcast.12, f32[4,4,8,128]{3,2,1,0:T(8,128)S(1)} %get-tuple-element.7.refs_2_, bf16[4,5,4,8,128]{4,3,2,1,0:T(8,128)(2,1)S(1)} %all_to_all.20.refs_0_.refs_3_, ...), custom_call_target="tpu_custom_call" | custom-call | tf_op jit(solution)/shard_map/step/pallas_call | solution.py:165
  69.4 17.6 %all_to_all.22 = bf16[16,4,4,8,128]{4,3,2,1,0:T(8,128)(2,1)S(1)} all-to-all(bf16[16,4,4,8,128]{4,3,2,1,0:T(8,128)(2,1)S(1)} %get-tuple-element.8), channel_id=1, replica_groups=mesh['y'=8,'z_hi'=4,'z_lo'=2,'x'=4,'core'=2] {'y','z_lo'}, dimensions={0} | all-to-all | bytes 1048576 | tf_op jit(solution)/shard_map/all_to_all | solution.py:176
  87.0 1.6 %base.1 = f32[2,16,8192]{2,1,0:T(8,128)} custom-call(bf16[8,2,4,4,8,128]{5,4,3,2,1,0:T(8,128)(2,1)S(1)} %bitcast.11, f32[2,16,8192]{2,1,0:T(8,128)S(1)} %copy-done), custom_call_target="tpu_custom_call" | custom-call | tf_op jit(solution)/shard_map/base/pallas_call | solution.py:178
  (1 shorter events, 0.0 us)
Async XLA Ops:
  0.6 27.3 %copy-start = (f32[2,16,8192]{2,1,0:T(8,128)S(1)}, f32[2,16,8192]{2,1,0:T(8,128)}, u32[]{:S(2)}) copy-start(f32[2,16,8192]{2,1,0:T(8,128)} %base_ref.3) | copy-start | bytes 3145732
  2.7 25.2 %all-to-all-start = ((bf16[16,4,4,8,128]{4,3,2,1,0:T(8,128)(2,1)}), bf16[16,4,4,8,128]{4,3,2,1,0:T(8,128)(2,1)S(1)}, u32[]{:S(2)}, u32[]{:S(2)}) async-start(bf16[16,4,4,8,128]{4,3,2,1,0:T(8,128)(2,1)} %bitcast.16), calls=%async_computation | async-start | bytes 1048576 | tf_op jit(solution)/shard_map/all_to_all | solution.py:138
  12.3 15.6 %copy-start.1 = (f32[2,16,128]{2,1,0:T(8,128)S(1)}, f32[2,16,128]{2,1,0:T(8,128)}, u32[]{:S(2)}) copy-start(f32[2,16,128]{2,1,0:T(8,128)} %param.5) | copy-start | bytes 49156

commit v5 on v4

--- a/solution.py
+++ b/solution.py
@@ -19,31 +19,38 @@
 VMEM_LIMIT = 8 * 2**20
 
 
-def split_kernel(params_ref, blocks_ref, held_ref, semaphores):
+def split_kernel(params_ref, blocks_ref, held_ref, moved_ref, in_semaphores, out_semaphores):
     ys, lows, highs = blocks_ref.shape[:3]
     share = highs * lows
-    copies = [
+    reads = [
         pltpu.make_async_copy(
-            params_ref.at[:, pl.ds(y * share, share)],
-            held_ref.at[:, pl.ds(y * share, share)],
-            semaphores.at[y],
+            params_ref.at[:, pl.ds(y * share, share)], held_ref.at[y], in_semaphores.at[y]
         )
         for y in range(ys)
     ]
-    for copy in copies:
-        copy.start()
+    writes = [
+        pltpu.make_async_copy(moved_ref.at[y], blocks_ref.at[y], out_semaphores.at[y])
+        for y in range(ys)
+    ]
+    for read in reads:
+        read.start()
     for y in range(ys):
-        copies[y].wait()
+        reads[y].wait()
         for low in range(lows):
             for high in range(highs):
-                blocks_ref[y, low, high] = held_ref[:, y * share + high * lows + low]
-
-
-def partial_kernel(place_ref, received_ref, base_ref, momentum_ref, packed_ref):
+                moved_ref[y, low, high] = held_ref[y, :, high * lows + low]
+        writes[y].start()
+    for write in writes:
+        write.wait()
+
+
+def partial_kernel(received_ref, base_ref, momentum_ref, packed_ref):
     sources, blocks, groups = received_ref.shape[:3]
     peers = packed_ref.shape[0]
+    lows = lax.axis_size("z_lo")
+    first = lax.axis_index("y") * (blocks * lows) + lax.axis_index("z_lo")
     for block in range(blocks):
-        start = pl.multiple_of((place_ref[0] + block * place_ref[1]) * BLOCK, BLOCK)
+        start = pl.multiple_of((first + block * lows) * BLOCK, BLOCK)
         base = base_ref[:, :, pl.ds(start, BLOCK)].reshape(groups, SUBLANES, BLOCK)
         summed = jnp.zeros(base.shape, jnp.float32)
         for source in range(sources):
@@ -78,10 +85,10 @@
     square_ref[...] = jnp.where(lanes < BLOCK // 2, first, second)
 
 
-def step_kernel(limit, mine_ref, squares_ref, averaged_ref, packed_ref, momentum_ref, momentum_next_ref, step_ref):
+def step_kernel(limit, squares_ref, averaged_ref, packed_ref, momentum_ref, momentum_next_ref, step_ref):
     blocks, groups = averaged_ref.shape[:2]
     sums = jnp.sum(squares_ref[...], axis=0, keepdims=True)
-    mine = mine_ref[2]
+    mine = lax.axis_index("z_hi")
     for group in range(groups):
         layer = group * 2 // groups
         total = jnp.max(sums[:, layer * 64 : (layer + 1) * 64], axis=-1, keepdims=True)
@@ -95,18 +102,30 @@
                 step_ref[target, block, group] = step
 
 
-def base_kernel(steps_ref, base_ref, new_base_ref):
+def base_kernel(steps_ref, base_ref, new_base_ref, made_ref, semaphores):
     ys, lows, highs, groups = steps_ref.shape[:4]
     layers = base_ref.shape[0]
-    for y in range(ys):
-        for high in range(highs):
-            for low in range(lows):
-                columns = pl.ds(((y * highs + high) * lows + low) * BLOCK, BLOCK)
-                for group in range(groups):
-                    layer, part = divmod(group, groups // layers)
-                    rows = pl.ds(part * SUBLANES, SUBLANES)
-                    step = steps_ref[y, low, high, group].astype(jnp.float32)
-                    new_base_ref[layer, rows, columns] = base_ref[layer, rows, columns] - step
+    chunks = semaphores.shape[0]
+    chunk = base_ref.shape[2] // chunks
+    writes = []
+    for part in range(chunks):
+        for y in range(part * ys // chunks, (part + 1) * ys // chunks):
+            for high in range(highs):
+                for low in range(lows):
+                    columns = pl.ds(((y * highs + high) * lows + low) * BLOCK, BLOCK)
+                    for group in range(groups):
+                        layer, half = divmod(group, groups // layers)
+                        rows = pl.ds(half * SUBLANES, SUBLANES)
+                        step = steps_ref[y, low, high, group].astype(jnp.float32)
+                        made_ref[layer, rows, columns] = base_ref[layer, rows, columns] - step
+        columns = pl.ds(part * chunk, chunk)
+        write = pltpu.make_async_copy(
+            made_ref.at[:, :, columns], new_base_ref.at[:, :, columns], semaphores.at[part]
+        )
+        write.start()
+        writes.append(write)
+    for write in writes:
+        write.wait()
 
 
 def per_device(replica_params, outer_base, outer_momentum):
@@ -119,22 +138,23 @@
     params = pltpu.CompilerParams(vmem_limit_bytes=VMEM_LIMIT)
     tile = (groups, SUBLANES, BLOCK)
     vmem = pl.BlockSpec(memory_space=pltpu.VMEM)
-    smem = pl.BlockSpec(memory_space=pltpu.SMEM)
-    y, high, low = (lax.axis_index(name) for name in ("y", "z_hi", "z_lo"))
-    place = jnp.stack([y * (highs * lows) + low, jnp.int32(lows), high]).astype(jnp.int32)
-
     grouped = replica_params.reshape(groups, SUBLANES, replicas, BLOCK).transpose(0, 2, 1, 3)
+    anywhere = pl.BlockSpec(memory_space=pl.ANY)
     blocks = pl.pallas_call(
         split_kernel,
-        in_specs=[pl.BlockSpec(memory_space=pltpu.HBM)],
+        in_specs=[anywhere],
+        out_specs=anywhere,
         out_shape=jax.ShapeDtypeStruct((ys, lows, highs, *tile), replica_params.dtype),
         scratch_shapes=[
-            pltpu.VMEM((groups, replicas, SUBLANES, BLOCK), replica_params.dtype),
+            pltpu.VMEM((ys, groups, highs * lows, SUBLANES, BLOCK), replica_params.dtype),
+            pltpu.VMEM((ys, lows, highs, *tile), replica_params.dtype),
+            pltpu.SemaphoreType.DMA((ys,)),
             pltpu.SemaphoreType.DMA((ys,)),
         ],
         compiler_params=pltpu.CompilerParams(vmem_limit_bytes=60 * 2**20),
         name="split",
     )(grouped)
+    blocks, outer_base = lax.optimization_barrier((blocks, outer_base))
     received = lax.all_to_all(
         blocks.reshape(ys * lows, highs, *tile), ("y", "z_lo"), 0, 0, tiled=True
     )
@@ -142,11 +162,10 @@
 
     packed = pl.pallas_call(
         partial_kernel,
-        in_specs=[smem, vmem, vmem, vmem],
         out_shape=jax.ShapeDtypeStruct((highs, highs + 1, *tile), jnp.bfloat16),
         compiler_params=params,
         name="partial",
-    )(place, received, outer_base, momentum)
+    )(received, outer_base, momentum)
     packed = lax.all_to_all(packed, "z_hi", 0, 0, tiled=True)
 
     averaged, squares = pl.pallas_call(
@@ -164,26 +183,25 @@
 
     momentum_next, step = pl.pallas_call(
         lambda *refs: step_kernel(limit, *refs),
-        in_specs=[smem, vmem, vmem, vmem, vmem],
         out_shape=(
             jax.ShapeDtypeStruct(tile, jnp.float32),
             jax.ShapeDtypeStruct((ys * lows, highs, *tile), jnp.bfloat16),
         ),
         compiler_params=params,
         name="step",
-    )(place, squares, averaged, packed, momentum)
+    )(squares, averaged, packed, momentum)
 
     steps = lax.all_to_all(step, ("y", "z_lo"), 0, 0, tiled=True)
     chunks = 4
     new_base = pl.pallas_call(
         base_kernel,
-        grid=(chunks,),
-        in_specs=[
-            pl.BlockSpec((ys // chunks, lows, highs, *tile), lambda i: (i, 0, 0, 0, 0, 0)),
-            pl.BlockSpec((layers, rows, width // chunks), lambda i: (0, 0, i)),
+        in_specs=[vmem, vmem],
+        out_specs=anywhere,
+        out_shape=jax.ShapeDtypeStruct((layers, rows, width), jnp.float32),
+        scratch_shapes=[
+            pltpu.VMEM((layers, rows, width), jnp.float32),
+            pltpu.SemaphoreType.DMA((chunks,)),
         ],
-        out_specs=pl.BlockSpec((layers, rows, width // chunks), lambda i: (0, 0, i)),
-        out_shape=jax.ShapeDtypeStruct((layers, rows, width), jnp.float32),
         compiler_params=params,
         name="base",
     )(steps.reshape(ys, lows, highs, *tile), outer_base)

time: 90.2 us -> 88.5 us (0.981)
  blocking collectives: 56.7 us -> 81.9 us
  waiting for transfers between devices: 15.5 us -> 0 us
  starting transfers between devices: 9.58 us -> 0 us
  Pallas kernels: 6.06 us -> 4.3 us
    all_to_all x0 -> x1, blocking collectives: none -> 25.2 us  [per_device(): lax.all_to_all(blocks.reshape(ys * lows, highs, *tile), ('y', 'z_lo'), 0,...]
    all_to_all x1 -> x0, waiting for transfers between devices: 15.5 us -> none  [per_device(): lax.all_to_all(blocks.reshape(ys * lows, highs, *tile), ('y', 'z_lo'), 0,...]
    all_to_all x1 -> x0, starting transfers between devices: 9.58 us -> none  [per_device(): lax.all_to_all(blocks.reshape(ys * lows, highs, *tile), ('y', 'z_lo'), 0,...]
    pallas_call x4, Pallas kernels: 5.97 us -> 4.2 us  [the longest x1 1.93 us: per_device(): pl.pallas_call(split_kernel, in_specs=[anywhere], out_specs=anywhere, out...]
  transfers between devices with their start and end apart: 1 -> 0, of which waited for: 1 -> 0; matrix products, arithmetic and copies ran while one was open for 0% -> 0% of each run, Pallas kernels for 0% -> 0%
where the time goes in v5:
time: 88.5 us; the launch traced here: 86.9 us
  blocking collectives  81.9 us (93%)
  Pallas kernels  4.3 us (5%)
    all_to_all x1, blocking collectives, per_device(): lax.all_to_all(blocks.reshape(ys * lows, highs, *tile), ('y', 'z_lo'), 0,...  25.2 us
    all_to_all x1, blocking collectives, per_device(): steps = lax.all_to_all(step, ('y', 'z_lo'), 0, 0, tiled=True)  17.6 us
    all_to_all x1, blocking collectives, per_device(): packed = lax.all_to_all(packed, 'z_hi', 0, 0, tiled=True)  16.3 us
    all_to_all x1, blocking collectives, per_device(): lax.all_to_all(squares, ('y', 'z_lo', 'x'), 0, 0, tiled=True)  16.3 us
    psum x1, blocking collectives, per_device(): lax.psum(squares, 'core')[None]  6.45 us
    pallas_call x1, Pallas kernels, per_device(): pl.pallas_call(split_kernel, in_specs=[anywhere], out_specs=anywhere, out...  1.93 us

profile of v5, /device:TPU:1, one launch (start us, length us, event | category | flops | bytes accessed | tf_op | source)
XLA Modules:
  0.0 86.9 jit_solution(14240918085021164352)
XLA Ops:
  0.6 0.0 copy-start
  0.6 1.9 %split.1 = bf16[8,2,4,4,8,128]{5,4,3,2,1,0:T(8,128)(2,1)} custom-call(bf16[4,64,8,128]{3,2,1,0:T(8,128)(2,1)} %bitcast.15), custom_call_target="tpu_custom_call" | custom-call | tf_op jit(solution)/shard_map/split/pallas_call | solution.py:143
  2.6 0.0 copy-start.1
  2.6 25.2 %all_to_all.20.received_ref = bf16[16,4,4,8,128]{4,3,2,1,0:T(8,128)(2,1)S(1)} all-to-all(bf16[16,4,4,8,128]{4,3,2,1,0:T(8,128)(2,1)} %bitcast.14), channel_id=1, replica_groups=mesh['y'=8,'z_hi'=4,'z_lo'=2,'x'=4,'core'=2] {'y','z_lo'}, dimensions={0} | all-to-all | bytes 1048576 | tf_op jit(solution)/shard_map/all_to_all | solution.py:158
  27.8 0.0 copy-done
  27.8 0.0 copy-done.1
  27.8 0.5 partial.1
  28.3 16.3 %all_to_all.21.refs_0_.refs_2_ = bf16[4,5,4,8,128]{4,3,2,1,0:T(8,128)(2,1)S(1)} all-to-all(bf16[4,5,4,8,128]{4,3,2,1,0:T(8,128)(2,1)S(1)} %partial.1), channel_id=1, replica_groups=mesh['y'=8,'z_hi'=4,'z_lo'=2,'x'=4,'core'=2] {'z_hi'}, dimensions={0} | all-to-all | bytes 327680 | tf_op jit(solution)/shard_map/all_to_all | solution.py:169
  44.6 0.1 average.1
  44.7 6.5 %psum.7 = f32[128]{0:T(128)S(1)} all-reduce(f32[128]{0:T(128)S(1)} %bitcast.13), channel_id=1, replica_groups=mesh['y'=8,'z_hi'=4,'z_lo'=2,'x'=4,'core'=2] {'core'}, use_global_device_ids=true, to_apply=%region_0.0 | all-reduce | flops 128 | bytes 1024 | tf_op jit(solution)/shard_map/psum | solution.py:181
  51.2 16.3 %all_to_all.22 = f32[64,1,128]{2,1,0:T(1,128)S(1)} all-to-all(f32[64,1,128]{2,1,0:T(1,128)S(1)} %broadcast_in_dim.9), channel_id=1, replica_groups=mesh['y'=8,'z_hi'=4,'z_lo'=2,'x'=4,'core'=2] {'y','z_lo','x'}, dimensions={0} | all-to-all | bytes 65536 | tf_op jit(solution)/shard_map/all_to_all | solution.py:182
  67.5 0.8 step.1
  68.3 17.6 %all_to_all.23 = bf16[16,4,4,8,128]{4,3,2,1,0:T(8,128)(2,1)S(1)} all-to-all(bf16[16,4,4,8,128]{4,3,2,1,0:T(8,128)(2,1)S(1)} %get-tuple-element.12), channel_id=1, replica_groups=mesh['y'=8,'z_hi'=4,'z_lo'=2,'x'=4,'core'=2] {'y','z_lo'}, dimensions={0} | all-to-all | bytes 1048576 | tf_op jit(solution)/shard_map/all_to_all | solution.py:194
  85.8 1.0 %base.1 = f32[2,16,8192]{2,1,0:T(8,128)} custom-call(bf16[8,2,4,4,8,128]{5,4,3,2,1,0:T(8,128)(2,1)S(1)} %bitcast.9, f32[2,16,8192]{2,1,0:T(8,128)S(1)} %copy-done), custom_call_target="tpu_custom_call" | custom-call | tf_op jit(solution)/shard_map/base/pallas_call | solution.py:196
  (1 shorter events, 0.0 us)
Async XLA Ops:
  0.6 27.2 %copy-start = (f32[2,16,8192]{2,1,0:T(8,128)S(1)}, f32[2,16,8192]{2,1,0:T(8,128)}, u32[]{:S(2)}) copy-start(f32[2,16,8192]{2,1,0:T(8,128)} %base_ref.1) | copy-start | bytes 3145732
  2.6 25.2 %copy-start.1 = (f32[2,16,128]{2,1,0:T(8,128)S(1)}, f32[2,16,128]{2,1,0:T(8,128)}, u32[]{:S(2)}) copy-start(f32[2,16,128]{2,1,0:T(8,128)} %param.5) | copy-start | bytes 49156

commit v6 on v5

--- a/solution.py
+++ b/solution.py
@@ -19,29 +19,12 @@
 VMEM_LIMIT = 8 * 2**20
 
 
-def split_kernel(params_ref, blocks_ref, held_ref, moved_ref, in_semaphores, out_semaphores):
+def split_kernel(params_ref, blocks_ref):
     ys, lows, highs = blocks_ref.shape[:3]
-    share = highs * lows
-    reads = [
-        pltpu.make_async_copy(
-            params_ref.at[:, pl.ds(y * share, share)], held_ref.at[y], in_semaphores.at[y]
-        )
-        for y in range(ys)
-    ]
-    writes = [
-        pltpu.make_async_copy(moved_ref.at[y], blocks_ref.at[y], out_semaphores.at[y])
-        for y in range(ys)
-    ]
-    for read in reads:
-        read.start()
     for y in range(ys):
-        reads[y].wait()
         for low in range(lows):
             for high in range(highs):
-                moved_ref[y, low, high] = held_ref[y, :, high * lows + low]
-        writes[y].start()
-    for write in writes:
-        write.wait()
+                blocks_ref[y, low, high] = params_ref[:, (y * highs + high) * lows + low]
 
 
 def partial_kernel(received_ref, base_ref, momentum_ref, packed_ref):
@@ -68,16 +51,21 @@
 
 
 def average_kernel(replicas, packed_ref, averaged_ref, square_ref):
-    sources = packed_ref.shape[0]
+    sources, cores = packed_ref.shape[:2]
     blocks, groups = averaged_ref.shape[:2]
+
+    def average(core, block):
+        summed = packed_ref[0, core, block].astype(jnp.float32)
+        for source in range(1, sources):
+            summed = summed + packed_ref[source, core, block].astype(jnp.float32)
+        return summed / replicas
+
     squares = jnp.zeros((groups, SUBLANES, BLOCK), jnp.float32)
     for block in range(blocks):
-        summed = packed_ref[0, block].astype(jnp.float32)
-        for source in range(1, sources):
-            summed = summed + packed_ref[source, block].astype(jnp.float32)
-        averaged = summed / replicas
-        averaged_ref[block] = averaged
-        squares = squares + averaged * averaged
+        averaged_ref[block] = average(lax.axis_index("core"), block)
+        for core in range(cores):
+            averaged = average(core, block)
+            squares = squares + averaged * averaged
     half = groups // 2
     first = jnp.sum(jnp.sum(jnp.sum(squares[:half], axis=0), axis=0, keepdims=True), axis=-1, keepdims=True)
     second = jnp.sum(jnp.sum(jnp.sum(squares[half:], axis=0), axis=0, keepdims=True), axis=-1, keepdims=True)
@@ -88,7 +76,7 @@
 def step_kernel(limit, squares_ref, averaged_ref, packed_ref, momentum_ref, momentum_next_ref, step_ref):
     blocks, groups = averaged_ref.shape[:2]
     sums = jnp.sum(squares_ref[...], axis=0, keepdims=True)
-    mine = lax.axis_index("z_hi")
+    mine, core = lax.axis_index("z_hi"), lax.axis_index("core")
     for group in range(groups):
         layer = group * 2 // groups
         total = jnp.max(sums[:, layer * 64 : (layer + 1) * 64], axis=-1, keepdims=True)
@@ -96,7 +84,7 @@
         momentum_next_ref[group] = NESTEROV * momentum_ref[group] + averaged_ref[mine, group] * factor
         for block in range(blocks):
             clipped = averaged_ref[block, group] * factor
-            momentum_next = NESTEROV * packed_ref[block, blocks, group].astype(jnp.float32) + clipped
+            momentum_next = NESTEROV * packed_ref[block, core, blocks, group].astype(jnp.float32) + clipped
             step = (OUTER_RATE * (clipped + NESTEROV * momentum_next)).astype(jnp.bfloat16)
             for target in range(step_ref.shape[0]):
                 step_ref[target, block, group] = step
@@ -139,22 +127,12 @@
     tile = (groups, SUBLANES, BLOCK)
     vmem = pl.BlockSpec(memory_space=pltpu.VMEM)
     grouped = replica_params.reshape(groups, SUBLANES, replicas, BLOCK).transpose(0, 2, 1, 3)
-    anywhere = pl.BlockSpec(memory_space=pl.ANY)
     blocks = pl.pallas_call(
         split_kernel,
-        in_specs=[anywhere],
-        out_specs=anywhere,
         out_shape=jax.ShapeDtypeStruct((ys, lows, highs, *tile), replica_params.dtype),
-        scratch_shapes=[
-            pltpu.VMEM((ys, groups, highs * lows, SUBLANES, BLOCK), replica_params.dtype),
-            pltpu.VMEM((ys, lows, highs, *tile), replica_params.dtype),
-            pltpu.SemaphoreType.DMA((ys,)),
-            pltpu.SemaphoreType.DMA((ys,)),
-        ],
-        compiler_params=pltpu.CompilerParams(vmem_limit_bytes=60 * 2**20),
+        compiler_params=params,
         name="split",
     )(grouped)
-    blocks, outer_base = lax.optimization_barrier((blocks, outer_base))
     received = lax.all_to_all(
         blocks.reshape(ys * lows, highs, *tile), ("y", "z_lo"), 0, 0, tiled=True
     )
@@ -162,24 +140,26 @@
 
     packed = pl.pallas_call(
         partial_kernel,
-        out_shape=jax.ShapeDtypeStruct((highs, highs + 1, *tile), jnp.bfloat16),
+        out_shape=jax.ShapeDtypeStruct((highs * cores, highs + 1, *tile), jnp.bfloat16),
         compiler_params=params,
         name="partial",
     )(received, outer_base, momentum)
-    packed = lax.all_to_all(packed, "z_hi", 0, 0, tiled=True)
-
+    packed = lax.all_to_all(packed, ("z_hi", "core"), 0, 0, tiled=True)
+    packed = packed.reshape(highs, cores, highs + 1, *tile)
+
+    owners = ys * lows * xs
     averaged, squares = pl.pallas_call(
         lambda *refs: average_kernel(replicas, *refs),
         out_shape=(
             jax.ShapeDtypeStruct((highs, *tile), jnp.float32),
-            jax.ShapeDtypeStruct((1, BLOCK), jnp.float32),
+            jax.ShapeDtypeStruct((owners, BLOCK), jnp.float32),
         ),
         compiler_params=params,
         name="average",
     )(packed)
-    owners = ys * lows * xs
-    squares = jnp.broadcast_to(lax.psum(squares, "core")[None], (owners, 1, BLOCK))
-    squares = lax.all_to_all(squares, ("y", "z_lo", "x"), 0, 0, tiled=True).reshape(owners, BLOCK)
+    squares = lax.all_to_all(
+        squares.reshape(owners, 1, BLOCK), ("y", "z_lo", "x"), 0, 0, tiled=True
+    ).reshape(owners, BLOCK)
 
     momentum_next, step = pl.pallas_call(
         lambda *refs: step_kernel(limit, *refs),
@@ -196,7 +176,7 @@
     new_base = pl.pallas_call(
         base_kernel,
         in_specs=[vmem, vmem],
-        out_specs=anywhere,
+        out_specs=pl.BlockSpec(memory_space=pl.ANY),
         out_shape=jax.ShapeDtypeStruct((layers, rows, width), jnp.float32),
         scratch_shapes=[
             pltpu.VMEM((layers, rows, width), jnp.float32),

time: 88.5 us -> 88.7 us (level)
  the two profiles are of different devices: /device:TPU:1 before, /device:TPU:2 now
where the time goes in v6:
time: 88.7 us; the launch traced here: 88.4 us
  blocking collectives  84.2 us (95%)
  Pallas kernels  2.48 us (3%)
  local copies, waits for them, and re-layouts  1.04 us (1%)
    all_to_all x1, blocking collectives, per_device(): lax.all_to_all(blocks.reshape(ys * lows, highs, *tile), ('y', 'z_lo'), 0,...  26.1 us
    all_to_all x1, blocking collectives, per_device(): packed = lax.all_to_all(packed, ('z_hi', 'core'), 0, 0, tiled=True)  22.1 us
    all_to_all x1, blocking collectives, per_device(): steps = lax.all_to_all(step, ('y', 'z_lo'), 0, 0, tiled=True)  19 us
    all_to_all x1, blocking collectives, per_device(): lax.all_to_all(squares.reshape(owners, 1, BLOCK), ('y', 'z_lo', 'x'), 0,...  17 us

profile of v6, /device:TPU:2, one launch (start us, length us, event | category | flops | bytes accessed | tf_op | source)
XLA Modules:
  0.0 88.4 jit_solution(4278957674756458306)
XLA Ops:
  0.6 0.0 copy-start.1
  0.6 1.0 %copy-done.1 = bf16[1,2,16,8192]{3,2,1,0:T(8,128)(2,1)S(1)} copy-done((bf16[1,2,16,8192]{3,2,1,0:T(8,128)(2,1)S(1)}, bf16[1,2,16,8192]{3,2,1,0:T(8,128)(2,1)}, u32[]{:S(2)}) %copy-start.1) | copy-done | bytes 524312
  1.7 0.0 copy-start
  1.7 0.1 split.1
  1.8 0.0 copy-start.2
  1.8 26.1 %all_to_all.20.received_ref = bf16[16,4,4,8,128]{4,3,2,1,0:T(8,128)(2,1)S(1)} all-to-all(bf16[16,4,4,8,128]{4,3,2,1,0:T(8,128)(2,1)S(1)} %bitcast.15), channel_id=1, replica_groups=mesh['y'=8,'z_hi'=4,'z_lo'=2,'x'=4,'core'=2] {'y','z_lo'}, dimensions={0} | all-to-all | bytes 1048576 | tf_op jit(solution)/shard_map/all_to_all | solution.py:136
  27.9 0.0 copy-done
  27.9 0.0 copy-done.2
  27.9 0.5 partial.1
  28.4 22.1 %all_to_all.21 = bf16[8,5,4,8,128]{4,3,2,1,0:T(8,128)(2,1)S(1)} all-to-all(bf16[8,5,4,8,128]{4,3,2,1,0:T(8,128)(2,1)S(1)} %partial.1), channel_id=1, replica_groups=mesh['y'=8,'z_hi'=4,'z_lo'=2,'x'=4,'core'=2] {'z_hi','core'}, dimensions={0} | all-to-all | bytes 655360 | tf_op jit(solution)/shard_map/all_to_all | solution.py:147
  50.5 0.1 average.1
  50.6 17.0 %all_to_all.22 = f32[64,1,128]{2,1,0:T(1,128)S(1)} all-to-all(f32[64,1,128]{2,1,0:T(1,128)S(1)} %bitcast.20), channel_id=1, replica_groups=mesh['y'=8,'z_hi'=4,'z_lo'=2,'x'=4,'core'=2] {'y','z_lo','x'}, dimensions={0} | all-to-all | bytes 65536 | tf_op jit(solution)/shard_map/all_to_all | solution.py:160
  67.6 0.8 step.1
  68.4 19.0 %all_to_all.23 = bf16[16,4,4,8,128]{4,3,2,1,0:T(8,128)(2,1)S(1)} all-to-all(bf16[16,4,4,8,128]{4,3,2,1,0:T(8,128)(2,1)S(1)} %get-tuple-element.8), channel_id=1, replica_groups=mesh['y'=8,'z_hi'=4,'z_lo'=2,'x'=4,'core'=2] {'y','z_lo'}, dimensions={0} | all-to-all | bytes 1048576 | tf_op jit(solution)/shard_map/all_to_all | solution.py:174
  87.4 1.0 %base.1 = f32[2,16,8192]{2,1,0:T(8,128)} custom-call(bf16[8,2,4,4,8,128]{5,4,3,2,1,0:T(8,128)(2,1)S(1)} %bitcast.14, f32[2,16,8192]{2,1,0:T(8,128)S(1)} %copy-done), custom_call_target="tpu_custom_call" | custom-call | tf_op jit(solution)/shard_map/base/pallas_call | solution.py:176
Async XLA Ops:
  0.6 1.0 %copy-start.1 = (bf16[1,2,16,8192]{3,2,1,0:T(8,128)(2,1)S(1)}, bf16[1,2,16,8192]{3,2,1,0:T(8,128)(2,1)}, u32[]{:S(2)}) copy-start(bf16[1,2,16,8192]{3,2,1,0:T(8,128)(2,1)} %param.3) | copy-start | bytes 1572868
  1.7 26.2 %copy-start = (f32[2,16,8192]{2,1,0:T(8,128)S(1)}, f32[2,16,8192]{2,1,0:T(8,128)}, u32[]{:S(2)}) copy-start(f32[2,16,8192]{2,1,0:T(8,128)} %base_ref.3) | copy-start | bytes 3145732
  1.8 26.1 %copy-start.2 = (f32[2,16,128]{2,1,0:T(8,128)S(1)}, f32[2,16,128]{2,1,0:T(8,128)}, u32[]{:S(2)}) copy-start(f32[2,16,128]{2,1,0:T(8,128)} %param.5) | copy-start | bytes 49156

commit v7 on v6

v7 whole, which is shorter than its diff:
```python
import math

import jax
import jax.numpy as jnp
from jax import lax
from jax.experimental import pallas as pl
from jax.experimental.pallas import tpu as pltpu
from jax.sharding import Mesh, PartitionSpec as P

BLOCK = 128


CODE_RANGE = 448.0
EPSILON = 1e-06
OUTER_RATE = 0.7
NESTEROV = 0.9
CLIP_RMS = 0.001
SUBLANES = 8
VMEM_LIMIT = 8 * 2**20


def split_kernel(params_ref, momentum_ref, blocks_ref):
    ys, lows, entries = blocks_ref.shape[:3]
    highs = entries - 1
    momentum = momentum_ref[...].astype(jnp.bfloat16)
    for y in range(ys):
        for low in range(lows):
            for high in range(highs):
                blocks_ref[y, low, high] = params_ref[:, (y * highs + high) * lows + low]
            blocks_ref[y, low, highs] = momentum


def partial_kernel(received_ref, base_ref, packed_ref):
    sources = received_ref.shape[0]
    peers, blocks, groups = packed_ref.shape[:3]
    lows = lax.axis_size("z_lo")
    first = lax.axis_index("y") * (blocks * lows) + lax.axis_index("z_lo")
    for block in range(blocks):
        start = pl.multiple_of((first + block * lows) * BLOCK, BLOCK)
        base = base_ref[:, :, pl.ds(start, BLOCK)].reshape(groups, SUBLANES, BLOCK)
        summed = jnp.zeros(base.shape, jnp.float32)
        for source in range(sources):
            difference = base - received_ref[source, block].astype(jnp.float32)
            largest = jnp.max(jnp.abs(difference), axis=-1, keepdims=True)
            scales = ((largest + EPSILON) / CODE_RANGE).astype(jnp.bfloat16).astype(jnp.float32)
            code_words = (difference / scales).astype(jnp.bfloat16)
            summed = summed + code_words.astype(jnp.float32) * scales
        sent = summed.astype(jnp.bfloat16)
        for peer in range(peers):
            packed_ref[peer, block] = sent


def average_kernel(replicas, packed_ref, received_ref, averaged_ref, sent_ref, momenta_ref):
    sources, blocks, groups = packed_ref.shape[:3]
    peers = sent_ref.shape[0]

    def average(block):
        summed = packed_ref[0, block].astype(jnp.float32)
        for source in range(1, sources):
            summed = summed + packed_ref[source, block].astype(jnp.float32)
        return summed / replicas

    averaged_ref[...] = average(lax.axis_index("z_hi"))
    squares = jnp.zeros((groups, SUBLANES, BLOCK), jnp.float32)
    for block in range(blocks):
        averaged = average(block)
        squares = squares + averaged * averaged
        sent = averaged.astype(jnp.bfloat16)
        for peer in range(peers):
            sent_ref[peer, block * groups : (block + 1) * groups] = sent
    half = groups // 2
    first = jnp.sum(jnp.sum(jnp.sum(squares[:half], axis=0), axis=0, keepdims=True), axis=-1, keepdims=True)
    second = jnp.sum(jnp.sum(jnp.sum(squares[half:], axis=0), axis=0, keepdims=True), axis=-1, keepdims=True)
    tile = (SUBLANES, BLOCK)
    lanes = lax.broadcasted_iota(jnp.int32, tile, 1)
    rows = lax.broadcasted_iota(jnp.int32, tile, 0)
    rest = jnp.where(lanes < BLOCK // 2, first, second)
    pieces = jnp.zeros(tile, jnp.float32)
    for piece in range(3):
        rounded = rest.astype(jnp.bfloat16).astype(jnp.float32)
        pieces = jnp.where(rows == piece, rounded, pieces)
        rest = rest - rounded
    pieces = pieces.astype(jnp.bfloat16)
    for peer in range(peers):
        sent_ref[peer, blocks * groups] = pieces
        momenta_ref[peer] = received_ref[peer, blocks]


def sum_kernel(sent_ref, sums_ref):
    sources, tiles = sent_ref.shape[:2]
    total = sent_ref[0, tiles - 1].astype(jnp.float32)
    for source in range(1, sources):
        total = total + sent_ref[source, tiles - 1].astype(jnp.float32)
    sums_ref[...] = jnp.broadcast_to(jnp.sum(total, axis=0, keepdims=True), sums_ref.shape)


def base_kernel(limit, sums_ref, sent_ref, base_ref, averaged_ref, momentum_ref, *refs):
    *momenta_refs, new_base_ref, momentum_next_ref, made_ref, semaphores = refs
    highs = len(momenta_refs)
    groups = averaged_ref.shape[0]
    layers, _, width = base_ref.shape
    lows = lax.axis_size("z_lo")
    ys = sent_ref.shape[0] // lows
    sums = jnp.sum(sums_ref[...], axis=0, keepdims=True)
    factors = []
    for layer in range(layers):
        share = BLOCK // layers
        total = jnp.max(sums[:, layer * share : (layer + 1) * share], axis=-1, keepdims=True)
        factors.append(jnp.minimum(1.0, limit / (jnp.sqrt(total) + EPSILON)))
    for group in range(groups):
        factor = factors[group * layers // groups]
        momentum_next_ref[group] = NESTEROV * momentum_ref[group] + averaged_ref[group] * factor
    chunks = semaphores.shape[0]
    chunk = width // chunks
    mine = lax.axis_index("z_hi")
    writes = []
    for part in range(chunks):
        for y in range(part * ys // chunks, (part + 1) * ys // chunks):
            for shift in range(highs):
                high = lax.rem(mine + shift, highs)
                for low in range(lows):
                    start = pl.multiple_of(((y * highs + high) * lows + low) * BLOCK, BLOCK)
                    columns = pl.ds(start, BLOCK)
                    source = y * lows + low
                    for group in range(groups):
                        layer, half = divmod(group, groups // layers)
                        rows = pl.ds(half * SUBLANES, SUBLANES)
                        averaged = sent_ref[source, high * groups + group].astype(jnp.float32)
                        clipped = averaged * factors[layer]
                        momentum = momenta_refs[shift][source, group].astype(jnp.float32)
                        momentum_next = NESTEROV * momentum + clipped
                        step = (OUTER_RATE * (clipped + NESTEROV * momentum_next)).astype(jnp.bfloat16)
                        made_ref[layer, rows, columns] = (
                            base_ref[layer, rows, columns] - step.astype(jnp.float32)
                        )
        columns = pl.ds(part * chunk, chunk)
        write = pltpu.make_async_copy(
            made_ref.at[:, :, columns], new_base_ref.at[:, :, columns], semaphores.at[part]
        )
        write.start()
        writes.append(write)
    for write in writes:
        write.wait()


def per_device(replica_params, outer_base, outer_momentum):
    ys, highs, lows = lax.axis_size("y"), lax.axis_size("z_hi"), lax.axis_size("z_lo")
    xs, cores = lax.axis_size("x"), lax.axis_size("core")
    replicas = ys * highs * lows
    layers, rows, width = outer_base.shape
    groups = layers * rows // SUBLANES
    limit = CLIP_RMS * math.sqrt(rows * xs * cores * width)
    params = pltpu.CompilerParams(vmem_limit_bytes=VMEM_LIMIT)
    tile = (groups, SUBLANES, BLOCK)
    owners = ys * lows
    momentum = outer_momentum.reshape(tile)

    grouped = replica_params.reshape(groups, SUBLANES, replicas, BLOCK).transpose(0, 2, 1, 3)
    blocks = pl.pallas_call(
        split_kernel,
        out_shape=jax.ShapeDtypeStruct((ys, lows, highs + 1, *tile), replica_params.dtype),
        compiler_params=params,
        name="split",
    )(grouped, momentum)
    received = lax.all_to_all(
        blocks.reshape(owners, highs + 1, *tile), ("y", "z_lo"), 0, 0, tiled=True
    )
    packed = pl.pallas_call(
        partial_kernel,
        out_shape=jax.ShapeDtypeStruct((highs, highs, *tile), jnp.bfloat16),
        compiler_params=params,
        name="partial",
    )(received, outer_base)
    packed = lax.all_to_all(packed, "z_hi", 0, 0, tiled=True)

    averaged, sent, momenta = pl.pallas_call(
        lambda *refs: average_kernel(replicas, *refs),
        out_shape=(
            jax.ShapeDtypeStruct(tile, jnp.float32),
            jax.ShapeDtypeStruct((owners, highs * groups + 1, SUBLANES, BLOCK), jnp.bfloat16),
            jax.ShapeDtypeStruct((owners, *tile), jnp.bfloat16),
        ),
        compiler_params=params,
        name="average",
    )(packed, received)
    sent = lax.all_to_all(sent, ("y", "z_lo"), 0, 0, tiled=True)
    all_momenta = [momenta] + [
        lax.ppermute(momenta, "z_hi", [(i, (i - shift) % highs) for i in range(highs)])
        for shift in range(1, highs)
    ]
    shards = xs * cores
    sums = pl.pallas_call(
        sum_kernel,
        out_shape=jax.ShapeDtypeStruct((shards, BLOCK), jnp.float32),
        compiler_params=params,
        name="sum",
    )(sent)
    sums = lax.all_to_all(
        sums.reshape(shards, 1, BLOCK), ("x", "core"), 0, 0, tiled=True
    ).reshape(shards, BLOCK)

    chunks = 4
    vmem = pl.BlockSpec(memory_space=pltpu.VMEM)
    new_base, momentum_next = pl.pallas_call(
        lambda *refs: base_kernel(limit, *refs),
        in_specs=[vmem] * (5 + highs),
        out_specs=(pl.BlockSpec(memory_space=pl.ANY), vmem),
        out_shape=(
            jax.ShapeDtypeStruct((layers, rows, width), jnp.float32),
            jax.ShapeDtypeStruct(tile, jnp.float32),
        ),
        scratch_shapes=[
            pltpu.VMEM((layers, rows, width), jnp.float32),
            pltpu.SemaphoreType.DMA((chunks,)),
        ],
        compiler_params=params,
        name="base",
    )(sums, sent, outer_base, averaged, momentum, *all_momenta)
    return (new_base, momentum_next.reshape(outer_momentum.shape))


def solution(mesh):
    replicas, fsdp = mesh.devices.shape
    side = math.isqrt(replicas)
    owners, shards = ("y", "z_hi", "z_lo"), ("x", "core")
    torus = Mesh(
        mesh.devices.reshape(side, side // 2, 2, fsdp // 2, 2), owners + shards
    )
    return jax.shard_map(
        per_device,
        mesh=torus,
        in_specs=(
            P(owners, None, shards, None),
            P(None, shards, None),
            P(None, shards, owners),
        ),
        out_specs=(P(None, shards, None), P(None, shards, owners)),
        check_vma=False,
    )
```

time: 88.7 us -> 84 us (0.947)
  the two profiles are of different devices: /device:TPU:2 before, /device:TPU:1 now
where the time goes in v7:
time: 84 us; the launch traced here: 83.5 us
  blocking collectives  45.3 us (54%)
  starting transfers between devices  23.4 us (28%)
  waiting for transfers between devices  8.39 us (10%)
  Pallas kernels  3.92 us (5%)
  local copies, waits for them, and re-layouts  1.76 us (2%)
    all_to_all x1, blocking collectives, per_device(): lax.all_to_all(blocks.reshape(owners, highs + 1, *tile), ('y', 'z_lo'), 0...  29.1 us
    all_to_all x1, blocking collectives, per_device(): packed = lax.all_to_all(packed, 'z_hi', 0, 0, tiled=True)  16.3 us
    ppermute x3, starting transfers between devices, per_device(): lax.ppermute(momenta, 'z_hi', [(i, (i - shift) % highs) for i in range(hi...  10.4 us
    all_to_all x1, starting transfers between devices, per_device(): lax.all_to_all(sums.reshape(shards, 1, BLOCK), ('x', 'core'), 0, 0, tiled...  9.27 us
    all_to_all x1, waiting for transfers between devices, per_device(): lax.all_to_all(sums.reshape(shards, 1, BLOCK), ('x', 'core'), 0, 0, tiled...  4.48 us
    all_to_all x1, waiting for transfers between devices, per_device(): sent = lax.all_to_all(sent, ('y', 'z_lo'), 0, 0, tiled=True)  3.9 us
    all_to_all x1, starting transfers between devices, per_device(): sent = lax.all_to_all(sent, ('y', 'z_lo'), 0, 0, tiled=True)  3.78 us
    pallas_call x1, Pallas kernels, per_device(): pl.pallas_call(lambda *refs: base_kernel(limit, *refs), in_specs=[vmem] *...  1.81 us
  transfers between devices with their start and end apart: 5, of which 2 were waited for; matrix products, arithmetic and copies ran while one was open for 0% of the time, Pallas kernels for 1%

profile of v7, /device:TPU:1, one launch (start us, length us, event | category | flops | bytes accessed | tf_op | source)
XLA Modules:
  0.0 83.5 jit_solution(10093695204977204589)
XLA Ops:
  0.6 0.0 copy-start.1
  0.6 1.0 %copy-done.1 = bf16[1,2,16,8192]{3,2,1,0:T(8,128)(2,1)S(1)} copy-done((bf16[1,2,16,8192]{3,2,1,0:T(8,128)(2,1)S(1)}, bf16[1,2,16,8192]{3,2,1,0:T(8,128)(2,1)}, u32[]{:S(2)}) %copy-start.1) | copy-done | bytes 524312
  1.7 0.0 copy-start.2
  1.7 0.7 copy-done.2
  2.4 0.0 copy-start
  2.4 0.1 split.1
  2.5 29.1 %all_to_all.20.received_ref.refs_1_ = bf16[16,5,4,8,128]{4,3,2,1,0:T(8,128)(2,1)S(1)} all-to-all(bf16[16,5,4,8,128]{4,3,2,1,0:T(8,128)(2,1)S(1)} %bitcast.10), channel_id=1, replica_groups=mesh['y'=8,'z_hi'=4,'z_lo'=2,'x'=4,'core'=2] {'y','z_lo'}, dimensions={0} | all-to-all | bytes 1310720 | tf_op jit(solution)/shard_map/all_to_all | solution.py:165
  31.5 0.0 copy-done
  31.6 0.5 partial.1
  32.0 16.3 %all_to_all.21.refs_0_ = bf16[4,4,4,8,128]{4,3,2,1,0:T(8,128)(2,1)S(1)} all-to-all(bf16[4,4,4,8,128]{4,3,2,1,0:T(8,128)(2,1)S(1)} %partial.1), channel_id=1, replica_groups=mesh['y'=8,'z_hi'=4,'z_lo'=2,'x'=4,'core'=2] {'z_hi'}, dimensions={0} | all-to-all | bytes 262144 | tf_op jit(solution)/shard_map/all_to_all | solution.py:174
  48.3 0.9 %average.1 = (f32[4,8,128]{2,1,0:T(8,128)S(1)}, bf16[16,17,8,128]{3,2,1,0:T(8,128)(2,1)}, bf16[16,4,8,128]{3,2,1,0:T(8,128)(2,1)S(1)}) custom-call(bf16[4,4,4,8,128]{4,3,2,1,0:T(8,128)(2,1)S(1)} %all_to_all.21.refs_0_, bf16[16,5,4,8,128]{4,3,2,1,0:T(8,128)(2,1)S(1)} %all_to_all.20.received_ref.refs_1_), custom_call_target="tpu_custom_call" | custom-call | tf_op jit(solution)/shard_map/average/pallas_call | solution.py:176
  49.2 3.8 %all-to-all-start.2 = ((bf16[16,17,8,128]{3,2,1,0:T(8,128)(2,1)}), bf16[16,17,8,128]{3,2,1,0:T(8,128)(2,1)S(1)}, u32[]{:S(2)}, u32[]{:S(2)}) async-start(bf16[16,17,8,128]{3,2,1,0:T(8,128)(2,1)} %get-tuple-element.7), calls=%async_computation.2 | async-start | bytes 1114112 | tf_op jit(solution)/shard_map/all_to_all | solution.py:186
  53.0 3.2 %collective-permute-start.2 = (bf16[16,4,8,128]{3,2,1,0:T(8,128)(2,1)S(1)}, bf16[16,4,8,128]{3,2,1,0:T(8,128)(2,1)S(1)}, u32[]{:S(2)}, u32[]{:S(2)}) collective-permute-start(bf16[16,4,8,128]{3,2,1,0:T(8,128)(2,1)S(1)} %get-tuple-element.9.refs_5_), channel_id=1, source_target_pairs={{0,16},{16,32},{32,48},{48,0},{1,17},{17,33},{33,49},{49,1},{2,18}... | collective-permute-start | bytes 393224 | tf_op jit(solution)/shard_map/ppermute | solution.py:188
  56.2 4.0 %collective-permute-start.1 = (bf16[16,4,8,128]{3,2,1,0:T(8,128)(2,1)S(1)}, bf16[16,4,8,128]{3,2,1,0:T(8,128)(2,1)S(1)}, u32[]{:S(2)}, u32[]{:S(2)}) collective-permute-start(bf16[16,4,8,128]{3,2,1,0:T(8,128)(2,1)S(1)} %get-tuple-element.9.refs_5_), channel_id=1, source_target_pairs={{0,32},{16,48},{32,0},{48,16},{1,33},{17,49},{33,1},{49,17},{2,34}... | collective-permute-start | bytes 393224 | tf_op jit(solution)/shard_map/ppermute | solution.py:188
  60.2 3.2 %collective-permute-start = (bf16[16,4,8,128]{3,2,1,0:T(8,128)(2,1)S(1)}, bf16[16,4,8,128]{3,2,1,0:T(8,128)(2,1)S(1)}, u32[]{:S(2)}, u32[]{:S(2)}) collective-permute-start(bf16[16,4,8,128]{3,2,1,0:T(8,128)(2,1)S(1)} %get-tuple-element.9.refs_5_), channel_id=1, source_target_pairs={{0,48},{16,0},{32,16},{48,32},{1,49},{17,1},{33,17},{49,33},{2,50}... | collective-permute-start | bytes 393224 | tf_op jit(solution)/shard_map/ppermute | solution.py:188
  63.4 3.9 %all-to-all-done.2.sent_ref.refs_1_ = bf16[16,17,8,128]{3,2,1,0:T(8,128)(2,1)S(1)} async-done(((bf16[16,17,8,128]{3,2,1,0:T(8,128)(2,1)}), bf16[16,17,8,128]{3,2,1,0:T(8,128)(2,1)S(1)}, u32[]{:S(2)}, u32[]{:S(2)}) %all-to-all-start.2) | async-done | bytes 557088 | tf_op jit(solution)/shard_map/all_to_all | solution.py:186
  67.3 0.0 copy-start.3
  67.3 0.6 sum.1
  67.9 9.3 %all-to-all-start.3 = ((f32[8,1,128]{2,1,0:T(1,128)}), f32[8,1,128]{2,1,0:T(1,128)S(1)}, u32[]{:S(2)}, u32[]{:S(2)}) async-start(f32[8,1,128]{2,1,0:T(1,128)} %bitcast.5), calls=%async_computation.3 | async-start | bytes 8192 | tf_op jit(solution)/shard_map/all_to_all | solution.py:198
  77.2 0.0 collective-permute-done.2.refs_8_
  77.2 0.0 collective-permute-done.1.refs_7_
  77.2 0.0 collective-permute-done.refs_6_
  77.2 4.5 %all-to-all-done.3 = f32[8,1,128]{2,1,0:T(1,128)S(1)} async-done(((f32[8,1,128]{2,1,0:T(1,128)}), f32[8,1,128]{2,1,0:T(1,128)S(1)}, u32[]{:S(2)}, u32[]{:S(2)}) %all-to-all-start.3) | async-done | bytes 4128 | tf_op jit(solution)/shard_map/all_to_all | solution.py:198
  81.7 0.0 copy-done.3
  81.7 1.8 %base.1 = (f32[2,16,8192]{2,1,0:T(8,128)}, f32[4,8,128]{2,1,0:T(8,128)}) custom-call(f32[8,128]{1,0:T(8,128)S(1)} %bitcast.14, bf16[16,17,8,128]{3,2,1,0:T(8,128)(2,1)S(1)} %all-to-all-done.2.sent_ref.refs_1_, f32[2,16,8192]{2,1,0:T(8,128)S(1)} %copy-done, f32[4,8,128]{2,1,0:T(8,128)S(1)} %get-tuple-element.8.refs_3_, f32[4,8,128]{2,1,0:T(8,128)S(1)} %bitcast.13, ...), custom_call_target="tpu_custom_call" | custom-call | tf_op jit(solution)/shard_map/base/pallas_call | solution.py:204
Async XLA Ops:
  0.6 1.0 %copy-start.1 = (bf16[1,2,16,8192]{3,2,1,0:T(8,128)(2,1)S(1)}, bf16[1,2,16,8192]{3,2,1,0:T(8,128)(2,1)}, u32[]{:S(2)}) copy-start(bf16[1,2,16,8192]{3,2,1,0:T(8,128)(2,1)} %param.3) | copy-start | bytes 1572868
  1.7 0.7 copy-start.2
  2.4 29.2 %copy-start = (f32[2,16,8192]{2,1,0:T(8,128)S(1)}, f32[2,16,8192]{2,1,0:T(8,128)}, u32[]{:S(2)}) copy-start(f32[2,16,8192]{2,1,0:T(8,128)} %refs_2_.1) | copy-start | bytes 3145732
  49.2 18.1 %all-to-all-start.2 = ((bf16[16,17,8,128]{3,2,1,0:T(8,128)(2,1)}), bf16[16,17,8,128]{3,2,1,0:T(8,128)(2,1)S(1)}, u32[]{:S(2)}, u32[]{:S(2)}) async-start(bf16[16,17,8,128]{3,2,1,0:T(8,128)(2,1)} %get-tuple-element.7), calls=%async_computation.2 | async-start | bytes 1114112 | tf_op jit(solution)/shard_map/all_to_all | solution.py:186
  53.0 24.2 %collective-permute-start.2 = (bf16[16,4,8,128]{3,2,1,0:T(8,128)(2,1)S(1)}, bf16[16,4,8,128]{3,2,1,0:T(8,128)(2,1)S(1)}, u32[]{:S(2)}, u32[]{:S(2)}) collective-permute-start(bf16[16,4,8,128]{3,2,1,0:T(8,128)(2,1)S(1)} %get-tuple-element.9.refs_5_), channel_id=1, source_target_pairs={{0,16},{16,32},{32,48},{48,0},{1,17},{17,33},{33,49},{49,1},{2,18}... | collective-permute-start | bytes 393224 | tf_op jit(solution)/shard_map/ppermute | solution.py:188
  56.2 21.0 %collective-permute-start.1 = (bf16[16,4,8,128]{3,2,1,0:T(8,128)(2,1)S(1)}, bf16[16,4,8,128]{3,2,1,0:T(8,128)(2,1)S(1)}, u32[]{:S(2)}, u32[]{:S(2)}) collective-permute-start(bf16[16,4,8,128]{3,2,1,0:T(8,128)(2,1)S(1)} %get-tuple-element.9.refs_5_), channel_id=1, source_target_pairs={{0,32},{16,48},{32,0},{48,16},{1,33},{17,49},{33,1},{49,17},{2,34}... | collective-permute-start | bytes 393224 | tf_op jit(solution)/shard_map/ppermute | solution.py:188
  60.2 17.0 %collective-permute-start = (bf16[16,4,8,128]{3,2,1,0:T(8,128)(2,1)S(1)}, bf16[16,4,8,128]{3,2,1,0:T(8,128)(2,1)S(1)}, u32[]{:S(2)}, u32[]{:S(2)}) collective-permute-start(bf16[16,4,8,128]{3,2,1,0:T(8,128)(2,1)S(1)} %get-tuple-element.9.refs_5_), channel_id=1, source_target_pairs={{0,48},{16,0},{32,16},{48,32},{1,49},{17,1},{33,17},{49,33},{2,50}... | collective-permute-start | bytes 393224 | tf_op jit(solution)/shard_map/ppermute | solution.py:188
  67.3 14.4 %copy-start.3 = (f32[2,16,128]{2,1,0:T(8,128)S(1)}, f32[2,16,128]{2,1,0:T(8,128)}, u32[]{:S(2)}) copy-start(f32[2,16,128]{2,1,0:T(8,128)} %param.5) | copy-start | bytes 49156
  67.9 13.8 %all-to-all-start.3 = ((f32[8,1,128]{2,1,0:T(1,128)}), f32[8,1,128]{2,1,0:T(1,128)S(1)}, u32[]{:S(2)}, u32[]{:S(2)}) async-start(f32[8,1,128]{2,1,0:T(1,128)} %bitcast.5), calls=%async_computation.3 | async-start | bytes 8192 | tf_op jit(solution)/shard_map/all_to_all | solution.py:198

commit v8 on v7

--- a/solution.py
+++ b/solution.py
@@ -22,7 +22,7 @@
 def split_kernel(params_ref, momentum_ref, blocks_ref):
     ys, lows, entries = blocks_ref.shape[:3]
     highs = entries - 1
-    momentum = momentum_ref[...].astype(jnp.bfloat16)
+    momentum = momentum_ref[...]
     for y in range(ys):
         for low in range(lows):
             for high in range(highs):
@@ -107,9 +107,8 @@
         share = BLOCK // layers
         total = jnp.max(sums[:, layer * share : (layer + 1) * share], axis=-1, keepdims=True)
         factors.append(jnp.minimum(1.0, limit / (jnp.sqrt(total) + EPSILON)))
-    for group in range(groups):
-        factor = factors[group * layers // groups]
-        momentum_next_ref[group] = NESTEROV * momentum_ref[group] + averaged_ref[group] * factor
+    rates = [OUTER_RATE * (1.0 + NESTEROV) * factor for factor in factors]
+    momentum_rate = OUTER_RATE * NESTEROV * NESTEROV
     chunks = semaphores.shape[0]
     chunk = width // chunks
     mine = lax.axis_index("z_hi")
@@ -126,10 +125,8 @@
                         layer, half = divmod(group, groups // layers)
                         rows = pl.ds(half * SUBLANES, SUBLANES)
                         averaged = sent_ref[source, high * groups + group].astype(jnp.float32)
-                        clipped = averaged * factors[layer]
                         momentum = momenta_refs[shift][source, group].astype(jnp.float32)
-                        momentum_next = NESTEROV * momentum + clipped
-                        step = (OUTER_RATE * (clipped + NESTEROV * momentum_next)).astype(jnp.bfloat16)
+                        step = (averaged * rates[layer] + momentum * momentum_rate).astype(jnp.bfloat16)
                         made_ref[layer, rows, columns] = (
                             base_ref[layer, rows, columns] - step.astype(jnp.float32)
                         )
@@ -139,6 +136,9 @@
         )
         write.start()
         writes.append(write)
+    for group in range(groups):
+        factor = factors[group * layers // groups]
+        momentum_next_ref[group] = NESTEROV * momentum_ref[group] + averaged_ref[group] * factor
     for write in writes:
         write.wait()
 
@@ -161,7 +161,7 @@
         out_shape=jax.ShapeDtypeStruct((ys, lows, highs + 1, *tile), replica_params.dtype),
         compiler_params=params,
         name="split",
-    )(grouped, momentum)
+    )(grouped, momentum.astype(jnp.bfloat16))
     received = lax.all_to_all(
         blocks.reshape(owners, highs + 1, *tile), ("y", "z_lo"), 0, 0, tiled=True
     )
@@ -199,7 +199,7 @@
         sums.reshape(shards, 1, BLOCK), ("x", "core"), 0, 0, tiled=True
     ).reshape(shards, BLOCK)
 
-    chunks = 4
+    chunks = 8
     vmem = pl.BlockSpec(memory_space=pltpu.VMEM)
     new_base, momentum_next = pl.pallas_call(
         lambda *refs: base_kernel(limit, *refs),

time: 84 us -> 84 us (level)
    unnamed x8 -> x6, local copies, waits for them, and re-layouts: 1.76 us -> 1.05 us
where the time goes in v8:
time: 84 us; the launch traced here: 83.5 us
  blocking collectives  45.3 us (54%)
  starting transfers between devices  23.4 us (28%)
  waiting for transfers between devices  8.39 us (10%)
  Pallas kernels  3.88 us (5%)
  local copies, waits for them, and re-layouts  1.05 us (1%)
    all_to_all x1, blocking collectives, per_device(): lax.all_to_all(blocks.reshape(owners, highs + 1, *tile), ('y', 'z_lo'), 0...  29.1 us
    all_to_all x1, blocking collectives, per_device(): packed = lax.all_to_all(packed, 'z_hi', 0, 0, tiled=True)  16.3 us
    ppermute x3, starting transfers between devices, per_device(): lax.ppermute(momenta, 'z_hi', [(i, (i - shift) % highs) for i in range(hi...  10.4 us
    all_to_all x1, starting transfers between devices, per_device(): lax.all_to_all(sums.reshape(shards, 1, BLOCK), ('x', 'core'), 0, 0, tiled...  9.27 us
    all_to_all x1, waiting for transfers between devices, per_device(): lax.all_to_all(sums.reshape(shards, 1, BLOCK), ('x', 'core'), 0, 0, tiled...  4.48 us
    all_to_all x1, waiting for transfers between devices, per_device(): sent = lax.all_to_all(sent, ('y', 'z_lo'), 0, 0, tiled=True)  3.9 us
    all_to_all x1, starting transfers between devices, per_device(): sent = lax.all_to_all(sent, ('y', 'z_lo'), 0, 0, tiled=True)  3.78 us
    pallas_call x1, Pallas kernels, per_device(): pl.pallas_call(lambda *refs: base_kernel(limit, *refs), in_specs=[vmem] *...  1.76 us
  transfers between devices with their start and end apart: 5, of which 2 were waited for; matrix products, arithmetic and copies ran while one was open for 0% of the time, Pallas kernels for 1%

profile of v8, /device:TPU:1, one launch (start us, length us, event | category | flops | bytes accessed | tf_op | source)
XLA Modules:
  0.0 83.5 jit_solution(2594313014758511652)
XLA Ops:
  0.6 0.7 convert_element_type.3.momentum_ref
  1.4 0.0 copy-start.1
  1.4 1.0 %copy-done.1 = bf16[1,2,16,8192]{3,2,1,0:T(8,128)(2,1)S(1)} copy-done((bf16[1,2,16,8192]{3,2,1,0:T(8,128)(2,1)S(1)}, bf16[1,2,16,8192]{3,2,1,0:T(8,128)(2,1)}, u32[]{:S(2)}) %copy-start.1) | copy-done | bytes 524312
  2.4 0.0 copy-start
  2.4 0.1 split.1
  2.5 29.1 %all_to_all.20.received_ref.refs_1_ = bf16[16,5,4,8,128]{4,3,2,1,0:T(8,128)(2,1)S(1)} all-to-all(bf16[16,5,4,8,128]{4,3,2,1,0:T(8,128)(2,1)S(1)} %bitcast.10), channel_id=1, replica_groups=mesh['y'=8,'z_hi'=4,'z_lo'=2,'x'=4,'core'=2] {'y','z_lo'}, dimensions={0} | all-to-all | bytes 1310720 | tf_op jit(solution)/shard_map/all_to_all | solution.py:165
  31.6 0.0 copy-done
  31.6 0.5 partial.1
  32.0 16.3 %all_to_all.21.refs_0_ = bf16[4,4,4,8,128]{4,3,2,1,0:T(8,128)(2,1)S(1)} all-to-all(bf16[4,4,4,8,128]{4,3,2,1,0:T(8,128)(2,1)S(1)} %partial.1), channel_id=1, replica_groups=mesh['y'=8,'z_hi'=4,'z_lo'=2,'x'=4,'core'=2] {'z_hi'}, dimensions={0} | all-to-all | bytes 262144 | tf_op jit(solution)/shard_map/all_to_all | solution.py:174
  48.3 0.9 %average.1 = (f32[4,8,128]{2,1,0:T(8,128)S(1)}, bf16[16,17,8,128]{3,2,1,0:T(8,128)(2,1)}, bf16[16,4,8,128]{3,2,1,0:T(8,128)(2,1)S(1)}) custom-call(bf16[4,4,4,8,128]{4,3,2,1,0:T(8,128)(2,1)S(1)} %all_to_all.21.refs_0_, bf16[16,5,4,8,128]{4,3,2,1,0:T(8,128)(2,1)S(1)} %all_to_all.20.received_ref.refs_1_), custom_call_target="tpu_custom_call" | custom-call | tf_op jit(solution)/shard_map/average/pallas_call | solution.py:176
  49.2 3.8 %all-to-all-start.2 = ((bf16[16,17,8,128]{3,2,1,0:T(8,128)(2,1)}), bf16[16,17,8,128]{3,2,1,0:T(8,128)(2,1)S(1)}, u32[]{:S(2)}, u32[]{:S(2)}) async-start(bf16[16,17,8,128]{3,2,1,0:T(8,128)(2,1)} %get-tuple-element.7), calls=%async_computation.2 | async-start | bytes 1114112 | tf_op jit(solution)/shard_map/all_to_all | solution.py:186
  53.0 3.2 %collective-permute-start.2 = (bf16[16,4,8,128]{3,2,1,0:T(8,128)(2,1)S(1)}, bf16[16,4,8,128]{3,2,1,0:T(8,128)(2,1)S(1)}, u32[]{:S(2)}, u32[]{:S(2)}) collective-permute-start(bf16[16,4,8,128]{3,2,1,0:T(8,128)(2,1)S(1)} %get-tuple-element.9.refs_5_), channel_id=1, source_target_pairs={{0,16},{16,32},{32,48},{48,0},{1,17},{17,33},{33,49},{49,1},{2,18}... | collective-permute-start | bytes 393224 | tf_op jit(solution)/shard_map/ppermute | solution.py:188
  56.2 4.0 %collective-permute-start.1 = (bf16[16,4,8,128]{3,2,1,0:T(8,128)(2,1)S(1)}, bf16[16,4,8,128]{3,2,1,0:T(8,128)(2,1)S(1)}, u32[]{:S(2)}, u32[]{:S(2)}) collective-permute-start(bf16[16,4,8,128]{3,2,1,0:T(8,128)(2,1)S(1)} %get-tuple-element.9.refs_5_), channel_id=1, source_target_pairs={{0,32},{16,48},{32,0},{48,16},{1,33},{17,49},{33,1},{49,17},{2,34}... | collective-permute-start | bytes 393224 | tf_op jit(solution)/shard_map/ppermute | solution.py:188
  60.2 3.2 %collective-permute-start = (bf16[16,4,8,128]{3,2,1,0:T(8,128)(2,1)S(1)}, bf16[16,4,8,128]{3,2,1,0:T(8,128)(2,1)S(1)}, u32[]{:S(2)}, u32[]{:S(2)}) collective-permute-start(bf16[16,4,8,128]{3,2,1,0:T(8,128)(2,1)S(1)} %get-tuple-element.9.refs_5_), channel_id=1, source_target_pairs={{0,48},{16,0},{32,16},{48,32},{1,49},{17,1},{33,17},{49,33},{2,50}... | collective-permute-start | bytes 393224 | tf_op jit(solution)/shard_map/ppermute | solution.py:188
  63.4 3.9 %all-to-all-done.2.sent_ref.refs_1_ = bf16[16,17,8,128]{3,2,1,0:T(8,128)(2,1)S(1)} async-done(((bf16[16,17,8,128]{3,2,1,0:T(8,128)(2,1)}), bf16[16,17,8,128]{3,2,1,0:T(8,128)(2,1)S(1)}, u32[]{:S(2)}, u32[]{:S(2)}) %all-to-all-start.2) | async-done | bytes 557088 | tf_op jit(solution)/shard_map/all_to_all | solution.py:186
  67.3 0.0 copy-start.2
  67.3 0.6 sum.1
  67.9 9.3 %all-to-all-start.3 = ((f32[8,1,128]{2,1,0:T(1,128)}), f32[8,1,128]{2,1,0:T(1,128)S(1)}, u32[]{:S(2)}, u32[]{:S(2)}) async-start(f32[8,1,128]{2,1,0:T(1,128)} %bitcast.5), calls=%async_computation.3 | async-start | bytes 8192 | tf_op jit(solution)/shard_map/all_to_all | solution.py:198
  77.2 0.0 collective-permute-done.2.refs_8_
  77.2 0.0 collective-permute-done.1.refs_7_
  77.2 0.0 collective-permute-done.refs_6_
  77.2 4.5 %all-to-all-done.3 = f32[8,1,128]{2,1,0:T(1,128)S(1)} async-done(((f32[8,1,128]{2,1,0:T(1,128)}), f32[8,1,128]{2,1,0:T(1,128)S(1)}, u32[]{:S(2)}, u32[]{:S(2)}) %all-to-all-start.3) | async-done | bytes 4128 | tf_op jit(solution)/shard_map/all_to_all | solution.py:198
  81.7 0.0 copy-done.2
  81.7 1.8 %base.1 = (f32[2,16,8192]{2,1,0:T(8,128)}, f32[4,8,128]{2,1,0:T(8,128)}) custom-call(f32[8,128]{1,0:T(8,128)S(1)} %bitcast.14, bf16[16,17,8,128]{3,2,1,0:T(8,128)(2,1)S(1)} %all-to-all-done.2.sent_ref.refs_1_, f32[2,16,8192]{2,1,0:T(8,128)S(1)} %copy-done, f32[4,8,128]{2,1,0:T(8,128)S(1)} %get-tuple-element.8.refs_3_, f32[4,8,128]{2,1,0:T(8,128)S(1)} %bitcast.13, ...), custom_call_target="tpu_custom_call" | custom-call | tf_op jit(solution)/shard_map/base/pallas_call | solution.py:204
Async XLA Ops:
  1.4 1.0 %copy-start.1 = (bf16[1,2,16,8192]{3,2,1,0:T(8,128)(2,1)S(1)}, bf16[1,2,16,8192]{3,2,1,0:T(8,128)(2,1)}, u32[]{:S(2)}) copy-start(bf16[1,2,16,8192]{3,2,1,0:T(8,128)(2,1)} %param.3) | copy-start | bytes 1572868
  2.4 29.2 %copy-start = (f32[2,16,8192]{2,1,0:T(8,128)S(1)}, f32[2,16,8192]{2,1,0:T(8,128)}, u32[]{:S(2)}) copy-start(f32[2,16,8192]{2,1,0:T(8,128)} %refs_2_.1) | copy-start | bytes 3145732
  49.2 18.1 %all-to-all-start.2 = ((bf16[16,17,8,128]{3,2,1,0:T(8,128)(2,1)}), bf16[16,17,8,128]{3,2,1,0:T(8,128)(2,1)S(1)}, u32[]{:S(2)}, u32[]{:S(2)}) async-start(bf16[16,17,8,128]{3,2,1,0:T(8,128)(2,1)} %get-tuple-element.7), calls=%async_computation.2 | async-start | bytes 1114112 | tf_op jit(solution)/shard_map/all_to_all | solution.py:186
  53.0 24.2 %collective-permute-start.2 = (bf16[16,4,8,128]{3,2,1,0:T(8,128)(2,1)S(1)}, bf16[16,4,8,128]{3,2,1,0:T(8,128)(2,1)S(1)}, u32[]{:S(2)}, u32[]{:S(2)}) collective-permute-start(bf16[16,4,8,128]{3,2,1,0:T(8,128)(2,1)S(1)} %get-tuple-element.9.refs_5_), channel_id=1, source_target_pairs={{0,16},{16,32},{32,48},{48,0},{1,17},{17,33},{33,49},{49,1},{2,18}... | collective-permute-start | bytes 393224 | tf_op jit(solution)/shard_map/ppermute | solution.py:188
  56.2 21.0 %collective-permute-start.1 = (bf16[16,4,8,128]{3,2,1,0:T(8,128)(2,1)S(1)}, bf16[16,4,8,128]{3,2,1,0:T(8,128)(2,1)S(1)}, u32[]{:S(2)}, u32[]{:S(2)}) collective-permute-start(bf16[16,4,8,128]{3,2,1,0:T(8,128)(2,1)S(1)} %get-tuple-element.9.refs_5_), channel_id=1, source_target_pairs={{0,32},{16,48},{32,0},{48,16},{1,33},{17,49},{33,1},{49,17},{2,34}... | collective-permute-start | bytes 393224 | tf_op jit(solution)/shard_map/ppermute | solution.py:188
  60.2 17.0 %collective-permute-start = (bf16[16,4,8,128]{3,2,1,0:T(8,128)(2,1)S(1)}, bf16[16,4,8,128]{3,2,1,0:T(8,128)(2,1)S(1)}, u32[]{:S(2)}, u32[]{:S(2)}) collective-permute-start(bf16[16,4,8,128]{3,2,1,0:T(8,128)(2,1)S(1)} %get-tuple-element.9.refs_5_), channel_id=1, source_target_pairs={{0,48},{16,0},{32,16},{48,32},{1,49},{17,1},{33,17},{49,33},{2,50}... | collective-permute-start | bytes 393224 | tf_op jit(solution)/shard_map/ppermute | solution.py:188
  67.3 14.4 %copy-start.2 = (f32[2,16,128]{2,1,0:T(8,128)S(1)}, f32[2,16,128]{2,1,0:T(8,128)}, u32[]{:S(2)}) copy-start(f32[2,16,128]{2,1,0:T(8,128)} %param.5) | copy-start | bytes 49156
  67.9 13.8 %all-to-all-start.3 = ((f32[8,1,128]{2,1,0:T(1,128)}), f32[8,1,128]{2,1,0:T(1,128)S(1)}, u32[]{:S(2)}, u32[]{:S(2)}) async-start(f32[8,1,128]{2,1,0:T(1,128)} %bitcast.5), calls=%async_computation.3 | async-start | bytes 8192 | tf_op jit(solution)/shard_map/all_to_all | solution.py:198

commit v9 on v8

--- a/solution.py
+++ b/solution.py
@@ -50,9 +50,8 @@
             packed_ref[peer, block] = sent
 
 
-def average_kernel(replicas, packed_ref, received_ref, averaged_ref, sent_ref, momenta_ref):
+def average_kernel(replicas, packed_ref, received_ref, averaged_ref, rounded_ref, squares_ref, momenta_ref):
     sources, blocks, groups = packed_ref.shape[:3]
-    peers = sent_ref.shape[0]
 
     def average(block):
         summed = packed_ref[0, block].astype(jnp.float32)
@@ -65,16 +64,20 @@
     for block in range(blocks):
         averaged = average(block)
         squares = squares + averaged * averaged
-        sent = averaged.astype(jnp.bfloat16)
-        for peer in range(peers):
-            sent_ref[peer, block * groups : (block + 1) * groups] = sent
+        rounded_ref[block * groups : (block + 1) * groups] = averaged.astype(jnp.bfloat16)
     half = groups // 2
     first = jnp.sum(jnp.sum(jnp.sum(squares[:half], axis=0), axis=0, keepdims=True), axis=-1, keepdims=True)
     second = jnp.sum(jnp.sum(jnp.sum(squares[half:], axis=0), axis=0, keepdims=True), axis=-1, keepdims=True)
+    lanes = lax.broadcasted_iota(jnp.int32, squares_ref.shape, 1)
+    squares_ref[...] = jnp.where(lanes < BLOCK // 2, first, second)
+    momenta_ref[...] = received_ref[:, blocks]
+
+
+def pack_kernel(sums_ref, rounded_ref, received_ref, sent_ref, momenta_ref):
+    peers, entries = sent_ref.shape[:2]
     tile = (SUBLANES, BLOCK)
-    lanes = lax.broadcasted_iota(jnp.int32, tile, 1)
     rows = lax.broadcasted_iota(jnp.int32, tile, 0)
-    rest = jnp.where(lanes < BLOCK // 2, first, second)
+    rest = jnp.broadcast_to(jnp.sum(sums_ref[...], axis=0, keepdims=True), tile)
     pieces = jnp.zeros(tile, jnp.float32)
     for piece in range(3):
         rounded = rest.astype(jnp.bfloat16).astype(jnp.float32)
@@ -82,26 +85,23 @@
         rest = rest - rounded
     pieces = pieces.astype(jnp.bfloat16)
     for peer in range(peers):
-        sent_ref[peer, blocks * groups] = pieces
-        momenta_ref[peer] = received_ref[peer, blocks]
-
-
-def sum_kernel(sent_ref, sums_ref):
-    sources, tiles = sent_ref.shape[:2]
-    total = sent_ref[0, tiles - 1].astype(jnp.float32)
-    for source in range(1, sources):
-        total = total + sent_ref[source, tiles - 1].astype(jnp.float32)
-    sums_ref[...] = jnp.broadcast_to(jnp.sum(total, axis=0, keepdims=True), sums_ref.shape)
-
-
-def base_kernel(limit, sums_ref, sent_ref, base_ref, averaged_ref, momentum_ref, *refs):
-    *momenta_refs, new_base_ref, momentum_next_ref, made_ref, semaphores = refs
+        sent_ref[peer, : entries - 1] = rounded_ref[...]
+        sent_ref[peer, entries - 1] = pieces
+    momenta_ref[...] = received_ref[:, received_ref.shape[1] - 1]
+
+
+def base_kernel(limit, sent_ref, base_ref, averaged_ref, momentum_ref, *refs):
+    *momenta_refs, new_base_ref, momentum_next_ref, made_ref, made_momentum_ref, semaphores = refs
     highs = len(momenta_refs)
     groups = averaged_ref.shape[0]
     layers, _, width = base_ref.shape
     lows = lax.axis_size("z_lo")
     ys = sent_ref.shape[0] // lows
-    sums = jnp.sum(sums_ref[...], axis=0, keepdims=True)
+    sources, entries = sent_ref.shape[:2]
+    sums = sent_ref[0, entries - 1].astype(jnp.float32)
+    for source in range(1, sources):
+        sums = sums + sent_ref[source, entries - 1].astype(jnp.float32)
+    sums = jnp.sum(sums, axis=0, keepdims=True)
     factors = []
     for layer in range(layers):
         share = BLOCK // layers
@@ -109,10 +109,14 @@
         factors.append(jnp.minimum(1.0, limit / (jnp.sqrt(total) + EPSILON)))
     rates = [OUTER_RATE * (1.0 + NESTEROV) * factor for factor in factors]
     momentum_rate = OUTER_RATE * NESTEROV * NESTEROV
-    chunks = semaphores.shape[0]
+    for group in range(groups):
+        factor = factors[group * layers // groups]
+        made_momentum_ref[group] = NESTEROV * momentum_ref[group] + averaged_ref[group] * factor
+    chunks = semaphores.shape[0] - 1
+    writes = [pltpu.make_async_copy(made_momentum_ref, momentum_next_ref, semaphores.at[chunks])]
+    writes[0].start()
     chunk = width // chunks
     mine = lax.axis_index("z_hi")
-    writes = []
     for part in range(chunks):
         for y in range(part * ys // chunks, (part + 1) * ys // chunks):
             for shift in range(highs):
@@ -136,9 +140,6 @@
         )
         write.start()
         writes.append(write)
-    for group in range(groups):
-        factor = factors[group * layers // groups]
-        momentum_next_ref[group] = NESTEROV * momentum_ref[group] + averaged_ref[group] * factor
     for write in writes:
         write.wait()
 
@@ -153,6 +154,7 @@
     params = pltpu.CompilerParams(vmem_limit_bytes=VMEM_LIMIT)
     tile = (groups, SUBLANES, BLOCK)
     owners = ys * lows
+    anywhere = pl.BlockSpec(memory_space=pl.ANY)
     momentum = outer_momentum.reshape(tile)
 
     grouped = replica_params.reshape(groups, SUBLANES, replicas, BLOCK).transpose(0, 2, 1, 3)
@@ -173,49 +175,59 @@
     )(received, outer_base)
     packed = lax.all_to_all(packed, "z_hi", 0, 0, tiled=True)
 
-    averaged, sent, momenta = pl.pallas_call(
+    shards = xs * cores
+    spread = jax.ShapeDtypeStruct((owners, *tile), jnp.bfloat16)
+    averaged, rounded, squares, early_momenta = pl.pallas_call(
         lambda *refs: average_kernel(replicas, *refs),
         out_shape=(
             jax.ShapeDtypeStruct(tile, jnp.float32),
-            jax.ShapeDtypeStruct((owners, highs * groups + 1, SUBLANES, BLOCK), jnp.bfloat16),
-            jax.ShapeDtypeStruct((owners, *tile), jnp.bfloat16),
+            jax.ShapeDtypeStruct((highs * groups, SUBLANES, BLOCK), jnp.bfloat16),
+            jax.ShapeDtypeStruct((shards, BLOCK), jnp.float32),
+            spread,
         ),
         compiler_params=params,
         name="average",
     )(packed, received)
+    sums = lax.all_to_all(
+        squares.reshape(shards, 1, BLOCK), ("x", "core"), 0, 0, tiled=True
+    ).reshape(shards, BLOCK)
+    sent, momenta = pl.pallas_call(
+        pack_kernel,
+        out_shape=(
+            jax.ShapeDtypeStruct((owners, highs * groups + 1, SUBLANES, BLOCK), jnp.bfloat16),
+            spread,
+        ),
+        compiler_params=params,
+        name="pack",
+    )(sums, rounded, received)
     sent = lax.all_to_all(sent, ("y", "z_lo"), 0, 0, tiled=True)
     all_momenta = [momenta] + [
-        lax.ppermute(momenta, "z_hi", [(i, (i - shift) % highs) for i in range(highs)])
+        lax.ppermute(
+            early_momenta if shift == highs // 2 else momenta,
+            "z_hi",
+            [(i, (i - shift) % highs) for i in range(highs)],
+        )
         for shift in range(1, highs)
     ]
-    shards = xs * cores
-    sums = pl.pallas_call(
-        sum_kernel,
-        out_shape=jax.ShapeDtypeStruct((shards, BLOCK), jnp.float32),
-        compiler_params=params,
-        name="sum",
-    )(sent)
-    sums = lax.all_to_all(
-        sums.reshape(shards, 1, BLOCK), ("x", "core"), 0, 0, tiled=True
-    ).reshape(shards, BLOCK)
 
     chunks = 8
     vmem = pl.BlockSpec(memory_space=pltpu.VMEM)
     new_base, momentum_next = pl.pallas_call(
         lambda *refs: base_kernel(limit, *refs),
-        in_specs=[vmem] * (5 + highs),
-        out_specs=(pl.BlockSpec(memory_space=pl.ANY), vmem),
+        in_specs=[vmem] * (4 + highs),
+        out_specs=(anywhere, anywhere),
         out_shape=(
             jax.ShapeDtypeStruct((layers, rows, width), jnp.float32),
             jax.ShapeDtypeStruct(tile, jnp.float32),
         ),
         scratch_shapes=[
             pltpu.VMEM((layers, rows, width), jnp.float32),
-            pltpu.SemaphoreType.DMA((chunks,)),
+            pltpu.VMEM(tile, jnp.float32),
+            pltpu.SemaphoreType.DMA((chunks + 1,)),
         ],
         compiler_params=params,
         name="base",
-    )(sums, sent, outer_base, averaged, momentum, *all_momenta)
+    )(sent, outer_base, averaged, momentum, *all_momenta)
     return (new_base, momentum_next.reshape(outer_momentum.shape))
 
 

time: 84 us -> 89.4 us (1.064)
  blocking collectives: 45.3 us -> 57.9 us
  starting transfers between devices: 23.4 us -> 13.6 us
  waiting for transfers between devices: 8.39 us -> 12.1 us
  Pallas kernels: 3.88 us -> 2.76 us
    all_to_all x0 -> x1, blocking collectives: none -> 12.6 us  [per_device(): lax.all_to_all(squares.reshape(shards, 1, BLOCK), ('x', 'core'), 0, 0, ti...]
    ppermute x3, waiting for transfers between devices: 0.01 us -> 12.1 us  [per_device(): lax.ppermute(early_momenta if shift == highs // 2 else momenta, 'z_hi', [...]
    all_to_all x1 -> x0, starting transfers between devices: 9.27 us -> none  [per_device(): lax.all_to_all(sums.reshape(shards, 1, BLOCK), ('x', 'core'), 0, 0, tiled...]
    all_to_all x1 -> x0, waiting for transfers between devices: 4.48 us -> none  [per_device(): lax.all_to_all(sums.reshape(shards, 1, BLOCK), ('x', 'core'), 0, 0, tiled...]
    all_to_all x1, waiting for transfers between devices: 3.9 us -> 0.01 us  [per_device(): sent = lax.all_to_all(sent, ('y', 'z_lo'), 0, 0, tiled=True)]
  transfers between devices with their start and end apart: 5 -> 4, of which waited for: 2 -> 2; matrix products, arithmetic and copies ran while one was open for 0% -> 0% of each run, Pallas kernels for 1% -> 0%
where the time goes in v9:
time: 89.4 us; the launch traced here: 88.9 us
  blocking collectives  57.9 us (65%)
  starting transfers between devices  13.6 us (15%)
  waiting for transfers between devices  12.1 us (14%)
  Pallas kernels  2.76 us (3%)
  local copies, waits for them, and re-layouts  1.05 us (1%)
    all_to_all x1, blocking collectives, per_device(): lax.all_to_all(blocks.reshape(owners, highs + 1, *tile), ('y', 'z_lo'), 0...  29.1 us
    all_to_all x1, blocking collectives, per_device(): packed = lax.all_to_all(packed, 'z_hi', 0, 0, tiled=True)  16.3 us
    all_to_all x1, blocking collectives, per_device(): lax.all_to_all(squares.reshape(shards, 1, BLOCK), ('x', 'core'), 0, 0, ti...  12.6 us
    ppermute x3, waiting for transfers between devices, per_device(): lax.ppermute(early_momenta if shift == highs // 2 else momenta, 'z_hi', [...  12.1 us
    ppermute x3, starting transfers between devices, per_device(): lax.ppermute(early_momenta if shift == highs // 2 else momenta, 'z_hi', [...  9.94 us
    all_to_all x1, starting transfers between devices, per_device(): sent = lax.all_to_all(sent, ('y', 'z_lo'), 0, 0, tiled=True)  3.71 us
  transfers between devices with their start and end apart: 4, of which 2 were waited for; matrix products, arithmetic and copies ran while one was open for 0% of the time, Pallas kernels for 0%

profile of v9, /device:TPU:1, one launch (start us, length us, event | category | flops | bytes accessed | tf_op | source)
XLA Modules:
  0.0 88.9 jit_solution(2047432321837689066)
XLA Ops:
  0.6 0.7 convert_element_type.3.momentum_ref
  1.4 0.0 copy-start.1
  1.4 1.0 %copy-done.1 = bf16[1,2,16,8192]{3,2,1,0:T(8,128)(2,1)S(1)} copy-done((bf16[1,2,16,8192]{3,2,1,0:T(8,128)(2,1)S(1)}, bf16[1,2,16,8192]{3,2,1,0:T(8,128)(2,1)}, u32[]{:S(2)}) %copy-start.1) | copy-done | bytes 524312
  2.4 0.0 copy-start
  2.4 0.1 split.1
  2.5 29.1 %all_to_all.20.received_ref.refs_1_ = bf16[16,5,4,8,128]{4,3,2,1,0:T(8,128)(2,1)S(1)} all-to-all(bf16[16,5,4,8,128]{4,3,2,1,0:T(8,128)(2,1)S(1)} %bitcast.10), channel_id=1, replica_groups=mesh['y'=8,'z_hi'=4,'z_lo'=2,'x'=4,'core'=2] {'y','z_lo'}, dimensions={0} | all-to-all | bytes 1310720 | tf_op jit(solution)/shard_map/all_to_all | solution.py:167
  31.6 0.0 copy-done
  31.6 0.5 partial.1
  32.0 16.3 %all_to_all.21.refs_0_ = bf16[4,4,4,8,128]{4,3,2,1,0:T(8,128)(2,1)S(1)} all-to-all(bf16[4,4,4,8,128]{4,3,2,1,0:T(8,128)(2,1)S(1)} %partial.1), channel_id=1, replica_groups=mesh['y'=8,'z_hi'=4,'z_lo'=2,'x'=4,'core'=2] {'z_hi'}, dimensions={0} | all-to-all | bytes 262144 | tf_op jit(solution)/shard_map/all_to_all | solution.py:176
  48.3 0.1 average.1
  48.4 12.6 %all_to_all.22 = f32[8,1,128]{2,1,0:T(1,128)S(1)} all-to-all(f32[8,1,128]{2,1,0:T(1,128)S(1)} %bitcast.15), channel_id=1, replica_groups=mesh['y'=8,'z_hi'=4,'z_lo'=2,'x'=4,'core'=2] {'x','core'}, dimensions={0} | all-to-all | bytes 8192 | tf_op jit(solution)/shard_map/all_to_all | solution.py:191
  61.0 0.9 %pack.1 = (bf16[16,17,8,128]{3,2,1,0:T(8,128)(2,1)}, bf16[16,4,8,128]{3,2,1,0:T(8,128)(2,1)S(1)}) custom-call(f32[8,128]{1,0:T(8,128)S(1)} %bitcast.14, bf16[16,8,128]{2,1,0:T(8,128)(2,1)S(1)} %get-tuple-element.11.rounded_ref, bf16[16,5,4,8,128]{4,3,2,1,0:T(8,128)(2,1)S(1)} %all_to_all.20.received_ref.refs_1_), custom_call_target="tpu_custom_call" | custom-call | tf_op jit(solution)/shard_map/pack/pallas_call | solution.py:194
  61.9 0.0 copy-start.2
  61.9 3.7 %all-to-all-start.3 = ((bf16[16,17,8,128]{3,2,1,0:T(8,128)(2,1)}), bf16[16,17,8,128]{3,2,1,0:T(8,128)(2,1)S(1)}, u32[]{:S(2)}, u32[]{:S(2)}) async-start(bf16[16,17,8,128]{3,2,1,0:T(8,128)(2,1)} %get-tuple-element.12), calls=%async_computation.3 | async-start | bytes 1114112 | tf_op jit(solution)/shard_map/all_to_all | solution.py:203
  65.6 2.5 %collective-permute-start.1 = (bf16[16,4,8,128]{3,2,1,0:T(8,128)(2,1)S(1)}, bf16[16,4,8,128]{3,2,1,0:T(8,128)(2,1)S(1)}, u32[]{:S(2)}, u32[]{:S(2)}) collective-permute-start(bf16[16,4,8,128]{3,2,1,0:T(8,128)(2,1)S(1)} %get-tuple-element.15), channel_id=1, source_target_pairs={{0,32},{16,48},{32,0},{48,16},{1,33},{17,49},{33,1},{49,17},{2,34}... | collective-permute-start | bytes 393224 | tf_op jit(solution)/shard_map/ppermute | solution.py:205
  68.1 3.5 %collective-permute-start.2 = (bf16[16,4,8,128]{3,2,1,0:T(8,128)(2,1)S(1)}, bf16[16,4,8,128]{3,2,1,0:T(8,128)(2,1)S(1)}, u32[]{:S(2)}, u32[]{:S(2)}) collective-permute-start(bf16[16,4,8,128]{3,2,1,0:T(8,128)(2,1)S(1)} %get-tuple-element.14.refs_4_), channel_id=1, source_target_pairs={{0,16},{16,32},{32,48},{48,0},{1,17},{17,33},{33,49},{49,1},{2,18}... | collective-permute-start | bytes 393224 | tf_op jit(solution)/shard_map/ppermute | solution.py:205
  71.7 3.9 %collective-permute-start = (bf16[16,4,8,128]{3,2,1,0:T(8,128)(2,1)S(1)}, bf16[16,4,8,128]{3,2,1,0:T(8,128)(2,1)S(1)}, u32[]{:S(2)}, u32[]{:S(2)}) collective-permute-start(bf16[16,4,8,128]{3,2,1,0:T(8,128)(2,1)S(1)} %get-tuple-element.14.refs_4_), channel_id=1, source_target_pairs={{0,48},{16,0},{32,16},{48,32},{1,49},{17,1},{33,17},{49,33},{2,50}... | collective-permute-start | bytes 393224 | tf_op jit(solution)/shard_map/ppermute | solution.py:205
  75.6 9.8 %collective-permute-done.1.refs_6_ = bf16[16,4,8,128]{3,2,1,0:T(8,128)(2,1)S(1)} collective-permute-done((bf16[16,4,8,128]{3,2,1,0:T(8,128)(2,1)S(1)}, bf16[16,4,8,128]{3,2,1,0:T(8,128)(2,1)S(1)}, u32[]{:S(2)}, u32[]{:S(2)}) %collective-permute-start.1) | collective-permute-done | bytes 131104 | tf_op jit(solution)/shard_map/ppermute | solution.py:205
  85.3 2.4 %collective-permute-done.2.refs_7_ = bf16[16,4,8,128]{3,2,1,0:T(8,128)(2,1)S(1)} collective-permute-done((bf16[16,4,8,128]{3,2,1,0:T(8,128)(2,1)S(1)}, bf16[16,4,8,128]{3,2,1,0:T(8,128)(2,1)S(1)}, u32[]{:S(2)}, u32[]{:S(2)}) %collective-permute-start.2) | collective-permute-done | bytes 131104 | tf_op jit(solution)/shard_map/ppermute | solution.py:205
  87.7 0.0 collective-permute-done.refs_5_
  87.7 0.0 all-to-all-done.3.refs_0_
  87.7 0.0 copy-done.2
  87.7 1.2 %base.1 = (f32[2,16,8192]{2,1,0:T(8,128)}, f32[4,8,128]{2,1,0:T(8,128)}) custom-call(bf16[16,17,8,128]{3,2,1,0:T(8,128)(2,1)S(1)} %all-to-all-done.3.refs_0_, f32[2,16,8192]{2,1,0:T(8,128)S(1)} %copy-done, f32[4,8,128]{2,1,0:T(8,128)S(1)} %get-tuple-element.13.refs_2_, f32[4,8,128]{2,1,0:T(8,128)S(1)} %bitcast.13, ...), custom_call_target="tpu_custom_call" | custom-call | tf_op jit(solution)/shard_map/base/pallas_call | solution.py:215
Async XLA Ops:
  1.4 1.0 %copy-start.1 = (bf16[1,2,16,8192]{3,2,1,0:T(8,128)(2,1)S(1)}, bf16[1,2,16,8192]{3,2,1,0:T(8,128)(2,1)}, u32[]{:S(2)}) copy-start(bf16[1,2,16,8192]{3,2,1,0:T(8,128)(2,1)} %param.3) | copy-start | bytes 1572868
  2.4 29.2 %copy-start = (f32[2,16,8192]{2,1,0:T(8,128)S(1)}, f32[2,16,8192]{2,1,0:T(8,128)}, u32[]{:S(2)}) copy-start(f32[2,16,8192]{2,1,0:T(8,128)} %refs_1_.1) | copy-start | bytes 3145732
  61.9 25.8 %copy-start.2 = (f32[2,16,128]{2,1,0:T(8,128)S(1)}, f32[2,16,128]{2,1,0:T(8,128)}, u32[]{:S(2)}) copy-start(f32[2,16,128]{2,1,0:T(8,128)} %param.5) | copy-start | bytes 49156
  61.9 25.8 %all-to-all-start.3 = ((bf16[16,17,8,128]{3,2,1,0:T(8,128)(2,1)}), bf16[16,17,8,128]{3,2,1,0:T(8,128)(2,1)S(1)}, u32[]{:S(2)}, u32[]{:S(2)}) async-start(bf16[16,17,8,128]{3,2,1,0:T(8,128)(2,1)} %get-tuple-element.12), calls=%async_computation.3 | async-start | bytes 1114112 | tf_op jit(solution)/shard_map/all_to_all | solution.py:203
  65.6 19.7 %collective-permute-start.1 = (bf16[16,4,8,128]{3,2,1,0:T(8,128)(2,1)S(1)}, bf16[16,4,8,128]{3,2,1,0:T(8,128)(2,1)S(1)}, u32[]{:S(2)}, u32[]{:S(2)}) collective-permute-start(bf16[16,4,8,128]{3,2,1,0:T(8,128)(2,1)S(1)} %get-tuple-element.15), channel_id=1, source_target_pairs={{0,32},{16,48},{32,0},{48,16},{1,33},{17,49},{33,1},{49,17},{2,34}... | collective-permute-start | bytes 393224 | tf_op jit(solution)/shard_map/ppermute | solution.py:205
  68.1 19.5 %collective-permute-start.2 = (bf16[16,4,8,128]{3,2,1,0:T(8,128)(2,1)S(1)}, bf16[16,4,8,128]{3,2,1,0:T(8,128)(2,1)S(1)}, u32[]{:S(2)}, u32[]{:S(2)}) collective-permute-start(bf16[16,4,8,128]{3,2,1,0:T(8,128)(2,1)S(1)} %get-tuple-element.14.refs_4_), channel_id=1, source_target_pairs={{0,16},{16,32},{32,48},{48,0},{1,17},{17,33},{33,49},{49,1},{2,18}... | collective-permute-start | bytes 393224 | tf_op jit(solution)/shard_map/ppermute | solution.py:205
  71.7 16.0 %collective-permute-start = (bf16[16,4,8,128]{3,2,1,0:T(8,128)(2,1)S(1)}, bf16[16,4,8,128]{3,2,1,0:T(8,128)(2,1)S(1)}, u32[]{:S(2)}, u32[]{:S(2)}) collective-permute-start(bf16[16,4,8,128]{3,2,1,0:T(8,128)(2,1)S(1)} %get-tuple-element.14.refs_4_), channel_id=1, source_target_pairs={{0,48},{16,0},{32,16},{48,32},{1,49},{17,1},{33,17},{49,33},{2,50}... | collective-permute-start | bytes 393224 | tf_op jit(solution)/shard_map/ppermute | solution.py:205

commit v10 on v8

--- a/solution.py
+++ b/solution.py
@@ -95,7 +95,7 @@
 
 
 def base_kernel(limit, sums_ref, sent_ref, base_ref, averaged_ref, momentum_ref, *refs):
-    *momenta_refs, new_base_ref, momentum_next_ref, made_ref, semaphores = refs
+    *momenta_refs, new_base_ref, momentum_next_ref, made_ref, made_momentum_ref, semaphores = refs
     highs = len(momenta_refs)
     groups = averaged_ref.shape[0]
     layers, _, width = base_ref.shape
@@ -109,10 +109,14 @@
         factors.append(jnp.minimum(1.0, limit / (jnp.sqrt(total) + EPSILON)))
     rates = [OUTER_RATE * (1.0 + NESTEROV) * factor for factor in factors]
     momentum_rate = OUTER_RATE * NESTEROV * NESTEROV
-    chunks = semaphores.shape[0]
+    for group in range(groups):
+        factor = factors[group * layers // groups]
+        made_momentum_ref[group] = NESTEROV * momentum_ref[group] + averaged_ref[group] * factor
+    chunks = semaphores.shape[0] - 1
+    writes = [pltpu.make_async_copy(made_momentum_ref, momentum_next_ref, semaphores.at[chunks])]
+    writes[0].start()
     chunk = width // chunks
     mine = lax.axis_index("z_hi")
-    writes = []
     for part in range(chunks):
         for y in range(part * ys // chunks, (part + 1) * ys // chunks):
             for shift in range(highs):
@@ -136,9 +140,6 @@
         )
         write.start()
         writes.append(write)
-    for group in range(groups):
-        factor = factors[group * layers // groups]
-        momentum_next_ref[group] = NESTEROV * momentum_ref[group] + averaged_ref[group] * factor
     for write in writes:
         write.wait()
 
@@ -153,6 +154,7 @@
     params = pltpu.CompilerParams(vmem_limit_bytes=VMEM_LIMIT)
     tile = (groups, SUBLANES, BLOCK)
     owners = ys * lows
+    anywhere = pl.BlockSpec(memory_space=pl.ANY)
     momentum = outer_momentum.reshape(tile)
 
     grouped = replica_params.reshape(groups, SUBLANES, replicas, BLOCK).transpose(0, 2, 1, 3)
@@ -204,14 +206,15 @@
     new_base, momentum_next = pl.pallas_call(
         lambda *refs: base_kernel(limit, *refs),
         in_specs=[vmem] * (5 + highs),
-        out_specs=(pl.BlockSpec(memory_space=pl.ANY), vmem),
+        out_specs=(anywhere, anywhere),
         out_shape=(
             jax.ShapeDtypeStruct((layers, rows, width), jnp.float32),
             jax.ShapeDtypeStruct(tile, jnp.float32),
         ),
         scratch_shapes=[
             pltpu.VMEM((layers, rows, width), jnp.float32),
-            pltpu.SemaphoreType.DMA((chunks,)),
+            pltpu.VMEM(tile, jnp.float32),
+            pltpu.SemaphoreType.DMA((chunks + 1,)),
         ],
         compiler_params=params,
         name="base",

time: 84 us -> 83.4 us (level)
  no operation moved by 1% of the time
where the time goes in v10:
time: 83.4 us; the launch traced here: 82.9 us
  blocking collectives  45.3 us (54%)
  starting transfers between devices  23.4 us (28%)
  waiting for transfers between devices  8.39 us (10%)
  Pallas kernels  3.29 us (4%)
  local copies, waits for them, and re-layouts  1.05 us (1%)
    all_to_all x1, blocking collectives, per_device(): lax.all_to_all(blocks.reshape(owners, highs + 1, *tile), ('y', 'z_lo'), 0...  29.1 us
    all_to_all x1, blocking collectives, per_device(): packed = lax.all_to_all(packed, 'z_hi', 0, 0, tiled=True)  16.3 us
    ppermute x3, starting transfers between devices, per_device(): lax.ppermute(momenta, 'z_hi', [(i, (i - shift) % highs) for i in range(hi...  10.4 us
    all_to_all x1, starting transfers between devices, per_device(): lax.all_to_all(sums.reshape(shards, 1, BLOCK), ('x', 'core'), 0, 0, tiled...  9.27 us
    all_to_all x1, waiting for transfers between devices, per_device(): lax.all_to_all(sums.reshape(shards, 1, BLOCK), ('x', 'core'), 0, 0, tiled...  4.48 us
    all_to_all x1, waiting for transfers between devices, per_device(): sent = lax.all_to_all(sent, ('y', 'z_lo'), 0, 0, tiled=True)  3.9 us
    all_to_all x1, starting transfers between devices, per_device(): sent = lax.all_to_all(sent, ('y', 'z_lo'), 0, 0, tiled=True)  3.78 us
  transfers between devices with their start and end apart: 5, of which 2 were waited for; matrix products, arithmetic and copies ran while one was open for 0% of the time, Pallas kernels for 1%

profile of v10, /device:TPU:1, one launch (start us, length us, event | category | flops | bytes accessed | tf_op | source)
XLA Modules:
  0.0 82.9 jit_solution(2893396157866004210)
XLA Ops:
  0.6 0.7 convert_element_type.3.momentum_ref
  1.4 0.0 copy-start.1
  1.4 1.0 %copy-done.1 = bf16[1,2,16,8192]{3,2,1,0:T(8,128)(2,1)S(1)} copy-done((bf16[1,2,16,8192]{3,2,1,0:T(8,128)(2,1)S(1)}, bf16[1,2,16,8192]{3,2,1,0:T(8,128)(2,1)}, u32[]{:S(2)}) %copy-start.1) | copy-done | bytes 524312
  2.4 0.0 copy-start
  2.4 0.1 split.1
  2.5 29.1 %all_to_all.20.received_ref.refs_1_ = bf16[16,5,4,8,128]{4,3,2,1,0:T(8,128)(2,1)S(1)} all-to-all(bf16[16,5,4,8,128]{4,3,2,1,0:T(8,128)(2,1)S(1)} %bitcast.10), channel_id=1, replica_groups=mesh['y'=8,'z_hi'=4,'z_lo'=2,'x'=4,'core'=2] {'y','z_lo'}, dimensions={0} | all-to-all | bytes 1310720 | tf_op jit(solution)/shard_map/all_to_all | solution.py:167
  31.6 0.0 copy-done
  31.6 0.5 partial.1
  32.0 16.3 %all_to_all.21.refs_0_ = bf16[4,4,4,8,128]{4,3,2,1,0:T(8,128)(2,1)S(1)} all-to-all(bf16[4,4,4,8,128]{4,3,2,1,0:T(8,128)(2,1)S(1)} %partial.1), channel_id=1, replica_groups=mesh['y'=8,'z_hi'=4,'z_lo'=2,'x'=4,'core'=2] {'z_hi'}, dimensions={0} | all-to-all | bytes 262144 | tf_op jit(solution)/shard_map/all_to_all | solution.py:176
  48.3 0.9 %average.1 = (f32[4,8,128]{2,1,0:T(8,128)S(1)}, bf16[16,17,8,128]{3,2,1,0:T(8,128)(2,1)}, bf16[16,4,8,128]{3,2,1,0:T(8,128)(2,1)S(1)}) custom-call(bf16[4,4,4,8,128]{4,3,2,1,0:T(8,128)(2,1)S(1)} %all_to_all.21.refs_0_, bf16[16,5,4,8,128]{4,3,2,1,0:T(8,128)(2,1)S(1)} %all_to_all.20.received_ref.refs_1_), custom_call_target="tpu_custom_call" | custom-call | tf_op jit(solution)/shard_map/average/pallas_call | solution.py:178
  49.2 3.8 %all-to-all-start.2 = ((bf16[16,17,8,128]{3,2,1,0:T(8,128)(2,1)}), bf16[16,17,8,128]{3,2,1,0:T(8,128)(2,1)S(1)}, u32[]{:S(2)}, u32[]{:S(2)}) async-start(bf16[16,17,8,128]{3,2,1,0:T(8,128)(2,1)} %get-tuple-element.7), calls=%async_computation.2 | async-start | bytes 1114112 | tf_op jit(solution)/shard_map/all_to_all | solution.py:188
  53.0 3.2 %collective-permute-start.2 = (bf16[16,4,8,128]{3,2,1,0:T(8,128)(2,1)S(1)}, bf16[16,4,8,128]{3,2,1,0:T(8,128)(2,1)S(1)}, u32[]{:S(2)}, u32[]{:S(2)}) collective-permute-start(bf16[16,4,8,128]{3,2,1,0:T(8,128)(2,1)S(1)} %get-tuple-element.9.refs_5_), channel_id=1, source_target_pairs={{0,16},{16,32},{32,48},{48,0},{1,17},{17,33},{33,49},{49,1},{2,18}... | collective-permute-start | bytes 393224 | tf_op jit(solution)/shard_map/ppermute | solution.py:190
  56.2 4.0 %collective-permute-start.1 = (bf16[16,4,8,128]{3,2,1,0:T(8,128)(2,1)S(1)}, bf16[16,4,8,128]{3,2,1,0:T(8,128)(2,1)S(1)}, u32[]{:S(2)}, u32[]{:S(2)}) collective-permute-start(bf16[16,4,8,128]{3,2,1,0:T(8,128)(2,1)S(1)} %get-tuple-element.9.refs_5_), channel_id=1, source_target_pairs={{0,32},{16,48},{32,0},{48,16},{1,33},{17,49},{33,1},{49,17},{2,34}... | collective-permute-start | bytes 393224 | tf_op jit(solution)/shard_map/ppermute | solution.py:190
  60.2 3.2 %collective-permute-start = (bf16[16,4,8,128]{3,2,1,0:T(8,128)(2,1)S(1)}, bf16[16,4,8,128]{3,2,1,0:T(8,128)(2,1)S(1)}, u32[]{:S(2)}, u32[]{:S(2)}) collective-permute-start(bf16[16,4,8,128]{3,2,1,0:T(8,128)(2,1)S(1)} %get-tuple-element.9.refs_5_), channel_id=1, source_target_pairs={{0,48},{16,0},{32,16},{48,32},{1,49},{17,1},{33,17},{49,33},{2,50}... | collective-permute-start | bytes 393224 | tf_op jit(solution)/shard_map/ppermute | solution.py:190
  63.4 3.9 %all-to-all-done.2.sent_ref.refs_1_ = bf16[16,17,8,128]{3,2,1,0:T(8,128)(2,1)S(1)} async-done(((bf16[16,17,8,128]{3,2,1,0:T(8,128)(2,1)}), bf16[16,17,8,128]{3,2,1,0:T(8,128)(2,1)S(1)}, u32[]{:S(2)}, u32[]{:S(2)}) %all-to-all-start.2) | async-done | bytes 557088 | tf_op jit(solution)/shard_map/all_to_all | solution.py:188
  67.3 0.0 copy-start.2
  67.3 0.6 sum.1
  67.9 9.3 %all-to-all-start.3 = ((f32[8,1,128]{2,1,0:T(1,128)}), f32[8,1,128]{2,1,0:T(1,128)S(1)}, u32[]{:S(2)}, u32[]{:S(2)}) async-start(f32[8,1,128]{2,1,0:T(1,128)} %bitcast.5), calls=%async_computation.3 | async-start | bytes 8192 | tf_op jit(solution)/shard_map/all_to_all | solution.py:200
  77.2 0.0 collective-permute-done.2.refs_8_
  77.2 0.0 collective-permute-done.1.refs_7_
  77.2 0.0 collective-permute-done.refs_6_
  77.2 4.5 %all-to-all-done.3 = f32[8,1,128]{2,1,0:T(1,128)S(1)} async-done(((f32[8,1,128]{2,1,0:T(1,128)}), f32[8,1,128]{2,1,0:T(1,128)S(1)}, u32[]{:S(2)}, u32[]{:S(2)}) %all-to-all-start.3) | async-done | bytes 4128 | tf_op jit(solution)/shard_map/all_to_all | solution.py:200
  81.7 0.0 copy-done.2
  81.7 1.2 %base.1 = (f32[2,16,8192]{2,1,0:T(8,128)}, f32[4,8,128]{2,1,0:T(8,128)}) custom-call(f32[8,128]{1,0:T(8,128)S(1)} %bitcast.14, bf16[16,17,8,128]{3,2,1,0:T(8,128)(2,1)S(1)} %all-to-all-done.2.sent_ref.refs_1_, f32[2,16,8192]{2,1,0:T(8,128)S(1)} %copy-done, f32[4,8,128]{2,1,0:T(8,128)S(1)} %get-tuple-element.8.refs_3_, f32[4,8,128]{2,1,0:T(8,128)S(1)} %bitcast.13, ...), custom_call_target="tpu_custom_call" | custom-call | tf_op jit(solution)/shard_map/base/pallas_call | solution.py:206
Async XLA Ops:
  1.4 1.0 %copy-start.1 = (bf16[1,2,16,8192]{3,2,1,0:T(8,128)(2,1)S(1)}, bf16[1,2,16,8192]{3,2,1,0:T(8,128)(2,1)}, u32[]{:S(2)}) copy-start(bf16[1,2,16,8192]{3,2,1,0:T(8,128)(2,1)} %param.3) | copy-start | bytes 1572868
  2.4 29.2 %copy-start = (f32[2,16,8192]{2,1,0:T(8,128)S(1)}, f32[2,16,8192]{2,1,0:T(8,128)}, u32[]{:S(2)}) copy-start(f32[2,16,8192]{2,1,0:T(8,128)} %refs_2_.1) | copy-start | bytes 3145732
  49.2 18.1 %all-to-all-start.2 = ((bf16[16,17,8,128]{3,2,1,0:T(8,128)(2,1)}), bf16[16,17,8,128]{3,2,1,0:T(8,128)(2,1)S(1)}, u32[]{:S(2)}, u32[]{:S(2)}) async-start(bf16[16,17,8,128]{3,2,1,0:T(8,128)(2,1)} %get-tuple-element.7), calls=%async_computation.2 | async-start | bytes 1114112 | tf_op jit(solution)/shard_map/all_to_all | solution.py:188
  53.0 24.2 %collective-permute-start.2 = (bf16[16,4,8,128]{3,2,1,0:T(8,128)(2,1)S(1)}, bf16[16,4,8,128]{3,2,1,0:T(8,128)(2,1)S(1)}, u32[]{:S(2)}, u32[]{:S(2)}) collective-permute-start(bf16[16,4,8,128]{3,2,1,0:T(8,128)(2,1)S(1)} %get-tuple-element.9.refs_5_), channel_id=1, source_target_pairs={{0,16},{16,32},{32,48},{48,0},{1,17},{17,33},{33,49},{49,1},{2,18}... | collective-permute-start | bytes 393224 | tf_op jit(solution)/shard_map/ppermute | solution.py:190
  56.2 21.0 %collective-permute-start.1 = (bf16[16,4,8,128]{3,2,1,0:T(8,128)(2,1)S(1)}, bf16[16,4,8,128]{3,2,1,0:T(8,128)(2,1)S(1)}, u32[]{:S(2)}, u32[]{:S(2)}) collective-permute-start(bf16[16,4,8,128]{3,2,1,0:T(8,128)(2,1)S(1)} %get-tuple-element.9.refs_5_), channel_id=1, source_target_pairs={{0,32},{16,48},{32,0},{48,16},{1,33},{17,49},{33,1},{49,17},{2,34}... | collective-permute-start | bytes 393224 | tf_op jit(solution)/shard_map/ppermute | solution.py:190
  60.2 17.0 %collective-permute-start = (bf16[16,4,8,128]{3,2,1,0:T(8,128)(2,1)S(1)}, bf16[16,4,8,128]{3,2,1,0:T(8,128)(2,1)S(1)}, u32[]{:S(2)}, u32[]{:S(2)}) collective-permute-start(bf16[16,4,8,128]{3,2,1,0:T(8,128)(2,1)S(1)} %get-tuple-element.9.refs_5_), channel_id=1, source_target_pairs={{0,48},{16,0},{32,16},{48,32},{1,49},{17,1},{33,17},{49,33},{2,50}... | collective-permute-start | bytes 393224 | tf_op jit(solution)/shard_map/ppermute | solution.py:190
  67.3 14.4 %copy-start.2 = (f32[2,16,128]{2,1,0:T(8,128)S(1)}, f32[2,16,128]{2,1,0:T(8,128)}, u32[]{:S(2)}) copy-start(f32[2,16,128]{2,1,0:T(8,128)} %param.5) | copy-start | bytes 49156
  67.9 13.8 %all-to-all-start.3 = ((f32[8,1,128]{2,1,0:T(1,128)}), f32[8,1,128]{2,1,0:T(1,128)S(1)}, u32[]{:S(2)}, u32[]{:S(2)}) async-start(f32[8,1,128]{2,1,0:T(1,128)} %bitcast.5), calls=%async_computation.3 | async-start | bytes 8192 | tf_op jit(solution)/shard_map/all_to_all | solution.py:200

commit v11 on v10

--- a/solution.py
+++ b/solution.py
@@ -50,7 +50,7 @@
             packed_ref[peer, block] = sent
 
 
-def average_kernel(replicas, packed_ref, received_ref, averaged_ref, sent_ref, momenta_ref):
+def average_kernel(replicas, packed_ref, received_ref, averaged_ref, sent_ref, momenta_ref, made_ref, semaphores):
     sources, blocks, groups = packed_ref.shape[:3]
     peers = sent_ref.shape[0]
 
@@ -60,14 +60,11 @@
             summed = summed + packed_ref[source, block].astype(jnp.float32)
         return summed / replicas
 
-    averaged_ref[...] = average(lax.axis_index("z_hi"))
     squares = jnp.zeros((groups, SUBLANES, BLOCK), jnp.float32)
     for block in range(blocks):
         averaged = average(block)
         squares = squares + averaged * averaged
-        sent = averaged.astype(jnp.bfloat16)
-        for peer in range(peers):
-            sent_ref[peer, block * groups : (block + 1) * groups] = sent
+        made_ref[block * groups : (block + 1) * groups] = averaged.astype(jnp.bfloat16)
     half = groups // 2
     first = jnp.sum(jnp.sum(jnp.sum(squares[:half], axis=0), axis=0, keepdims=True), axis=-1, keepdims=True)
     second = jnp.sum(jnp.sum(jnp.sum(squares[half:], axis=0), axis=0, keepdims=True), axis=-1, keepdims=True)
@@ -80,10 +77,17 @@
         rounded = rest.astype(jnp.bfloat16).astype(jnp.float32)
         pieces = jnp.where(rows == piece, rounded, pieces)
         rest = rest - rounded
-    pieces = pieces.astype(jnp.bfloat16)
-    for peer in range(peers):
-        sent_ref[peer, blocks * groups] = pieces
-        momenta_ref[peer] = received_ref[peer, blocks]
+    made_ref[blocks * groups] = pieces.astype(jnp.bfloat16)
+    writes = [
+        pltpu.make_async_copy(made_ref, sent_ref.at[peer], semaphores.at[peer])
+        for peer in range(peers)
+    ]
+    for write in writes:
+        write.start()
+    momenta_ref[...] = received_ref[:, blocks]
+    averaged_ref[...] = average(lax.axis_index("z_hi"))
+    for write in writes:
+        write.wait()
 
 
 def sum_kernel(sent_ref, sums_ref):
@@ -155,6 +159,7 @@
     tile = (groups, SUBLANES, BLOCK)
     owners = ys * lows
     anywhere = pl.BlockSpec(memory_space=pl.ANY)
+    vmem = pl.BlockSpec(memory_space=pltpu.VMEM)
     momentum = outer_momentum.reshape(tile)
 
     grouped = replica_params.reshape(groups, SUBLANES, replicas, BLOCK).transpose(0, 2, 1, 3)
@@ -182,6 +187,11 @@
             jax.ShapeDtypeStruct((owners, highs * groups + 1, SUBLANES, BLOCK), jnp.bfloat16),
             jax.ShapeDtypeStruct((owners, *tile), jnp.bfloat16),
         ),
+        out_specs=(vmem, anywhere, vmem),
+        scratch_shapes=[
+            pltpu.VMEM((highs * groups + 1, SUBLANES, BLOCK), jnp.bfloat16),
+            pltpu.SemaphoreType.DMA((owners,)),
+        ],
         compiler_params=params,
         name="average",
     )(packed, received)
@@ -202,7 +212,6 @@
     ).reshape(shards, BLOCK)
 
     chunks = 8
-    vmem = pl.BlockSpec(memory_space=pltpu.VMEM)
     new_base, momentum_next = pl.pallas_call(
         lambda *refs: base_kernel(limit, *refs),
         in_specs=[vmem] * (5 + highs),

time: 83.4 us -> 83.5 us (level)
  no operation moved by 1% of the time
where the time goes in v11:
time: 83.5 us; the launch traced here: 83 us
  blocking collectives  45.3 us (54%)
  starting transfers between devices  23.4 us (28%)
  waiting for transfers between devices  8.39 us (10%)
  Pallas kernels  3.4 us (4%)
  local copies, waits for them, and re-layouts  1.05 us (1%)
    all_to_all x1, blocking collectives, per_device(): lax.all_to_all(blocks.reshape(owners, highs + 1, *tile), ('y', 'z_lo'), 0...  29.1 us
    all_to_all x1, blocking collectives, per_device(): packed = lax.all_to_all(packed, 'z_hi', 0, 0, tiled=True)  16.3 us
    ppermute x3, starting transfers between devices, per_device(): lax.ppermute(momenta, 'z_hi', [(i, (i - shift) % highs) for i in range(hi...  10.4 us
    all_to_all x1, starting transfers between devices, per_device(): lax.all_to_all(sums.reshape(shards, 1, BLOCK), ('x', 'core'), 0, 0, tiled...  9.27 us
    all_to_all x1, waiting for transfers between devices, per_device(): lax.all_to_all(sums.reshape(shards, 1, BLOCK), ('x', 'core'), 0, 0, tiled...  4.48 us
    all_to_all x1, waiting for transfers between devices, per_device(): sent = lax.all_to_all(sent, ('y', 'z_lo'), 0, 0, tiled=True)  3.9 us
    all_to_all x1, starting transfers between devices, per_device(): sent = lax.all_to_all(sent, ('y', 'z_lo'), 0, 0, tiled=True)  3.79 us
  transfers between devices with their start and end apart: 5, of which 2 were waited for; matrix products, arithmetic and copies ran while one was open for 0% of the time, Pallas kernels for 1%

profile of v11, /device:TPU:1, one launch (start us, length us, event | category | flops | bytes accessed | tf_op | source)
XLA Modules:
  0.0 83.0 jit_solution(2719029846131644113)
XLA Ops:
  0.6 0.7 convert_element_type.3.momentum_ref
  1.4 0.0 copy-start.1
  1.4 1.0 %copy-done.1 = bf16[1,2,16,8192]{3,2,1,0:T(8,128)(2,1)S(1)} copy-done((bf16[1,2,16,8192]{3,2,1,0:T(8,128)(2,1)S(1)}, bf16[1,2,16,8192]{3,2,1,0:T(8,128)(2,1)}, u32[]{:S(2)}) %copy-start.1) | copy-done | bytes 524312
  2.4 0.0 copy-start
  2.4 0.1 split.1
  2.5 29.1 %all_to_all.20.received_ref.refs_1_ = bf16[16,5,4,8,128]{4,3,2,1,0:T(8,128)(2,1)S(1)} all-to-all(bf16[16,5,4,8,128]{4,3,2,1,0:T(8,128)(2,1)S(1)} %bitcast.10), channel_id=1, replica_groups=mesh['y'=8,'z_hi'=4,'z_lo'=2,'x'=4,'core'=2] {'y','z_lo'}, dimensions={0} | all-to-all | bytes 1310720 | tf_op jit(solution)/shard_map/all_to_all | solution.py:172
  31.6 0.0 copy-done
  31.6 0.5 partial.1
  32.0 16.3 %all_to_all.21.refs_0_ = bf16[4,4,4,8,128]{4,3,2,1,0:T(8,128)(2,1)S(1)} all-to-all(bf16[4,4,4,8,128]{4,3,2,1,0:T(8,128)(2,1)S(1)} %partial.1), channel_id=1, replica_groups=mesh['y'=8,'z_hi'=4,'z_lo'=2,'x'=4,'core'=2] {'z_hi'}, dimensions={0} | all-to-all | bytes 262144 | tf_op jit(solution)/shard_map/all_to_all | solution.py:181
  48.3 1.0 %average.1 = (f32[4,8,128]{2,1,0:T(8,128)S(1)}, bf16[16,17,8,128]{3,2,1,0:T(8,128)(2,1)}, bf16[16,4,8,128]{3,2,1,0:T(8,128)(2,1)S(1)}) custom-call(bf16[4,4,4,8,128]{4,3,2,1,0:T(8,128)(2,1)S(1)} %all_to_all.21.refs_0_, bf16[16,5,4,8,128]{4,3,2,1,0:T(8,128)(2,1)S(1)} %all_to_all.20.received_ref.refs_1_), custom_call_target="tpu_custom_call" | custom-call | tf_op jit(solution)/shard_map/average/pallas_call | solution.py:183
  49.3 3.8 %all-to-all-start.2 = ((bf16[16,17,8,128]{3,2,1,0:T(8,128)(2,1)}), bf16[16,17,8,128]{3,2,1,0:T(8,128)(2,1)S(1)}, u32[]{:S(2)}, u32[]{:S(2)}) async-start(bf16[16,17,8,128]{3,2,1,0:T(8,128)(2,1)} %get-tuple-element.7), calls=%async_computation.2 | async-start | bytes 1114112 | tf_op jit(solution)/shard_map/all_to_all | solution.py:198
  53.1 3.2 %collective-permute-start.2 = (bf16[16,4,8,128]{3,2,1,0:T(8,128)(2,1)S(1)}, bf16[16,4,8,128]{3,2,1,0:T(8,128)(2,1)S(1)}, u32[]{:S(2)}, u32[]{:S(2)}) collective-permute-start(bf16[16,4,8,128]{3,2,1,0:T(8,128)(2,1)S(1)} %get-tuple-element.9.refs_5_), channel_id=1, source_target_pairs={{0,16},{16,32},{32,48},{48,0},{1,17},{17,33},{33,49},{49,1},{2,18}... | collective-permute-start | bytes 393224 | tf_op jit(solution)/shard_map/ppermute | solution.py:200
  56.3 4.0 %collective-permute-start.1 = (bf16[16,4,8,128]{3,2,1,0:T(8,128)(2,1)S(1)}, bf16[16,4,8,128]{3,2,1,0:T(8,128)(2,1)S(1)}, u32[]{:S(2)}, u32[]{:S(2)}) collective-permute-start(bf16[16,4,8,128]{3,2,1,0:T(8,128)(2,1)S(1)} %get-tuple-element.9.refs_5_), channel_id=1, source_target_pairs={{0,32},{16,48},{32,0},{48,16},{1,33},{17,49},{33,1},{49,17},{2,34}... | collective-permute-start | bytes 393224 | tf_op jit(solution)/shard_map/ppermute | solution.py:200
  60.3 3.2 %collective-permute-start = (bf16[16,4,8,128]{3,2,1,0:T(8,128)(2,1)S(1)}, bf16[16,4,8,128]{3,2,1,0:T(8,128)(2,1)S(1)}, u32[]{:S(2)}, u32[]{:S(2)}) collective-permute-start(bf16[16,4,8,128]{3,2,1,0:T(8,128)(2,1)S(1)} %get-tuple-element.9.refs_5_), channel_id=1, source_target_pairs={{0,48},{16,0},{32,16},{48,32},{1,49},{17,1},{33,17},{49,33},{2,50}... | collective-permute-start | bytes 393224 | tf_op jit(solution)/shard_map/ppermute | solution.py:200
  63.5 3.9 %all-to-all-done.2.sent_ref.refs_1_ = bf16[16,17,8,128]{3,2,1,0:T(8,128)(2,1)S(1)} async-done(((bf16[16,17,8,128]{3,2,1,0:T(8,128)(2,1)}), bf16[16,17,8,128]{3,2,1,0:T(8,128)(2,1)S(1)}, u32[]{:S(2)}, u32[]{:S(2)}) %all-to-all-start.2) | async-done | bytes 557088 | tf_op jit(solution)/shard_map/all_to_all | solution.py:198
  67.5 0.0 copy-start.2
  67.5 0.6 sum.1
  68.1 9.3 %all-to-all-start.3 = ((f32[8,1,128]{2,1,0:T(1,128)}), f32[8,1,128]{2,1,0:T(1,128)S(1)}, u32[]{:S(2)}, u32[]{:S(2)}) async-start(f32[8,1,128]{2,1,0:T(1,128)} %bitcast.5), calls=%async_computation.3 | async-start | bytes 8192 | tf_op jit(solution)/shard_map/all_to_all | solution.py:210
  77.3 0.0 collective-permute-done.2.refs_8_
  77.4 0.0 collective-permute-done.1.refs_7_
  77.4 0.0 collective-permute-done.refs_6_
  77.4 4.5 %all-to-all-done.3 = f32[8,1,128]{2,1,0:T(1,128)S(1)} async-done(((f32[8,1,128]{2,1,0:T(1,128)}), f32[8,1,128]{2,1,0:T(1,128)S(1)}, u32[]{:S(2)}, u32[]{:S(2)}) %all-to-all-start.3) | async-done | bytes 4128 | tf_op jit(solution)/shard_map/all_to_all | solution.py:210
  81.8 0.0 copy-done.2
  81.8 1.2 %base.1 = (f32[2,16,8192]{2,1,0:T(8,128)}, f32[4,8,128]{2,1,0:T(8,128)}) custom-call(f32[8,128]{1,0:T(8,128)S(1)} %bitcast.14, bf16[16,17,8,128]{3,2,1,0:T(8,128)(2,1)S(1)} %all-to-all-done.2.sent_ref.refs_1_, f32[2,16,8192]{2,1,0:T(8,128)S(1)} %copy-done, f32[4,8,128]{2,1,0:T(8,128)S(1)} %get-tuple-element.8.refs_3_, f32[4,8,128]{2,1,0:T(8,128)S(1)} %bitcast.13, ...), custom_call_target="tpu_custom_call" | custom-call | tf_op jit(solution)/shard_map/base/pallas_call | solution.py:215
Async XLA Ops:
  1.4 1.0 %copy-start.1 = (bf16[1,2,16,8192]{3,2,1,0:T(8,128)(2,1)S(1)}, bf16[1,2,16,8192]{3,2,1,0:T(8,128)(2,1)}, u32[]{:S(2)}) copy-start(bf16[1,2,16,8192]{3,2,1,0:T(8,128)(2,1)} %param.3) | copy-start | bytes 1572868
  2.4 29.2 %copy-start = (f32[2,16,8192]{2,1,0:T(8,128)S(1)}, f32[2,16,8192]{2,1,0:T(8,128)}, u32[]{:S(2)}) copy-start(f32[2,16,8192]{2,1,0:T(8,128)} %refs_2_.1) | copy-start | bytes 3145732
  49.3 18.1 %all-to-all-start.2 = ((bf16[16,17,8,128]{3,2,1,0:T(8,128)(2,1)}), bf16[16,17,8,128]{3,2,1,0:T(8,128)(2,1)S(1)}, u32[]{:S(2)}, u32[]{:S(2)}) async-start(bf16[16,17,8,128]{3,2,1,0:T(8,128)(2,1)} %get-tuple-element.7), calls=%async_computation.2 | async-start | bytes 1114112 | tf_op jit(solution)/shard_map/all_to_all | solution.py:198
  53.1 24.2 %collective-permute-start.2 = (bf16[16,4,8,128]{3,2,1,0:T(8,128)(2,1)S(1)}, bf16[16,4,8,128]{3,2,1,0:T(8,128)(2,1)S(1)}, u32[]{:S(2)}, u32[]{:S(2)}) collective-permute-start(bf16[16,4,8,128]{3,2,1,0:T(8,128)(2,1)S(1)} %get-tuple-element.9.refs_5_), channel_id=1, source_target_pairs={{0,16},{16,32},{32,48},{48,0},{1,17},{17,33},{33,49},{49,1},{2,18}... | collective-permute-start | bytes 393224 | tf_op jit(solution)/shard_map/ppermute | solution.py:200
  56.3 21.0 %collective-permute-start.1 = (bf16[16,4,8,128]{3,2,1,0:T(8,128)(2,1)S(1)}, bf16[16,4,8,128]{3,2,1,0:T(8,128)(2,1)S(1)}, u32[]{:S(2)}, u32[]{:S(2)}) collective-permute-start(bf16[16,4,8,128]{3,2,1,0:T(8,128)(2,1)S(1)} %get-tuple-element.9.refs_5_), channel_id=1, source_target_pairs={{0,32},{16,48},{32,0},{48,16},{1,33},{17,49},{33,1},{49,17},{2,34}... | collective-permute-start | bytes 393224 | tf_op jit(solution)/shard_map/ppermute | solution.py:200
  60.3 17.0 %collective-permute-start = (bf16[16,4,8,128]{3,2,1,0:T(8,128)(2,1)S(1)}, bf16[16,4,8,128]{3,2,1,0:T(8,128)(2,1)S(1)}, u32[]{:S(2)}, u32[]{:S(2)}) collective-permute-start(bf16[16,4,8,128]{3,2,1,0:T(8,128)(2,1)S(1)} %get-tuple-element.9.refs_5_), channel_id=1, source_target_pairs={{0,48},{16,0},{32,16},{48,32},{1,49},{17,1},{33,17},{49,33},{2,50}... | collective-permute-start | bytes 393224 | tf_op jit(solution)/shard_map/ppermute | solution.py:200
  67.5 14.4 %copy-start.2 = (f32[2,16,128]{2,1,0:T(8,128)S(1)}, f32[2,16,128]{2,1,0:T(8,128)}, u32[]{:S(2)}) copy-start(f32[2,16,128]{2,1,0:T(8,128)} %param.5) | copy-start | bytes 49156
  68.1 13.8 %all-to-all-start.3 = ((f32[8,1,128]{2,1,0:T(1,128)}), f32[8,1,128]{2,1,0:T(1,128)S(1)}, u32[]{:S(2)}, u32[]{:S(2)}) async-start(f32[8,1,128]{2,1,0:T(1,128)} %bitcast.5), calls=%async_computation.3 | async-start | bytes 8192 | tf_op jit(solution)/shard_map/all_to_all | solution.py:210

commit v12 on v11

--- a/solution.py
+++ b/solution.py
@@ -19,14 +19,17 @@
 VMEM_LIMIT = 8 * 2**20
 
 
-def split_kernel(params_ref, momentum_ref, blocks_ref):
+def split_kernel(first_ref, second_ref, momentum_ref, blocks_ref):
     ys, lows, entries = blocks_ref.shape[:3]
     highs = entries - 1
     momentum = momentum_ref[...]
     for y in range(ys):
         for low in range(lows):
             for high in range(highs):
-                blocks_ref[y, low, high] = params_ref[:, (y * highs + high) * lows + low]
+                owner = (y * highs + high) * lows + low
+                half = first_ref.shape[0]
+                blocks_ref[y, low, high, :half] = first_ref[:, owner]
+                blocks_ref[y, low, high, half:] = second_ref[:, owner]
             blocks_ref[y, low, highs] = momentum
 
 
@@ -168,7 +171,7 @@
         out_shape=jax.ShapeDtypeStruct((ys, lows, highs + 1, *tile), replica_params.dtype),
         compiler_params=params,
         name="split",
-    )(grouped, momentum.astype(jnp.bfloat16))
+    )(grouped[: groups // 2], grouped[groups // 2 :], momentum.astype(jnp.bfloat16))
     received = lax.all_to_all(
         blocks.reshape(owners, highs + 1, *tile), ("y", "z_lo"), 0, 0, tiled=True
     )

time: 83.5 us -> 83.5 us (level)
    slice x0 -> x1, local copies, waits for them, and re-layouts: none -> 1.06 us  [per_device(): grouped[groups // 2:]]
    unnamed x6 -> x4, local copies, waits for them, and re-layouts: 1.05 us -> 0.01 us
where the time goes in v12:
time: 83.5 us; the launch traced here: 83.1 us
  blocking collectives  45.3 us (54%)
  starting transfers between devices  23.4 us (28%)
  waiting for transfers between devices  8.39 us (10%)
  Pallas kernels  3.41 us (4%)
  local copies, waits for them, and re-layouts  1.07 us (1%)
    all_to_all x1, blocking collectives, per_device(): lax.all_to_all(blocks.reshape(owners, highs + 1, *tile), ('y', 'z_lo'), 0...  29.1 us
    all_to_all x1, blocking collectives, per_device(): packed = lax.all_to_all(packed, 'z_hi', 0, 0, tiled=True)  16.3 us
    ppermute x3, starting transfers between devices, per_device(): lax.ppermute(momenta, 'z_hi', [(i, (i - shift) % highs) for i in range(hi...  10.4 us
    all_to_all x1, starting transfers between devices, per_device(): lax.all_to_all(sums.reshape(shards, 1, BLOCK), ('x', 'core'), 0, 0, tiled...  9.27 us
    all_to_all x1, waiting for transfers between devices, per_device(): lax.all_to_all(sums.reshape(shards, 1, BLOCK), ('x', 'core'), 0, 0, tiled...  4.48 us
    all_to_all x1, waiting for transfers between devices, per_device(): sent = lax.all_to_all(sent, ('y', 'z_lo'), 0, 0, tiled=True)  3.9 us
    all_to_all x1, starting transfers between devices, per_device(): sent = lax.all_to_all(sent, ('y', 'z_lo'), 0, 0, tiled=True)  3.79 us
  transfers between devices with their start and end apart: 5, of which 2 were waited for; matrix products, arithmetic and copies ran while one was open for 0% of the time, Pallas kernels for 1%

profile of v12, /device:TPU:1, one launch (start us, length us, event | category | flops | bytes accessed | tf_op | source)
XLA Modules:
  0.0 83.1 jit_solution(15083877380813804087)
XLA Ops:
  0.6 0.7 convert_element_type.3.momentum_ref
  1.4 1.1 %fusion = (bf16[2,64,8,128]{3,2,1,0:T(8,128)(2,1)S(1)}, bf16[2,64,8,128]{3,2,1,0:T(8,128)(2,1)S(1)}) fusion(bf16[4,64,8,128]{3,2,1,0:T(8,128)(2,1)} %bitcast.14), kind=kLoop, calls=%fused_computation | loop fusion | bytes 1048576 | tf_op jit(solution)/shard_map/slice | solution.py:174
  2.4 0.0 copy-start
  2.4 0.1 split.1
  2.5 29.1 %all_to_all.20.received_ref.refs_1_ = bf16[16,5,4,8,128]{4,3,2,1,0:T(8,128)(2,1)S(1)} all-to-all(bf16[16,5,4,8,128]{4,3,2,1,0:T(8,128)(2,1)S(1)} %bitcast.10), channel_id=1, replica_groups=mesh['y'=8,'z_hi'=4,'z_lo'=2,'x'=4,'core'=2] {'y','z_lo'}, dimensions={0} | all-to-all | bytes 1310720 | tf_op jit(solution)/shard_map/all_to_all | solution.py:175
  31.6 0.0 copy-done
  31.6 0.5 partial.1
  32.1 16.3 %all_to_all.21.refs_0_ = bf16[4,4,4,8,128]{4,3,2,1,0:T(8,128)(2,1)S(1)} all-to-all(bf16[4,4,4,8,128]{4,3,2,1,0:T(8,128)(2,1)S(1)} %partial.1), channel_id=1, replica_groups=mesh['y'=8,'z_hi'=4,'z_lo'=2,'x'=4,'core'=2] {'z_hi'}, dimensions={0} | all-to-all | bytes 262144 | tf_op jit(solution)/shard_map/all_to_all | solution.py:184
  48.3 1.0 %average.1 = (f32[4,8,128]{2,1,0:T(8,128)S(1)}, bf16[16,17,8,128]{3,2,1,0:T(8,128)(2,1)}, bf16[16,4,8,128]{3,2,1,0:T(8,128)(2,1)S(1)}) custom-call(bf16[4,4,4,8,128]{4,3,2,1,0:T(8,128)(2,1)S(1)} %all_to_all.21.refs_0_, bf16[16,5,4,8,128]{4,3,2,1,0:T(8,128)(2,1)S(1)} %all_to_all.20.received_ref.refs_1_), custom_call_target="tpu_custom_call" | custom-call | tf_op jit(solution)/shard_map/average/pallas_call | solution.py:186
  49.4 3.8 %all-to-all-start.2 = ((bf16[16,17,8,128]{3,2,1,0:T(8,128)(2,1)}), bf16[16,17,8,128]{3,2,1,0:T(8,128)(2,1)S(1)}, u32[]{:S(2)}, u32[]{:S(2)}) async-start(bf16[16,17,8,128]{3,2,1,0:T(8,128)(2,1)} %get-tuple-element.7), calls=%async_computation.2 | async-start | bytes 1114112 | tf_op jit(solution)/shard_map/all_to_all | solution.py:201
  53.2 3.2 %collective-permute-start.2 = (bf16[16,4,8,128]{3,2,1,0:T(8,128)(2,1)S(1)}, bf16[16,4,8,128]{3,2,1,0:T(8,128)(2,1)S(1)}, u32[]{:S(2)}, u32[]{:S(2)}) collective-permute-start(bf16[16,4,8,128]{3,2,1,0:T(8,128)(2,1)S(1)} %get-tuple-element.9.refs_5_), channel_id=1, source_target_pairs={{0,16},{16,32},{32,48},{48,0},{1,17},{17,33},{33,49},{49,1},{2,18}... | collective-permute-start | bytes 393224 | tf_op jit(solution)/shard_map/ppermute | solution.py:203
  56.4 4.0 %collective-permute-start.1 = (bf16[16,4,8,128]{3,2,1,0:T(8,128)(2,1)S(1)}, bf16[16,4,8,128]{3,2,1,0:T(8,128)(2,1)S(1)}, u32[]{:S(2)}, u32[]{:S(2)}) collective-permute-start(bf16[16,4,8,128]{3,2,1,0:T(8,128)(2,1)S(1)} %get-tuple-element.9.refs_5_), channel_id=1, source_target_pairs={{0,32},{16,48},{32,0},{48,16},{1,33},{17,49},{33,1},{49,17},{2,34}... | collective-permute-start | bytes 393224 | tf_op jit(solution)/shard_map/ppermute | solution.py:203
  60.4 3.2 %collective-permute-start = (bf16[16,4,8,128]{3,2,1,0:T(8,128)(2,1)S(1)}, bf16[16,4,8,128]{3,2,1,0:T(8,128)(2,1)S(1)}, u32[]{:S(2)}, u32[]{:S(2)}) collective-permute-start(bf16[16,4,8,128]{3,2,1,0:T(8,128)(2,1)S(1)} %get-tuple-element.9.refs_5_), channel_id=1, source_target_pairs={{0,48},{16,0},{32,16},{48,32},{1,49},{17,1},{33,17},{49,33},{2,50}... | collective-permute-start | bytes 393224 | tf_op jit(solution)/shard_map/ppermute | solution.py:203
  63.6 3.9 %all-to-all-done.2.sent_ref.refs_1_ = bf16[16,17,8,128]{3,2,1,0:T(8,128)(2,1)S(1)} async-done(((bf16[16,17,8,128]{3,2,1,0:T(8,128)(2,1)}), bf16[16,17,8,128]{3,2,1,0:T(8,128)(2,1)S(1)}, u32[]{:S(2)}, u32[]{:S(2)}) %all-to-all-start.2) | async-done | bytes 557088 | tf_op jit(solution)/shard_map/all_to_all | solution.py:201
  67.5 0.0 copy-start.1
  67.5 0.6 sum.1
  68.1 9.3 %all-to-all-start.3 = ((f32[8,1,128]{2,1,0:T(1,128)}), f32[8,1,128]{2,1,0:T(1,128)S(1)}, u32[]{:S(2)}, u32[]{:S(2)}) async-start(f32[8,1,128]{2,1,0:T(1,128)} %bitcast.6), calls=%async_computation.3 | async-start | bytes 8192 | tf_op jit(solution)/shard_map/all_to_all | solution.py:213
  77.4 0.0 collective-permute-done.2.refs_8_
  77.4 0.0 collective-permute-done.1.refs_7_
  77.4 0.0 collective-permute-done.refs_6_
  77.4 4.5 %all-to-all-done.3 = f32[8,1,128]{2,1,0:T(1,128)S(1)} async-done(((f32[8,1,128]{2,1,0:T(1,128)}), f32[8,1,128]{2,1,0:T(1,128)S(1)}, u32[]{:S(2)}, u32[]{:S(2)}) %all-to-all-start.3) | async-done | bytes 4128 | tf_op jit(solution)/shard_map/all_to_all | solution.py:213
  81.9 0.0 copy-done.1
  81.9 1.2 %base.1 = (f32[2,16,8192]{2,1,0:T(8,128)}, f32[4,8,128]{2,1,0:T(8,128)}) custom-call(f32[8,128]{1,0:T(8,128)S(1)} %bitcast.13, bf16[16,17,8,128]{3,2,1,0:T(8,128)(2,1)S(1)} %all-to-all-done.2.sent_ref.refs_1_, f32[2,16,8192]{2,1,0:T(8,128)S(1)} %copy-done, f32[4,8,128]{2,1,0:T(8,128)S(1)} %get-tuple-element.8.refs_3_, f32[4,8,128]{2,1,0:T(8,128)S(1)} %bitcast.12, ...), custom_call_target="tpu_custom_call" | custom-call | tf_op jit(solution)/shard_map/base/pallas_call | solution.py:218
Async XLA Ops:
  2.4 29.2 %copy-start = (f32[2,16,8192]{2,1,0:T(8,128)S(1)}, f32[2,16,8192]{2,1,0:T(8,128)}, u32[]{:S(2)}) copy-start(f32[2,16,8192]{2,1,0:T(8,128)} %refs_2_.1) | copy-start | bytes 3145732
  49.4 18.1 %all-to-all-start.2 = ((bf16[16,17,8,128]{3,2,1,0:T(8,128)(2,1)}), bf16[16,17,8,128]{3,2,1,0:T(8,128)(2,1)S(1)}, u32[]{:S(2)}, u32[]{:S(2)}) async-start(bf16[16,17,8,128]{3,2,1,0:T(8,128)(2,1)} %get-tuple-element.7), calls=%async_computation.2 | async-start | bytes 1114112 | tf_op jit(solution)/shard_map/all_to_all | solution.py:201
  53.2 24.2 %collective-permute-start.2 = (bf16[16,4,8,128]{3,2,1,0:T(8,128)(2,1)S(1)}, bf16[16,4,8,128]{3,2,1,0:T(8,128)(2,1)S(1)}, u32[]{:S(2)}, u32[]{:S(2)}) collective-permute-start(bf16[16,4,8,128]{3,2,1,0:T(8,128)(2,1)S(1)} %get-tuple-element.9.refs_5_), channel_id=1, source_target_pairs={{0,16},{16,32},{32,48},{48,0},{1,17},{17,33},{33,49},{49,1},{2,18}... | collective-permute-start | bytes 393224 | tf_op jit(solution)/shard_map/ppermute | solution.py:203
  56.4 21.0 %collective-permute-start.1 = (bf16[16,4,8,128]{3,2,1,0:T(8,128)(2,1)S(1)}, bf16[16,4,8,128]{3,2,1,0:T(8,128)(2,1)S(1)}, u32[]{:S(2)}, u32[]{:S(2)}) collective-permute-start(bf16[16,4,8,128]{3,2,1,0:T(8,128)(2,1)S(1)} %get-tuple-element.9.refs_5_), channel_id=1, source_target_pairs={{0,32},{16,48},{32,0},{48,16},{1,33},{17,49},{33,1},{49,17},{2,34}... | collective-permute-start | bytes 393224 | tf_op jit(solution)/shard_map/ppermute | solution.py:203
  60.4 17.0 %collective-permute-start = (bf16[16,4,8,128]{3,2,1,0:T(8,128)(2,1)S(1)}, bf16[16,4,8,128]{3,2,1,0:T(8,128)(2,1)S(1)}, u32[]{:S(2)}, u32[]{:S(2)}) collective-permute-start(bf16[16,4,8,128]{3,2,1,0:T(8,128)(2,1)S(1)} %get-tuple-element.9.refs_5_), channel_id=1, source_target_pairs={{0,48},{16,0},{32,16},{48,32},{1,49},{17,1},{33,17},{49,33},{2,50}... | collective-permute-start | bytes 393224 | tf_op jit(solution)/shard_map/ppermute | solution.py:203
  67.5 14.4 %copy-start.1 = (f32[2,16,128]{2,1,0:T(8,128)S(1)}, f32[2,16,128]{2,1,0:T(8,128)}, u32[]{:S(2)}) copy-start(f32[2,16,128]{2,1,0:T(8,128)} %param.5) | copy-start | bytes 49156
  68.1 13.8 %all-to-all-start.3 = ((f32[8,1,128]{2,1,0:T(1,128)}), f32[8,1,128]{2,1,0:T(1,128)S(1)}, u32[]{:S(2)}, u32[]{:S(2)}) async-start(f32[8,1,128]{2,1,0:T(1,128)} %bitcast.6), calls=%async_computation.3 | async-start | bytes 8192 | tf_op jit(solution)/shard_map/all_to_all | solution.py:213

commit v13 on v11

--- a/solution.py
+++ b/solution.py
@@ -30,9 +30,10 @@
             blocks_ref[y, low, highs] = momentum
 
 
-def partial_kernel(received_ref, base_ref, packed_ref):
+def partial_kernel(received_ref, base_ref, packed_ref, momenta_ref):
     sources = received_ref.shape[0]
     peers, blocks, groups = packed_ref.shape[:3]
+    momenta_ref[...] = received_ref[:, blocks]
     lows = lax.axis_size("z_lo")
     first = lax.axis_index("y") * (blocks * lows) + lax.axis_index("z_lo")
     for block in range(blocks):
@@ -50,7 +51,7 @@
             packed_ref[peer, block] = sent
 
 
-def average_kernel(replicas, packed_ref, received_ref, averaged_ref, sent_ref, momenta_ref, made_ref, semaphores):
+def average_kernel(replicas, packed_ref, received_ref, nearest_ref, averaged_ref, sent_ref, momenta_ref, made_ref, semaphores):
     sources, blocks, groups = packed_ref.shape[:3]
     peers = sent_ref.shape[0]
 
@@ -172,13 +173,17 @@
     received = lax.all_to_all(
         blocks.reshape(owners, highs + 1, *tile), ("y", "z_lo"), 0, 0, tiled=True
     )
-    packed = pl.pallas_call(
+    packed, early = pl.pallas_call(
         partial_kernel,
-        out_shape=jax.ShapeDtypeStruct((highs, highs, *tile), jnp.bfloat16),
+        out_shape=(
+            jax.ShapeDtypeStruct((highs, highs, *tile), jnp.bfloat16),
+            jax.ShapeDtypeStruct((owners, *tile), jnp.bfloat16),
+        ),
         compiler_params=params,
         name="partial",
     )(received, outer_base)
     packed = lax.all_to_all(packed, "z_hi", 0, 0, tiled=True)
+    nearest = lax.ppermute(early, "z_hi", [(i, (i - 1) % highs) for i in range(highs)])
 
     averaged, sent, momenta = pl.pallas_call(
         lambda *refs: average_kernel(replicas, *refs),
@@ -194,11 +199,11 @@
         ],
         compiler_params=params,
         name="average",
-    )(packed, received)
+    )(packed, received, nearest)
     sent = lax.all_to_all(sent, ("y", "z_lo"), 0, 0, tiled=True)
-    all_momenta = [momenta] + [
+    all_momenta = [momenta, nearest] + [
         lax.ppermute(momenta, "z_hi", [(i, (i - shift) % highs) for i in range(highs)])
-        for shift in range(1, highs)
+        for shift in range(2, highs)
     ]
     shards = xs * cores
     sums = pl.pallas_call(

time: 83.5 us -> 88.9 us (1.065)
  blocking collectives: 45.3 us -> 29.1 us
  waiting for transfers between devices: 8.39 us -> 19.7 us
  starting transfers between devices: 23.4 us -> 33 us
    all_to_all x1 -> x0, blocking collectives: 16.3 us -> none  [per_device(): packed = lax.all_to_all(packed, 'z_hi', 0, 0, tiled=True)]
    all_to_all x0 -> x1, starting transfers between devices: none -> 9.12 us  [per_device(): packed = lax.all_to_all(packed, 'z_hi', 0, 0, tiled=True)]
    ppermute x0 -> x1, waiting for transfers between devices: none -> 6.78 us  [per_device(): lax.ppermute(early, 'z_hi', [(i, (i - 1) % highs) for i in range(highs)])]
    ppermute x0 -> x1, starting transfers between devices: none -> 5.47 us  [per_device(): lax.ppermute(early, 'z_hi', [(i, (i - 1) % highs) for i in range(highs)])]
    all_to_all x1, waiting for transfers between devices: 3.9 us -> 8.39 us  [per_device(): sent = lax.all_to_all(sent, ('y', 'z_lo'), 0, 0, tiled=True)]
    all_to_all x1, starting transfers between devices: 9.27 us -> 6.31 us  [per_device(): lax.all_to_all(sums.reshape(shards, 1, BLOCK), ('x', 'core'), 0, 0, tiled...]
    ppermute x3 -> x2, starting transfers between devices: 10.4 us -> 8.55 us  [per_device(): lax.ppermute(momenta, 'z_hi', [(i, (i - shift) % highs) for i in range(hi...]
  transfers between devices with their start and end apart: 5 -> 6, of which waited for: 2 -> 4; matrix products, arithmetic and copies ran while one was open for 0% -> 0% of each run, Pallas kernels for 1% -> 1%
where the time goes in v13:
time: 88.9 us; the launch traced here: 88.3 us
  starting transfers between devices  33 us (37%)
  blocking collectives  29.1 us (33%)
  waiting for transfers between devices  19.7 us (22%)
  Pallas kernels  4.06 us (5%)
  local copies, waits for them, and re-layouts  1.05 us (1%)
    all_to_all x1, blocking collectives, per_device(): lax.all_to_all(blocks.reshape(owners, highs + 1, *tile), ('y', 'z_lo'), 0...  29.1 us
    all_to_all x1, starting transfers between devices, per_device(): packed = lax.all_to_all(packed, 'z_hi', 0, 0, tiled=True)  9.12 us
    ppermute x2, starting transfers between devices, per_device(): lax.ppermute(momenta, 'z_hi', [(i, (i - shift) % highs) for i in range(hi...  8.55 us
    all_to_all x1, waiting for transfers between devices, per_device(): sent = lax.all_to_all(sent, ('y', 'z_lo'), 0, 0, tiled=True)  8.39 us
    ppermute x1, waiting for transfers between devices, per_device(): lax.ppermute(early, 'z_hi', [(i, (i - 1) % highs) for i in range(highs)])  6.78 us
    all_to_all x1, starting transfers between devices, per_device(): lax.all_to_all(sums.reshape(shards, 1, BLOCK), ('x', 'core'), 0, 0, tiled...  6.31 us
    ppermute x1, starting transfers between devices, per_device(): lax.ppermute(early, 'z_hi', [(i, (i - 1) % highs) for i in range(highs)])  5.47 us
    all_to_all x1, waiting for transfers between devices, per_device(): lax.all_to_all(sums.reshape(shards, 1, BLOCK), ('x', 'core'), 0, 0, tiled...  3.68 us
  transfers between devices with their start and end apart: 6, of which 4 were waited for; matrix products, arithmetic and copies ran while one was open for 0% of the time, Pallas kernels for 1%

profile of v13, /device:TPU:1, one launch (start us, length us, event | category | flops | bytes accessed | tf_op | source)
XLA Modules:
  0.0 88.3 jit_solution(4414274494979869532)
XLA Ops:
  0.6 0.7 convert_element_type.3.momentum_ref
  1.4 0.0 copy-start.1
  1.4 1.0 %copy-done.1 = bf16[1,2,16,8192]{3,2,1,0:T(8,128)(2,1)S(1)} copy-done((bf16[1,2,16,8192]{3,2,1,0:T(8,128)(2,1)S(1)}, bf16[1,2,16,8192]{3,2,1,0:T(8,128)(2,1)}, u32[]{:S(2)}) %copy-start.1) | copy-done | bytes 524312
  2.4 0.0 copy-start
  2.4 0.1 split.1
  2.5 29.1 %all_to_all.20.received_ref.refs_1_ = bf16[16,5,4,8,128]{4,3,2,1,0:T(8,128)(2,1)S(1)} all-to-all(bf16[16,5,4,8,128]{4,3,2,1,0:T(8,128)(2,1)S(1)} %bitcast.10), channel_id=1, replica_groups=mesh['y'=8,'z_hi'=4,'z_lo'=2,'x'=4,'core'=2] {'y','z_lo'}, dimensions={0} | all-to-all | bytes 1310720 | tf_op jit(solution)/shard_map/all_to_all | solution.py:173
  31.6 0.0 copy-done
  31.6 1.1 %partial.1 = (bf16[4,4,4,8,128]{4,3,2,1,0:T(8,128)(2,1)}, bf16[16,4,8,128]{3,2,1,0:T(8,128)(2,1)S(1)}) custom-call(bf16[16,5,4,8,128]{4,3,2,1,0:T(8,128)(2,1)S(1)} %all_to_all.20.received_ref.refs_1_, f32[2,16,8192]{2,1,0:T(8,128)S(1)} %copy-done), custom_call_target="tpu_custom_call" | custom-call | tf_op jit(solution)/shard_map/partial/pallas_call | solution.py:176
  32.7 9.1 %all-to-all-start.1 = ((bf16[4,4,4,8,128]{4,3,2,1,0:T(8,128)(2,1)}), bf16[4,4,4,8,128]{4,3,2,1,0:T(8,128)(2,1)S(1)}, u32[]{:S(2)}, u32[]{:S(2)}) async-start(bf16[4,4,4,8,128]{4,3,2,1,0:T(8,128)(2,1)} %get-tuple-element.9), calls=%async_computation.1 | async-start | bytes 262144 | tf_op jit(solution)/shard_map/all_to_all | solution.py:185
  41.8 5.5 %collective-permute-start = (bf16[16,4,8,128]{3,2,1,0:T(8,128)(2,1)S(1)}, bf16[16,4,8,128]{3,2,1,0:T(8,128)(2,1)S(1)}, u32[]{:S(2)}, u32[]{:S(2)}) collective-permute-start(bf16[16,4,8,128]{3,2,1,0:T(8,128)(2,1)S(1)} %get-tuple-element.10), channel_id=1, source_target_pairs={{0,48},{16,0},{32,16},{48,32},{1,49},{17,1},{33,17},{49,33},{2,50}... | collective-permute-start | bytes 393224 | tf_op jit(solution)/shard_map/ppermute | solution.py:186
  47.3 6.8 %collective-permute-done.refs_2_.refs_6_ = bf16[16,4,8,128]{3,2,1,0:T(8,128)(2,1)S(1)} collective-permute-done((bf16[16,4,8,128]{3,2,1,0:T(8,128)(2,1)S(1)}, bf16[16,4,8,128]{3,2,1,0:T(8,128)(2,1)S(1)}, u32[]{:S(2)}, u32[]{:S(2)}) %collective-permute-start) | collective-permute-done | bytes 131104 | tf_op jit(solution)/shard_map/ppermute | solution.py:186
  54.1 0.0 all-to-all-done.1.refs_0_
  54.1 1.0 %average.1 = (f32[4,8,128]{2,1,0:T(8,128)S(1)}, bf16[16,17,8,128]{3,2,1,0:T(8,128)(2,1)}, bf16[16,4,8,128]{3,2,1,0:T(8,128)(2,1)S(1)}) custom-call(bf16[4,4,4,8,128]{4,3,2,1,0:T(8,128)(2,1)S(1)} %all-to-all-done.1.refs_0_, bf16[16,5,4,8,128]{4,3,2,1,0:T(8,128)(2,1)S(1)} %all_to_all.20.received_ref.refs_1_, ...), custom_call_target="tpu_custom_call" | custom-call | tf_op jit(solution)/shard_map/average/pallas_call | solution.py:188
  55.1 3.6 %all-to-all-start.2 = ((bf16[16,17,8,128]{3,2,1,0:T(8,128)(2,1)}), bf16[16,17,8,128]{3,2,1,0:T(8,128)(2,1)S(1)}, u32[]{:S(2)}, u32[]{:S(2)}) async-start(bf16[16,17,8,128]{3,2,1,0:T(8,128)(2,1)} %get-tuple-element.11), calls=%async_computation.2 | async-start | bytes 1114112 | tf_op jit(solution)/shard_map/all_to_all | solution.py:203
  58.7 5.2 %collective-permute-start.2 = (bf16[16,4,8,128]{3,2,1,0:T(8,128)(2,1)S(1)}, bf16[16,4,8,128]{3,2,1,0:T(8,128)(2,1)S(1)}, u32[]{:S(2)}, u32[]{:S(2)}) collective-permute-start(bf16[16,4,8,128]{3,2,1,0:T(8,128)(2,1)S(1)} %get-tuple-element.13.refs_5_), channel_id=1, source_target_pairs={{0,16},{16,32},{32,48},{48,0},{1,17},{17,33},{33,49},{49,1},{2,18}... | collective-permute-start | bytes 393224 | tf_op jit(solution)/shard_map/ppermute | solution.py:205
  63.9 3.4 %collective-permute-start.1 = (bf16[16,4,8,128]{3,2,1,0:T(8,128)(2,1)S(1)}, bf16[16,4,8,128]{3,2,1,0:T(8,128)(2,1)S(1)}, u32[]{:S(2)}, u32[]{:S(2)}) collective-permute-start(bf16[16,4,8,128]{3,2,1,0:T(8,128)(2,1)S(1)} %get-tuple-element.13.refs_5_), channel_id=1, source_target_pairs={{0,32},{16,48},{32,0},{48,16},{1,33},{17,49},{33,1},{49,17},{2,34}... | collective-permute-start | bytes 393224 | tf_op jit(solution)/shard_map/ppermute | solution.py:205
  67.3 8.4 %all-to-all-done.2.sent_ref.refs_1_ = bf16[16,17,8,128]{3,2,1,0:T(8,128)(2,1)S(1)} async-done(((bf16[16,17,8,128]{3,2,1,0:T(8,128)(2,1)}), bf16[16,17,8,128]{3,2,1,0:T(8,128)(2,1)S(1)}, u32[]{:S(2)}, u32[]{:S(2)}) %all-to-all-start.2) | async-done | bytes 557088 | tf_op jit(solution)/shard_map/all_to_all | solution.py:203
  75.7 0.0 copy-start.2
  75.7 0.6 sum.1
  76.3 6.3 %all-to-all-start.3 = ((f32[8,1,128]{2,1,0:T(1,128)}), f32[8,1,128]{2,1,0:T(1,128)S(1)}, u32[]{:S(2)}, u32[]{:S(2)}) async-start(f32[8,1,128]{2,1,0:T(1,128)} %bitcast.5), calls=%async_computation.3 | async-start | bytes 8192 | tf_op jit(solution)/shard_map/all_to_all | solution.py:215
  82.6 0.0 collective-permute-done.2.refs_8_
  82.6 0.8 collective-permute-done.1.refs_7_
  83.4 3.7 %all-to-all-done.3 = f32[8,1,128]{2,1,0:T(1,128)S(1)} async-done(((f32[8,1,128]{2,1,0:T(1,128)}), f32[8,1,128]{2,1,0:T(1,128)S(1)}, u32[]{:S(2)}, u32[]{:S(2)}) %all-to-all-start.3) | async-done | bytes 4128 | tf_op jit(solution)/shard_map/all_to_all | solution.py:215
  87.1 0.0 copy-done.2
  87.1 1.2 %base.1 = (f32[2,16,8192]{2,1,0:T(8,128)}, f32[4,8,128]{2,1,0:T(8,128)}) custom-call(f32[8,128]{1,0:T(8,128)S(1)} %bitcast.14, bf16[16,17,8,128]{3,2,1,0:T(8,128)(2,1)S(1)} %all-to-all-done.2.sent_ref.refs_1_, f32[2,16,8192]{2,1,0:T(8,128)S(1)} %copy-done, f32[4,8,128]{2,1,0:T(8,128)S(1)} %get-tuple-element.12.refs_3_, f32[4,8,128]{2,1,0:T(8,128)S(1)} %bitcast.13, ...), custom_call_target="tpu_custom_call" | custom-call | tf_op jit(solution)/shard_map/base/pallas_call | solution.py:220
Async XLA Ops:
  1.4 1.0 %copy-start.1 = (bf16[1,2,16,8192]{3,2,1,0:T(8,128)(2,1)S(1)}, bf16[1,2,16,8192]{3,2,1,0:T(8,128)(2,1)}, u32[]{:S(2)}) copy-start(bf16[1,2,16,8192]{3,2,1,0:T(8,128)(2,1)} %param.3) | copy-start | bytes 1572868
  2.4 29.2 %copy-start = (f32[2,16,8192]{2,1,0:T(8,128)S(1)}, f32[2,16,8192]{2,1,0:T(8,128)}, u32[]{:S(2)}) copy-start(f32[2,16,8192]{2,1,0:T(8,128)} %refs_2_.1) | copy-start | bytes 3145732
  32.7 21.4 %all-to-all-start.1 = ((bf16[4,4,4,8,128]{4,3,2,1,0:T(8,128)(2,1)}), bf16[4,4,4,8,128]{4,3,2,1,0:T(8,128)(2,1)S(1)}, u32[]{:S(2)}, u32[]{:S(2)}) async-start(bf16[4,4,4,8,128]{4,3,2,1,0:T(8,128)(2,1)} %get-tuple-element.9), calls=%async_computation.1 | async-start | bytes 262144 | tf_op jit(solution)/shard_map/all_to_all | solution.py:185
  41.8 12.3 %collective-permute-start = (bf16[16,4,8,128]{3,2,1,0:T(8,128)(2,1)S(1)}, bf16[16,4,8,128]{3,2,1,0:T(8,128)(2,1)S(1)}, u32[]{:S(2)}, u32[]{:S(2)}) collective-permute-start(bf16[16,4,8,128]{3,2,1,0:T(8,128)(2,1)S(1)} %get-tuple-element.10), channel_id=1, source_target_pairs={{0,48},{16,0},{32,16},{48,32},{1,49},{17,1},{33,17},{49,33},{2,50}... | collective-permute-start | bytes 393224 | tf_op jit(solution)/shard_map/ppermute | solution.py:186
  55.1 20.6 %all-to-all-start.2 = ((bf16[16,17,8,128]{3,2,1,0:T(8,128)(2,1)}), bf16[16,17,8,128]{3,2,1,0:T(8,128)(2,1)S(1)}, u32[]{:S(2)}, u32[]{:S(2)}) async-start(bf16[16,17,8,128]{3,2,1,0:T(8,128)(2,1)} %get-tuple-element.11), calls=%async_computation.2 | async-start | bytes 1114112 | tf_op jit(solution)/shard_map/all_to_all | solution.py:203
  58.7 23.9 %collective-permute-start.2 = (bf16[16,4,8,128]{3,2,1,0:T(8,128)(2,1)S(1)}, bf16[16,4,8,128]{3,2,1,0:T(8,128)(2,1)S(1)}, u32[]{:S(2)}, u32[]{:S(2)}) collective-permute-start(bf16[16,4,8,128]{3,2,1,0:T(8,128)(2,1)S(1)} %get-tuple-element.13.refs_5_), channel_id=1, source_target_pairs={{0,16},{16,32},{32,48},{48,0},{1,17},{17,33},{33,49},{49,1},{2,18}... | collective-permute-start | bytes 393224 | tf_op jit(solution)/shard_map/ppermute | solution.py:205
  63.9 19.5 %collective-permute-start.1 = (bf16[16,4,8,128]{3,2,1,0:T(8,128)(2,1)S(1)}, bf16[16,4,8,128]{3,2,1,0:T(8,128)(2,1)S(1)}, u32[]{:S(2)}, u32[]{:S(2)}) collective-permute-start(bf16[16,4,8,128]{3,2,1,0:T(8,128)(2,1)S(1)} %get-tuple-element.13.refs_5_), channel_id=1, source_target_pairs={{0,32},{16,48},{32,0},{48,16},{1,33},{17,49},{33,1},{49,17},{2,34}... | collective-permute-start | bytes 393224 | tf_op jit(solution)/shard_map/ppermute | solution.py:205
  75.7 11.4 %copy-start.2 = (f32[2,16,128]{2,1,0:T(8,128)S(1)}, f32[2,16,128]{2,1,0:T(8,128)}, u32[]{:S(2)}) copy-start(f32[2,16,128]{2,1,0:T(8,128)} %param.5) | copy-start | bytes 49156
  76.3 10.8 %all-to-all-start.3 = ((f32[8,1,128]{2,1,0:T(1,128)}), f32[8,1,128]{2,1,0:T(1,128)S(1)}, u32[]{:S(2)}, u32[]{:S(2)}) async-start(f32[8,1,128]{2,1,0:T(1,128)} %bitcast.5), calls=%async_computation.3 | async-start | bytes 8192 | tf_op jit(solution)/shard_map/all_to_all | solution.py:215
